TPU v7x, 256 devices: a whole 4x4x8 slice. The times are simulated.
256 devices in a mesh: dp: 32 (over z, x_hi, core), tensor: 8 (over x_lo, y).
Axes of the slice: x: 4 (x_hi: 2, x_lo: 2; x = x_hi * 2 + x_lo), y: 4, z: 8, core: 2. Of those that a mesh axis runs over, the one named last changes fastest.
Arguments:
- tokens: bfloat16 [16384, 3072], P('dp', 'tensor'), may hold values from -6 to 6
- hidden_cot: bfloat16 [16384, 8192], P('dp', 'tensor'), may hold values from -1.5 to 1.5
- w_gate: bfloat16 [3072, 8192], P(None, 'tensor'), may hold values from -0.109375 to 0.109375
- w_up: bfloat16 [3072, 8192], P(None, 'tensor'), may hold values from -0.109375 to 0.109375
- expert_ids: int32 [16384, 2], P('dp'), may hold values from 0 to 7, as said below
- route_fixed: int32 [16384, 2], P('dp'), may hold values from 4096 to 65535
Outputs:
- token_grad: bfloat16 [16384, 3072], P('dp', 'tensor')
- gate_grad: bfloat16 [3072, 8192], P('dp', 'tensor')
- up_grad: bfloat16 [3072, 8192], P('dp', 'tensor')
- route_grad: float32 [16384], P('dp')
Inputs may be any that keep to these rules, and one draw needn't show every extreme that they name: `expert_ids`: each row names 2 different experts; in each aligned block of 512 rows (the rows of one index of dp), between 128 and 256 rows name expert 0, and exactly 256 in some block.
All inputs are finite; a program needn't handle non-finite values.
Results may differ from a plain program's by a relative error of at most 0.0049.
Values may be sent and summed in bfloat16 or wider, within the bound.
No kernel may reach another device: no remote copies, remote signals or barrier semaphores. Data moves between devices by JAX's collectives and lax.ppermute only.
A program may use at most 128 MiB of HBM per device.

v0:
```python
import jax
import jax.numpy as jnp
from jax import lax
from jax.experimental import pallas as pl
from jax.experimental.pallas import tpu as pltpu
from jax.sharding import PartitionSpec as P

CAP = 256
CHUNKS = 2
BF = jnp.bfloat16
F32 = jnp.float32
MIB = 2**20


def whole(shape):
    return pl.BlockSpec(shape, lambda *_: (0,) * len(shape))


def dispatch_kernel(info, slots, tokens, picked, far, turned):
    cap, rows = picked.shape[0], far.shape[0]
    tok_dev = slots.shape[1]
    ids = lax.broadcasted_iota(jnp.int32, (cap, tok_dev), 0)
    mask = (slots[...] == ids).astype(F32).astype(BF)
    got = jnp.dot(mask, tokens[...], preferred_element_type=F32)
    picked[...] = got.astype(BF)
    turned[...] = got.T.astype(BF)
    start = pl.multiple_of((1 - info[2]) * rows, rows)
    far[...] = turned[pl.ds(start, rows), :]


def dispatch_tokens(info, slots, tokens):
    tok_dev, piece = tokens.shape
    return pl.pallas_call(
        dispatch_kernel,
        grid_spec=pltpu.PrefetchScalarGridSpec(
            num_scalar_prefetch=1,
            grid=(1,),
            in_specs=[whole((1, tok_dev)), whole((tok_dev, piece))],
            out_specs=[whole((CAP, piece)), whole((piece // 2, CAP))],
            scratch_shapes=[pltpu.VMEM((piece, CAP), BF)],
        ),
        out_shape=[
            jax.ShapeDtypeStruct((CAP, piece), BF),
            jax.ShapeDtypeStruct((piece // 2, CAP), BF),
        ],
        compiler_params=pltpu.CompilerParams(vmem_limit_bytes=8 * MIB),
        cost_estimate=pl.CostEstimate(
            flops=2 * CAP * tok_dev * piece, bytes_accessed=4 * tok_dev * piece, transcendentals=0
        ),
    )(info, slots, tokens)


def cot_kernel(slots, share_all, cot, rows, share):
    cap, tok_dev = rows.shape[0], slots.shape[1]
    mask = slots[...] == lax.broadcasted_iota(jnp.int32, (cap, tok_dev), 0)
    hot = mask.astype(F32).astype(BF)
    rows[...] = jnp.dot(hot, cot[...], preferred_element_type=F32).astype(BF)
    share[...] = jnp.sum(jnp.where(mask, share_all[...], 0.0), axis=1, keepdims=True)


def dispatch_cots(slots, share_all, hidden_cot):
    tok_dev, width = hidden_cot.shape
    return pl.pallas_call(
        cot_kernel,
        out_shape=[
            jax.ShapeDtypeStruct((CAP, width), BF),
            jax.ShapeDtypeStruct((CAP, 1), F32),
        ],
        compiler_params=pltpu.CompilerParams(vmem_limit_bytes=8 * MIB),
        cost_estimate=pl.CostEstimate(
            flops=2 * CAP * tok_dev * width, bytes_accessed=4 * tok_dev * width, transcendentals=0
        ),
    )(slots, share_all, hidden_cot)


def early_kernel(n, order, *refs):
    pieces = refs[:n]
    wg, wu, gate, up, near, all_g, all_u, held, turned, sems = refs[n:]
    cap, piece = pieces[0].shape
    half = near.shape[1]

    def copies(i):
        start = pl.multiple_of(order[i] * piece, piece)
        return [
            pltpu.make_async_copy(
                w.at[pl.ds(start, piece)], ref.at[pl.ds(i * piece, piece)], sems.at[i, j]
            )
            for j, (w, ref) in enumerate(((wg, all_g), (wu, all_u)))
        ]

    every = [copies(i) for i in range(2 * n)]
    for pair in every:
        for copy in pair:
            copy.start()
    for k in range(n):
        held[:, k * piece : (k + 1) * piece] = pieces[k][...]

    def turn(k, _):
        turned[...] = held[:, pl.ds(pl.multiple_of(k * piece, piece), piece)].T
        start = pl.multiple_of(order[2 * n] * half, half)
        near[k] = turned[pl.ds(start, half), :]
        return 0

    lax.fori_loop(0, n, turn, 0)
    for pair in every[:n]:
        for copy in pair:
            copy.wait()
    block = gate.shape[1] // CHUNKS

    def multiply(c, _):
        here = pl.ds(pl.multiple_of(c * block, block), block)
        gate[:, here] = jnp.dot(held[...], all_g[: n * piece, here], preferred_element_type=F32)
        up[:, here] = jnp.dot(held[...], all_u[: n * piece, here], preferred_element_type=F32)
        return 0

    lax.fori_loop(0, CHUNKS, multiply, 0)
    for pair in every[n:]:
        for copy in pair:
            copy.wait()


def early(order, pieces, w_gate, w_up):
    n = len(pieces)
    cap, piece = pieces[0].shape
    width = w_gate.shape[1]
    hbm = pl.BlockSpec(memory_space=pl.ANY)
    return pl.pallas_call(
        lambda *a: early_kernel(n, *a),
        grid_spec=pltpu.PrefetchScalarGridSpec(
            num_scalar_prefetch=1,
            grid=(1,),
            in_specs=[whole((cap, piece))] * n + [hbm, hbm],
            out_specs=[whole((cap, width))] * 2
            + [whole((n, piece // 2, cap))]
            + [pl.BlockSpec(memory_space=pltpu.VMEM)] * 2,
            scratch_shapes=[
                pltpu.VMEM((cap, n * piece), BF),
                pltpu.VMEM((piece, cap), BF),
                pltpu.SemaphoreType.DMA((2 * n, 2)),
            ],
        ),
        out_shape=[jax.ShapeDtypeStruct((cap, width), F32)] * 2
        + [jax.ShapeDtypeStruct((n, piece // 2, cap), BF)]
        + [pltpu.VMEM((2 * n * piece, width), BF)] * 2,
        compiler_params=pltpu.CompilerParams(vmem_limit_bytes=28 * MIB),
        cost_estimate=pl.CostEstimate(
            flops=4 * cap * n * piece * width,
            bytes_accessed=8 * n * piece * width,
            transcendentals=0,
        ),
    )(order, *pieces, w_gate, w_up)


def forward_kernel(n, soon, late, n_z, info, *refs):
    pieces = refs[:n]
    wg, wu, gate_in, up_in, near_in, cot, share = refs[n : n + 7]
    mine, other = refs[n + 7 : n + 7 + CHUNKS], refs[n + 7 + CHUNKS : n + 7 + 2 * CHUNKS]
    near_left, route_out, held, turned = refs[n + 7 + 2 * CHUNKS :]
    step = pl.program_id(0)
    piece, cap = turned.shape
    half, block = near_left.shape[1], cot.shape[1]
    at = lambda k: lax.rem((info[0] ^ k) - info[1] + n_z, n_z)

    @pl.when(step == 0)
    def _():
        route_out[...] = jnp.zeros_like(route_out)
        for i in range(n):
            held[:, i * piece : (i + 1) * piece] = pieces[i][...]

    here = pl.ds(pl.multiple_of(step * block, block), block)
    gate = gate_in[...] + jnp.dot(held[...], wg[n * piece :, here], preferred_element_type=F32)
    up = up_in[...] + jnp.dot(held[...], wu[n * piece :, here], preferred_element_type=F32)
    sig = jax.nn.sigmoid(gate)
    activated = gate * sig
    hidden = (activated * up).astype(BF).astype(F32)
    cot_wide = cot[...].astype(F32)
    route_out[...] += jnp.sum(hidden * cot_wide, axis=1, keepdims=True)
    scaled = share[...] * cot_wide
    gate_cot = scaled * up * sig * (1.0 + gate * (1.0 - sig))
    up_cot = scaled * activated
    first = info[3] == 0
    own = jnp.where(first, gate_cot, up_cot).astype(BF)
    rest = jnp.where(first, up_cot, gate_cot).astype(BF)
    for c in range(CHUNKS):

        @pl.when(step == c)
        def _(c=c):
            mine[c][...] = own
            other[c][...] = rest

    @pl.when(step == CHUNKS - 1)
    def _():
        for i, k in enumerate(soon):
            near_left[at(k)] = near_in[i]
        for i, k in enumerate(late):
            turned[...] = held[:, i * piece : (i + 1) * piece].T
            start = pl.multiple_of(info[2] * half, half)
            near_left[at(k)] = turned[pl.ds(start, half), :]


def forward(info, pieces, soon, late, w_gate, w_up, gate, up, near, cot_rows, share, n_z):
    n = len(pieces)
    cap, piece = pieces[0].shape
    width = w_gate.shape[1]
    block = width // CHUNKS
    cols = pl.BlockSpec((cap, block), lambda j, *_: (0, j))
    near_left = (n_z, piece // 2, cap)
    outs = [((cap, block), BF)] * (2 * CHUNKS) + [(near_left, BF), ((cap, 1), F32)]
    held = pl.BlockSpec(memory_space=pltpu.VMEM)
    return pl.pallas_call(
        lambda *a: forward_kernel(n, soon, late, n_z, *a),
        grid_spec=pltpu.PrefetchScalarGridSpec(
            num_scalar_prefetch=1,
            grid=(CHUNKS,),
            in_specs=[whole((cap, piece))] * n
            + [held, held, cols, cols, whole(near.shape), cols, whole((cap, 1))],
            out_specs=[whole(shape) for shape, _ in outs],
            scratch_shapes=[pltpu.VMEM((cap, n * piece), BF), pltpu.VMEM((piece, cap), BF)],
        ),
        out_shape=[jax.ShapeDtypeStruct(shape, kind) for shape, kind in outs],
        compiler_params=pltpu.CompilerParams(vmem_limit_bytes=24 * MIB),
        cost_estimate=pl.CostEstimate(
            flops=4 * cap * n * piece * width,
            bytes_accessed=16 * cap * width,
            transcendentals=cap * width,
        ),
    )(info, *pieces, w_gate, w_up, gate, up, near, cot_rows, share)


def back_kernel(info, *refs):
    mine, other = refs[:CHUNKS], refs[CHUNKS : 2 * CHUNKS]
    wg, wu, own, first_out, third_out, second_out, gt, ut = refs[2 * CHUNKS :]
    piece = own.shape[1]
    chunk = mine[0].shape[1]
    first = info[3] == 0
    for c in range(CHUNKS):
        a, b = mine[c][...], other[c][...]
        gt[pl.ds(c * chunk, chunk), :] = jnp.where(first, a, b).T
        ut[pl.ds(c * chunk, chunk), :] = jnp.where(first, b, a).T

    targets = [(own, 0), (own, 1), (first_out, 0), (third_out, 0)]
    targets += [(first_out, 1), (third_out, 1), (second_out, 0), (second_out, 1)]

    def block(i, _):
        rows = pl.ds(pl.multiple_of(i * piece, piece), piece)
        out = jnp.dot(wg[rows, :], gt[...], preferred_element_type=F32)
        out += jnp.dot(wu[rows, :], ut[...], preferred_element_type=F32)
        for j, (ref, at) in enumerate(targets):

            @pl.when(i == j)
            def _(ref=ref, at=at):
                ref[at] = out.astype(ref.dtype)

        return 0

    lax.fori_loop(0, len(targets), block, 0)


def token_parts(info, mine, other, weights, piece):
    cap, chunk = mine[0].shape
    depth, width = weights[0].shape
    pair = (2, piece, cap)
    return pl.pallas_call(
        back_kernel,
        grid_spec=pltpu.PrefetchScalarGridSpec(
            num_scalar_prefetch=1,
            grid=(1,),
            in_specs=[whole((cap, chunk))] * (2 * CHUNKS)
            + [pl.BlockSpec(memory_space=pltpu.VMEM)] * 2,
            out_specs=[whole(pair)] * 4,
            scratch_shapes=[pltpu.VMEM((width, cap), BF), pltpu.VMEM((width, cap), BF)],
        ),
        out_shape=[jax.ShapeDtypeStruct(pair, F32)] + [jax.ShapeDtypeStruct(pair, BF)] * 3,
        compiler_params=pltpu.CompilerParams(vmem_limit_bytes=16 * MIB),
        cost_estimate=pl.CostEstimate(
            flops=4 * cap * depth * width, bytes_accessed=4 * depth * width, transcendentals=0
        ),
    )(info, *mine, *other, *weights)


def after(x, waited):
    def kernel(value, _, out):
        out[...] = value[...]

    return pl.pallas_call(
        kernel,
        grid=(1,),
        in_specs=[whole(x.shape), pl.BlockSpec(memory_space=pl.ANY)],
        out_specs=whole(x.shape),
        out_shape=jax.ShapeDtypeStruct(x.shape, x.dtype),
        compiler_params=pltpu.CompilerParams(vmem_limit_bytes=4 * MIB),
    )(x, waited)


def far_kernel(n, n_z, info, *refs):
    out = refs[-1]
    for y in range(n // 2):
        for x in range(2):
            at = lax.rem((info[0] ^ (y + x * (n // 2))) - info[1] + n_z, n_z)
            out[at] = refs[y][x]


def far_operand(info, arrays, n, n_z):
    rows, cap = arrays[0].shape[1:]
    return pl.pallas_call(
        lambda *a: far_kernel(n, n_z, *a),
        grid_spec=pltpu.PrefetchScalarGridSpec(
            num_scalar_prefetch=1,
            grid=(1,),
            in_specs=[whole(a.shape) for a in arrays],
            out_specs=whole((n_z, rows, cap)),
        ),
        out_shape=jax.ShapeDtypeStruct((n_z, rows, cap), BF),
        compiler_params=pltpu.CompilerParams(vmem_limit_bytes=8 * MIB),
        cost_estimate=pl.CostEstimate(
            flops=0, bytes_accessed=4 * n * rows * cap, transcendentals=0
        ),
    )(info, *arrays)


def on_device(tokens, hidden_cot, w_gate, w_up, expert_ids, route_fixed):
    tok_dev, piece = tokens.shape
    width = w_gate.shape[1]
    n_tensor = lax.axis_size("tensor")
    n_dp = lax.axis_size("dp")
    n_z = n_dp // 4
    half = piece // 2
    xlo = n_tensor // 2
    t = lax.axis_index("tensor")
    dp = lax.axis_index("dp")
    z, xh, core = dp // 4, (dp // 2) % 2, dp % 2
    info = jnp.stack([t, z, xh, core]).astype(jnp.int32)
    tie = lax.optimization_barrier

    def over_tensor(x, k):
        return lax.ppermute(x, "tensor", [(i, i ^ k) for i in range(n_tensor)])

    def over_dp(x, k):
        return lax.ppermute(x, "dp", [(i, i ^ k) for i in range(n_dp)])

    def along_z(x, k):
        return lax.ppermute(x, "dp", [(i, (i + 4 * k) % n_dp) for i in range(n_dp)])

    selected = expert_ids == 0
    flag = jnp.any(selected, axis=1)
    place = jnp.arange(tok_dev, dtype=jnp.int32)
    upto = (place[:, None] <= place[None, :]).astype(BF)
    slot_of = jnp.dot(flag.astype(BF)[None, :], upto, preferred_element_type=F32)[0] - 1.0
    slot_of = jnp.where(flag, slot_of.astype(jnp.int32), -1)
    mask = slot_of[None, :] == jnp.arange(CAP, dtype=jnp.int32)[:, None]
    dispatch = mask.astype(BF)
    share_all = jnp.sum(jnp.where(selected, route_fixed, 0), axis=1).astype(F32) / 65536.0

    hidden_cot = pltpu.with_memory_space_constraint(hidden_cot, pltpu.HBM)
    tokens = pltpu.with_memory_space_constraint(tokens, pltpu.HBM)
    w_gate = pltpu.with_memory_space_constraint(w_gate, pltpu.HBM)
    w_up = pltpu.with_memory_space_constraint(w_up, pltpu.HBM)
    picked, far_piece = dispatch_tokens(info, slot_of[None, :], tokens)
    cot_rows, share = dispatch_cots(slot_of[None, :], share_all[None, :], hidden_cot)
    near = [None] * n_tensor
    near[xlo] = over_tensor(picked, xlo)
    near[1] = over_tensor(picked, 1)
    near[3] = over_tensor(picked, 3)
    far_piece = over_dp(far_piece, 2)
    picked, near[1], near[3], near[xlo], cot_rows, share = tie(
        (picked, near[1], near[3], near[xlo], cot_rows, share)
    )
    near[0] = picked
    near[xlo + 1] = over_tensor(near[1], xlo)
    near[xlo + 3] = over_tensor(near[3], xlo)
    near[2] = over_tensor(picked, 2)
    near[xlo + 2] = over_tensor(near[xlo], 2)
    soon, late = (0, xlo, 1, 3), (xlo + 1, xlo + 3, 2, xlo + 2)
    order = jnp.stack([t ^ k for k in soon + late] + [xh]).astype(jnp.int32)
    gate, up, near_soon, *weights = early(order, [near[k] for k in soon], w_gate, w_up)
    far_piece, near[late[0]] = tie((far_piece, near[late[0]]))
    far_pair = jnp.stack([far_piece, over_tensor(far_piece, xlo)])
    late_near, far_pair, gate, up = tie(([near[k] for k in late], far_pair, gate, up))
    outs = forward(
        info, late_near, soon, late, *weights, gate, up, near_soon, cot_rows, share, n_z
    )
    mine, other = outs[:CHUNKS], outs[CHUNKS : 2 * CHUNKS]
    near_left, route_part = outs[2 * CHUNKS :]

    def to_partners(c):
        return [mine[c], over_dp(other[c], 1), over_dp(mine[c], 2), over_dp(other[c], 3)]

    cots = [to_partners(0)]
    far_pair, near_left, mine, other, route_part, cots[0][1] = tie(
        (far_pair, near_left, mine, other, route_part, cots[0][1])
    )
    near_sib = over_dp(near_left, 1)
    far = [far_pair] + [over_tensor(far_pair, k) for k in (1, 3)]
    far_pair, near_sib = tie((far_pair, near_sib))
    far.insert(2, over_tensor(far_pair, 2))
    own_part, *sent = token_parts(info, mine, other, weights, piece)
    far, own_part, sent, mine, other = tie((far, own_part, sent, mine, other))
    far_left = far_operand(info, far, n_tensor, n_z)
    far_sib = over_dp(far_left, 1)
    for c in range(1, CHUNKS):
        mine, other, cots[-1] = tie((mine, other, cots[-1]))
        cots.append(to_partners(c))
    sums = {1: over_tensor(sent[0], 1)}

    def product(a, b):
        return jnp.dot(a.reshape(n_z * half, CAP), b, preferred_element_type=F32)

    class Ring:
        def __init__(self, c):
            base = product(lefts[0], cots[c][0]) + product(lefts[1], cots[c][1])
            base = tie(base) + product(far_left, cots[c][2])
            base = tie(base + product(far_sib, cots[c][3]))
            self.base = base.reshape(n_z, half, width // CHUNKS)
            self.up_hops = n_z // 2 - c % 2
            self.down_hops = n_z - 1 - self.up_hops
            self.rising = self.falling = None

        def part(self, j):
            return self.base[j]

        def hop(self, i):
            up, down = i < self.up_hops, i < self.down_hops
            if up:
                out = self.part(self.up_hops - i)
                rising = (out if i == 0 else out + self.rising.astype(F32)).astype(BF)
            if down:
                out = self.part((n_z - self.down_hops + i) % n_z)
                falling = (out if i == 0 else out + self.falling.astype(F32)).astype(BF)
            if up and down:
                rising, falling = tie((rising, falling))
            if up:
                self.rising = along_z(rising, 1)
            if down:
                self.falling = along_z(falling, -1)

        def finish(self):
            total = self.part(0) + self.rising.astype(F32) + self.falling.astype(F32)
            total = total.astype(BF).reshape(2, half // 2, width // CHUNKS)
            return total

    lefts = [near_left, near_sib]
    rings = []
    for c in range(CHUNKS):
        rings.append(Ring(c))
        lefts, rings[c].base = tie((lefts, rings[c].base))
    route_part = route_part.reshape(1, CAP)
    for i in range(n_z // 2):
        for ring in rings:
            ring.hop(i)
        waited = rings[0].rising
        if i < 2:
            sums[3 - i] = over_tensor(after(sent[1 + i], waited), 3 - i)
        if i < 3:
            route_part = after(route_part, waited)
            route_part = route_part + over_tensor(route_part, 1 << i)
    whole_rows = jnp.concatenate([ring.finish() for ring in rings], axis=2)
    kept = lax.dynamic_index_in_dim(whole_rows, core, 0, keepdims=False)
    swapped = over_dp(lax.dynamic_index_in_dim(whole_rows, 1 - core, 0, keepdims=False), 1)
    gate_grad = jnp.where(core == 0, kept, swapped)
    up_grad = jnp.where(core == 0, swapped, kept)

    total = own_part
    for k in (1, 2, 3):
        total = total + sums[k].astype(F32)
    total = total[0] + over_tensor(total[1].astype(BF), xlo).astype(F32)
    token_grad = lax.dot_general(
        dispatch, total.astype(BF), (((0,), (1,)), ((), ())), preferred_element_type=F32
    ).astype(BF)
    route_grad = jnp.sum(jnp.where(mask, route_part[0][:, None], 0.0), axis=0)
    return token_grad, gate_grad, up_grad, route_grad


def solution(mesh):
    return jax.shard_map(
        on_device,
        mesh=mesh,
        in_specs=(
            P("dp", "tensor"),
            P("dp", "tensor"),
            P(None, "tensor"),
            P(None, "tensor"),
            P("dp", None),
            P("dp", None),
        ),
        out_specs=(P("dp", "tensor"), P("dp", "tensor"), P("dp", "tensor"), P("dp")),
        check_vma=False,
    )
```

profile of v0, /device:TPU:2, one launch (start us, length us, event | category | flops | bytes accessed | tf_op | source)
XLA Modules:
  0.0 129.5 jit_solution(8997855161164550957)
XLA Ops:
  1.6 1.9 %shard_map.93 = (bf16[256,384]{1,0:T(8,128)(2,1)S(1)}, bf16[192,256]{1,0:T(8,128)(2,1)S(1)}) custom-call(s32[4]{0:T(128)S(1)} %pad_add_fusion.info.a_0_, s32[1,512]{1,0:T(1,128)S(1)} %bitcast.126, bf16[512,384]{1,0:T(8,128)(2,1)} %tokens.1), custom_call_target="tpu_custom_call" | custom-call | flops 100663296 | bytes 786432 | tf_op jit(solution)/shard_map/pallas_call | solution.py:33
  3.6 1.7 %collective-permute-start.1 = (bf16[256,384]{1,0:T(8,128)(2,1)S(1)}, bf16[256,384]{1,0:T(8,128)(2,1)S(1)}, u32[]{:S(2)}, u32[]{:S(2)}) collective-permute-start(bf16[256,384]{1,0:T(8,128)(2,1)S(1)} %get-tuple-element.87.a_1_), channel_id=1, source_target_pairs={{0,1},{1,0},{2,3},{3,2},{4,5},{5,4},{6,7},{7,6},{8,9},{9,8},{10,11... | collective-permute-start | bytes 589832 | tf_op jit(solution)/shard_map/ppermute | solution.py:336
  5.2 2.2 %collective-permute-start.2 = (bf16[256,384]{1,0:T(8,128)(2,1)S(1)}, bf16[256,384]{1,0:T(8,128)(2,1)S(1)}, u32[]{:S(2)}, u32[]{:S(2)}) collective-permute-start(bf16[256,384]{1,0:T(8,128)(2,1)S(1)} %get-tuple-element.87.a_1_), channel_id=1, source_target_pairs={{0,3},{1,2},{2,1},{3,0},{4,7},{5,6},{6,5},{7,4},{8,11},{9,10},{10,... | collective-permute-start | bytes 589832 | tf_op jit(solution)/shard_map/ppermute | solution.py:336
  8.7 1.7 %shard_map.94 = (bf16[256,1024]{1,0:T(8,128)(2,1)S(1)}, f32[256,1]{1,0:T(8,128)S(1)}) custom-call(s32[1,512]{1,0:T(1,128)S(1)} %bitcast.127, f32[1,512]{1,0:T(1,128)S(1)} %bitcast.128, bf16[512,1024]{1,0:T(8,128)(2,1)} %cot.1), custom_call_target="tpu_custom_call" | custom-call | flops 268435456 | bytes 2097152 | tf_op jit(solution)/shard_map/pallas_call | solution.py:63
  10.4 2.4 %collective-permute-done.2.a_4_ = bf16[256,384]{1,0:T(8,128)(2,1)S(1)} collective-permute-done((bf16[256,384]{1,0:T(8,128)(2,1)S(1)}, bf16[256,384]{1,0:T(8,128)(2,1)S(1)}, u32[]{:S(2)}, u32[]{:S(2)}) %collective-permute-start.2) | collective-permute-done | bytes 196640 | tf_op jit(solution)/shard_map/ppermute | solution.py:336
  14.0 2.4 %collective-permute-start = (bf16[192,256]{1,0:T(8,128)(2,1)S(1)}, bf16[192,256]{1,0:T(8,128)(2,1)S(1)}, u32[]{:S(2)}, u32[]{:S(2)}) collective-permute-start(bf16[192,256]{1,0:T(8,128)(2,1)S(1)} %get-tuple-element.80), channel_id=1, source_target_pairs={{0,16},{8,24},{16,0},{24,8},{32,48},{40,56},{48,32},{56,40},{64,80... | collective-permute-start | bytes 294920 | tf_op jit(solution)/shard_map/ppermute | solution.py:339
  16.5 1.8 %collective-permute-start.5 = (bf16[256,384]{1,0:T(8,128)(2,1)S(1)}, bf16[256,384]{1,0:T(8,128)(2,1)S(1)}, u32[]{:S(2)}, u32[]{:S(2)}) collective-permute-start(bf16[256,384]{1,0:T(8,128)(2,1)S(1)} %collective-permute-done.2.a_4_), channel_id=1, source_target_pairs={{0,4},{1,5},{2,6},{3,7},{4,0},{5,1},{6,2},{7,3},{8,12},{9,13},{10,... | collective-permute-start | bytes 589832 | tf_op jit(solution)/shard_map/ppermute | solution.py:336
  18.4 1.0 collective-permute-start.6
  19.4 2.5 %collective-permute-start.7 = (bf16[256,384]{1,0:T(8,128)(2,1)S(1)}, bf16[256,384]{1,0:T(8,128)(2,1)S(1)}, u32[]{:S(2)}, u32[]{:S(2)}) collective-permute-start(bf16[256,384]{1,0:T(8,128)(2,1)S(1)} %collective-permute-done.3.a_2_), channel_id=1, source_target_pairs={{0,2},{1,3},{2,0},{3,1},{4,6},{5,7},{6,4},{7,5},{8,10},{9,11},{10,... | collective-permute-start | bytes 589832 | tf_op jit(solution)/shard_map/ppermute | solution.py:336
  21.9 2.5 %collective-permute-done = bf16[192,256]{1,0:T(8,128)(2,1)S(1)} collective-permute-done((bf16[192,256]{1,0:T(8,128)(2,1)S(1)}, bf16[192,256]{1,0:T(8,128)(2,1)S(1)}, u32[]{:S(2)}, u32[]{:S(2)}) %collective-permute-start) | collective-permute-done | bytes 98336 | tf_op jit(solution)/shard_map/ppermute | solution.py:339
  24.4 1.8 %collective-permute-start.8 = (bf16[192,256]{1,0:T(8,128)(2,1)S(1)}, bf16[192,256]{1,0:T(8,128)(2,1)S(1)}, u32[]{:S(2)}, u32[]{:S(2)}) collective-permute-start(bf16[192,256]{1,0:T(8,128)(2,1)S(1)} %collective-permute-done), channel_id=1, source_target_pairs={{0,4},{1,5},{2,6},{3,7},{4,0},{5,1},{6,2},{7,3},{8,12},{9,13},{10,... | collective-permute-start | bytes 294920 | tf_op jit(solution)/shard_map/ppermute | solution.py:336
  26.2 5.5 %shard_map.95 = (f32[256,1024]{1,0:T(8,128)S(1)}, f32[256,1024]{1,0:T(8,128)S(1)}, bf16[4,192,256]{2,1,0:T(8,128)(2,1)S(1)}, bf16[3072,1024]{1,0:T(8,128)(2,1)S(1)}, bf16[3072,1024]{1,0:T(8,128)(2,1)S(1)}) custom-call(s32[9]{0:T(128)S(1)} %stack.65.a_0_, bf16[256,384]{1,0:T(8,128)(2,1)S(1)} %get-tuple-element.87.a_1_, ...), custom_call_target="tpu_custom_call" | custom-call | flops 1610612736 | bytes 12582912 | tf_op jit(solution)/shard_map/pallas_call | solution.py:127
  31.8 4.6 %shard_map.96 = (bf16[256,512]{1,0:T(8,128)(2,1)S(1)}, bf16[256,512]{1,0:T(8,128)(2,1)S(1)}, bf16[256,512]{1,0:T(8,128)(2,1)}, bf16[256,512]{1,0:T(8,128)(2,1)S(...) custom-call(s32[4]{0:T(128)S(1)} %pad_add_fusion.info.a_0_, ...), custom_call_target="tpu_custom_call" | custom-call | flops 1610612736 | bytes 4194304 | tf_op jit(solution)/shard_map/pallas_call | solution.py:210
  37.0 1.7 %collective-permute-done.9 = bf16[256,512]{1,0:T(8,128)(2,1)S(1)} collective-permute-done((bf16[256,512]{1,0:T(8,128)(2,1)}, bf16[256,512]{1,0:T(8,128)(2,1)S(1)}, u32[]{:S(2)}, u32[]{:S(2)}) %collective-permute-start.9) | collective-permute-done | bytes 262176 | tf_op jit(solution)/shard_map/ppermute | solution.py:339
  39.5 2.7 %collective-permute-start.16 = (bf16[256,512]{1,0:T(8,128)(2,1)}, bf16[256,512]{1,0:T(8,128)(2,1)}, u32[]{:S(2)}, u32[]{:S(2)}) collective-permute-start(bf16[256,512]{1,0:T(8,128)(2,1)} %get-tuple-element.115.refs_2_), channel_id=1, source_target_pairs={{0,24},{8,16},{16,8},{24,0},{32,56},{40,48},{48,40},{56,32},{64,88... | collective-permute-start | bytes 786440 | tf_op jit(solution)/shard_map/ppermute | solution.py:339
  42.8 0.9 collective-permute-start.13
  43.7 0.9 copy-done.5
  44.6 2.5 %collective-permute-start.12 = (bf16[2,192,256]{2,1,0:T(8,128)(2,1)S(1)}, bf16[2,192,256]{2,1,0:T(8,128)(2,1)S(1)}, u32[]{:S(2)}, u32[]{:S(2)}) collective-permute-start(bf16[2,192,256]{2,1,0:T(8,128)(2,1)S(1)} %pad_maximum_fusion.a_1_), channel_id=1, source_target_pairs={{0,2},{1,3},{2,0},{3,1},{4,6},{5,7},{6,4},{7,5},{8,10},{9,11},{10,... | collective-permute-start | bytes 589832 | tf_op jit(solution)/shard_map/ppermute | solution.py:336
  47.1 6.8 %shard_map.97 = (f32[2,384,256]{2,1,0:T(8,128)S(1)}, bf16[2,384,256]{2,1,0:T(8,128)(2,1)S(1)}, bf16[2,384,256]{2,1,0:T(8,128)(2,1)S(1)}, bf16[2,384,256]{2,1,0:T(8,128)(2,1)S(1)}) custom-call(s32[4]{0:T(128)S(1)} %pad_add_fusion.info.a_0_, bf16[256,512]{1,0:T(8,128)(2,1)S(1)} %get-tuple-element.128.refs_0_, bf16[256,512]{1,0:T(8,128)(2,1)S(1)} %get-tuple-element.146.refs_1_, ...), custom_call_target="tpu_custom_call" | custom-call | flops 3221225472 | bytes 12582912 | tf_op jit(solution)/shard_map/pallas_call | solution.py:263
  54.0 1.2 collective-permute-done.13.a_4_
  56.0 1.0 reduce
  57.7 1.8 %fusion.29 = f32[1536,512]{1,0:T(8,128)S(1)} fusion(bf16[1536,256]{1,0:T(8,128)(2,1)} %bitcast.140, bf16[256,512]{1,0:T(8,128)(2,1)} %copy-done.7), kind=kOutput, calls=%fused_computation.66 | convolution fusion | flops 402653184 | bytes 4194304 | tf_op jit(solution)/shard_map/dot_general | solution.py:406
  60.6 3.0 %collective-permute-start.29 = (bf16[256,512]{1,0:T(8,128)(2,1)S(1)}, bf16[256,512]{1,0:T(8,128)(2,1)S(1)}, u32[]{:S(2)}, u32[]{:S(2)}) collective-permute-start(bf16[256,512]{1,0:T(8,128)(2,1)S(1)} %get-tuple-element.146.refs_1_), channel_id=1, source_target_pairs={{0,16},{8,24},{16,0},{24,8},{32,48},{40,56},{48,32},{56,40},{64,80... | collective-permute-start | bytes 786440 | tf_op jit(solution)/shard_map/ppermute | solution.py:339
  63.6 1.7 %fusion.30 = f32[1536,512]{1,0:T(8,128)S(1)} fusion(bf16[1536,256]{1,0:T(8,128)(2,1)} %bitcast.19, bf16[256,512]{1,0:T(8,128)(2,1)} %collective-permute-done.16), kind=kOutput, calls=%fused_computation.67 | convolution fusion | flops 402653184 | bytes 4194304 | tf_op jit(solution)/shard_map/dot_general | solution.py:406
  65.4 1.5 %fusion.1 = f32[1536,512]{1,0:T(8,128)S(1)} fusion(f32[1536,512]{1,0:T(8,128)S(1)} %fusion.30, f32[1536,512]{1,0:T(8,128)S(1)} %convolution_add_fusion.3, bf16[1536,256]{1,0:T(8,128)(2,1)S(1)} %bitcast.122, bf16[256,512]{1,0:T(8,128)(2,1)} %collective-permute-done.15), kind=kOutput, calls=%fused_computation.4 | convolution fusion | flops 404226048 | bytes 10485760 | tf_op jit(solution)/shard_map/dot_general | solution.py:406
  67.2 2.0 %collective-permute-start.18 = (bf16[192,512]{1,0:T(8,128)(2,1)S(1)}, bf16[192,512]{1,0:T(8,128)(2,1)S(1)}, u32[]{:S(2)}, u32[]{:S(2)}) collective-permute-start(bf16[192,512]{1,0:T(8,128)(2,1)S(1)} %get-tuple-element.137), channel_id=1, source_target_pairs={{0,32},{8,40},{16,48},{24,56},{32,64},{40,72},{48,80},{56,88},{64,... | collective-permute-start | bytes 589832 | tf_op jit(solution)/shard_map/ppermute | solution.py:342
  69.2 4.0 %collective-permute-start.19 = (bf16[192,512]{1,0:T(8,128)(2,1)S(1)}, bf16[192,512]{1,0:T(8,128)(2,1)S(1)}, u32[]{:S(2)}, u32[]{:S(2)}) collective-permute-start(bf16[192,512]{1,0:T(8,128)(2,1)S(1)} %get-tuple-element.138), channel_id=1, source_target_pairs={{0,224},{8,232},{16,240},{24,248},{32,0},{40,8},{48,16},{56,24},{6... | collective-permute-start | bytes 589832 | tf_op jit(solution)/shard_map/ppermute | solution.py:342
  74.4 1.7 %fusion.32 = f32[1536,512]{1,0:T(8,128)S(1)} fusion(bf16[1536,256]{1,0:T(8,128)(2,1)} %bitcast.19, bf16[256,512]{1,0:T(8,128)(2,1)S(1)} %collective-permute-done.30), kind=kOutput, calls=%fused_computation.69 | convolution fusion | flops 402653184 | bytes 4194304 | tf_op jit(solution)/shard_map/dot_general | solution.py:406
  77.0 2.6 %collective-permute-start.32 = (bf16[192,512]{1,0:T(8,128)(2,1)S(1)}, bf16[192,512]{1,0:T(8,128)(2,1)S(1)}, u32[]{:S(2)}, u32[]{:S(2)}) collective-permute-start(bf16[192,512]{1,0:T(8,128)(2,1)S(1)} %get-tuple-element.150), channel_id=1, source_target_pairs={{0,224},{8,232},{16,240},{24,248},{32,0},{40,8},{48,16},{56,24},{6... | collective-permute-start | bytes 589832 | tf_op jit(solution)/shard_map/ppermute | solution.py:342
  79.7 1.2 collective-permute-start.22
  81.3 2.3 %collective-permute-done.32 = bf16[192,512]{1,0:T(8,128)(2,1)S(1)} collective-permute-done((bf16[192,512]{1,0:T(8,128)(2,1)S(1)}, bf16[192,512]{1,0:T(8,128)(2,1)S(1)}, u32[]{:S(2)}, u32[]{:S(2)}) %collective-permute-start.32) | collective-permute-done | bytes 196640 | tf_op jit(solution)/shard_map/ppermute | solution.py:342
  83.7 3.5 %collective-permute-start.24 = (bf16[192,512]{1,0:T(8,128)(2,1)S(1)}, bf16[192,512]{1,0:T(8,128)(2,1)S(1)}, u32[]{:S(2)}, u32[]{:S(2)}) collective-permute-start(bf16[192,512]{1,0:T(8,128)(2,1)S(1)} %get-tuple-element.141), channel_id=1, source_target_pairs={{0,224},{8,232},{16,240},{24,248},{32,0},{40,8},{48,16},{56,24},{6... | collective-permute-start | bytes 589832 | tf_op jit(solution)/shard_map/ppermute | solution.py:342
  87.2 1.5 %collective-permute-done.31 = bf16[192,512]{1,0:T(8,128)(2,1)S(1)} collective-permute-done((bf16[192,512]{1,0:T(8,128)(2,1)S(1)}, bf16[192,512]{1,0:T(8,128)(2,1)S(1)}, u32[]{:S(2)}, u32[]{:S(2)}) %collective-permute-start.31) | collective-permute-done | bytes 196640 | tf_op jit(solution)/shard_map/ppermute | solution.py:342
  88.7 1.2 collective-permute-start.39
  90.1 2.2 %collective-permute-done.39 = f32[1,256]{1,0:T(1,128)S(1)} collective-permute-done((f32[1,256]{1,0:T(1,128)S(1)}, f32[1,256]{1,0:T(1,128)S(1)}, u32[]{:S(2)}, u32[]{:S(2)}) %collective-permute-start.39) | collective-permute-done | bytes 1056 | tf_op jit(solution)/shard_map/ppermute | solution.py:336
  92.3 2.0 %collective-permute-start.33 = (bf16[192,512]{1,0:T(8,128)(2,1)S(1)}, bf16[192,512]{1,0:T(8,128)(2,1)S(1)}, u32[]{:S(2)}, u32[]{:S(2)}) collective-permute-start(bf16[192,512]{1,0:T(8,128)(2,1)S(1)} %get-tuple-element.151), channel_id=1, source_target_pairs={{0,32},{8,40},{16,48},{24,56},{32,64},{40,72},{48,80},{56,88},{64,... | collective-permute-start | bytes 589832 | tf_op jit(solution)/shard_map/ppermute | solution.py:342
  94.3 1.9 %collective-permute-start.21 = (bf16[2,384,256]{2,1,0:T(8,128)(2,1)S(1)}, bf16[2,384,256]{2,1,0:T(8,128)(2,1)S(1)}, u32[]{:S(2)}, u32[]{:S(2)}) collective-permute-start(bf16[2,384,256]{2,1,0:T(8,128)(2,1)S(1)} %shard_map.99), channel_id=1, source_target_pairs={{0,2},{1,3},{2,0},{3,1},{4,6},{5,7},{6,4},{7,5},{8,10},{9,11},{10,... | collective-permute-start | bytes 1179656 | tf_op jit(solution)/shard_map/ppermute | solution.py:336
  96.4 1.6 %collective-permute-done.34 = bf16[192,512]{1,0:T(8,128)(2,1)S(1)} collective-permute-done((bf16[192,512]{1,0:T(8,128)(2,1)S(1)}, bf16[192,512]{1,0:T(8,128)(2,1)S(1)}, u32[]{:S(2)}, u32[]{:S(2)}) %collective-permute-start.34) | collective-permute-done | bytes 196640 | tf_op jit(solution)/shard_map/ppermute | solution.py:342
  97.9 3.1 %collective-permute-done.33 = bf16[192,512]{1,0:T(8,128)(2,1)S(1)} collective-permute-done((bf16[192,512]{1,0:T(8,128)(2,1)S(1)}, bf16[192,512]{1,0:T(8,128)(2,1)S(1)}, u32[]{:S(2)}, u32[]{:S(2)}) %collective-permute-start.33) | collective-permute-done | bytes 196640 | tf_op jit(solution)/shard_map/ppermute | solution.py:342
  101.0 1.7 %collective-permute-start.40 = (f32[1,256]{1,0:T(1,128)S(1)}, f32[1,256]{1,0:T(1,128)S(1)}, u32[]{:S(2)}, u32[]{:S(2)}) collective-permute-start(f32[1,256]{1,0:T(1,128)S(1)} %shard_map.102), channel_id=1, source_target_pairs={{0,2},{1,3},{2,0},{3,1},{4,6},{5,7},{6,4},{7,5},{8,10},{9,11},{10,... | collective-permute-start | bytes 3080 | tf_op jit(solution)/shard_map/ppermute | solution.py:336
  102.9 3.2 %collective-permute-done.40 = f32[1,256]{1,0:T(1,128)S(1)} collective-permute-done((f32[1,256]{1,0:T(1,128)S(1)}, f32[1,256]{1,0:T(1,128)S(1)}, u32[]{:S(2)}, u32[]{:S(2)}) %collective-permute-start.40) | collective-permute-done | bytes 1056 | tf_op jit(solution)/shard_map/ppermute | solution.py:336
  106.7 7.2 %collective-permute-done.36 = bf16[192,512]{1,0:T(8,128)(2,1)S(1)} collective-permute-done((bf16[192,512]{1,0:T(8,128)(2,1)S(1)}, bf16[192,512]{1,0:T(8,128)(2,1)S(1)}, u32[]{:S(2)}, u32[]{:S(2)}) %collective-permute-start.36) | collective-permute-done | bytes 196640 | tf_op jit(solution)/shard_map/ppermute | solution.py:342
  114.2 3.4 %collective-permute-done.41 = f32[1,256]{1,0:T(1,128)S(1)} collective-permute-done((f32[1,256]{1,0:T(1,128)S(1)}, f32[1,256]{1,0:T(1,128)S(1)}, u32[]{:S(2)}, u32[]{:S(2)}) %collective-permute-start.41) | collective-permute-done | bytes 1056 | tf_op jit(solution)/shard_map/ppermute | solution.py:336
  118.3 1.0 collective-permute-start.26
  119.2 2.4 %collective-permute-start.37 = (bf16[192,512]{1,0:T(8,128)(2,1)S(1)}, bf16[192,512]{1,0:T(8,128)(2,1)S(1)}, u32[]{:S(2)}, u32[]{:S(2)}) collective-permute-start(bf16[192,512]{1,0:T(8,128)(2,1)S(1)} %fusion.6), channel_id=1, source_target_pairs={{0,224},{8,232},{16,240},{24,248},{32,0},{40,8},{48,16},{56,24},{6... | collective-permute-start | bytes 589832 | tf_op jit(solution)/shard_map/ppermute | solution.py:342
  122.1 4.4 %collective-permute-done.26 = bf16[192,512]{1,0:T(8,128)(2,1)S(1)} collective-permute-done((bf16[192,512]{1,0:T(8,128)(2,1)S(1)}, bf16[192,512]{1,0:T(8,128)(2,1)S(1)}, u32[]{:S(2)}, u32[]{:S(2)}) %collective-permute-start.26) | collective-permute-done | bytes 196640 | tf_op jit(solution)/shard_map/ppermute | solution.py:342
  127.6 1.1 convolution_convert_fusion
  128.7 0.8 broadcast_select_fusion
  (102 shorter events, 14.6 us)
Async XLA Ops:
  3.6 6.8 %collective-permute-start.1 = (bf16[256,384]{1,0:T(8,128)(2,1)S(1)}, bf16[256,384]{1,0:T(8,128)(2,1)S(1)}, u32[]{:S(2)}, u32[]{:S(2)}) collective-permute-start(bf16[256,384]{1,0:T(8,128)(2,1)S(1)} %get-tuple-element.87.a_1_), channel_id=1, source_target_pairs={{0,1},{1,0},{2,3},{3,2},{4,5},{5,4},{6,7},{7,6},{8,9},{9,8},{10,11... | collective-permute-start | bytes 589832 | tf_op jit(solution)/shard_map/ppermute | solution.py:336
  5.2 7.6 %collective-permute-start.2 = (bf16[256,384]{1,0:T(8,128)(2,1)S(1)}, bf16[256,384]{1,0:T(8,128)(2,1)S(1)}, u32[]{:S(2)}, u32[]{:S(2)}) collective-permute-start(bf16[256,384]{1,0:T(8,128)(2,1)S(1)} %get-tuple-element.87.a_1_), channel_id=1, source_target_pairs={{0,3},{1,2},{2,1},{3,0},{4,7},{5,6},{6,5},{7,4},{8,11},{9,10},{10,... | collective-permute-start | bytes 589832 | tf_op jit(solution)/shard_map/ppermute | solution.py:336
  7.4 6.1 %collective-permute-start.3 = (bf16[256,384]{1,0:T(8,128)(2,1)S(1)}, bf16[256,384]{1,0:T(8,128)(2,1)S(1)}, u32[]{:S(2)}, u32[]{:S(2)}) collective-permute-start(bf16[256,384]{1,0:T(8,128)(2,1)S(1)} %get-tuple-element.87.a_1_), channel_id=1, source_target_pairs={{0,4},{1,5},{2,6},{3,7},{4,0},{5,1},{6,2},{7,3},{8,12},{9,13},{10,... | collective-permute-start | bytes 589832 | tf_op jit(solution)/shard_map/ppermute | solution.py:336
  13.5 10.9 %collective-permute-start.4 = (bf16[256,384]{1,0:T(8,128)(2,1)S(1)}, bf16[256,384]{1,0:T(8,128)(2,1)S(1)}, u32[]{:S(2)}, u32[]{:S(2)}) collective-permute-start(bf16[256,384]{1,0:T(8,128)(2,1)S(1)} %collective-permute-done.1.a_3_), channel_id=1, source_target_pairs={{0,4},{1,5},{2,6},{3,7},{4,0},{5,1},{6,2},{7,3},{8,12},{9,13},{10,... | collective-permute-start | bytes 589832 | tf_op jit(solution)/shard_map/ppermute | solution.py:336
  14.0 10.3 %collective-permute-start = (bf16[192,256]{1,0:T(8,128)(2,1)S(1)}, bf16[192,256]{1,0:T(8,128)(2,1)S(1)}, u32[]{:S(2)}, u32[]{:S(2)}) collective-permute-start(bf16[192,256]{1,0:T(8,128)(2,1)S(1)} %get-tuple-element.80), channel_id=1, source_target_pairs={{0,16},{8,24},{16,0},{24,8},{32,48},{40,56},{48,32},{56,40},{64,80... | collective-permute-start | bytes 294920 | tf_op jit(solution)/shard_map/ppermute | solution.py:339
  16.5 15.2 %collective-permute-start.5 = (bf16[256,384]{1,0:T(8,128)(2,1)S(1)}, bf16[256,384]{1,0:T(8,128)(2,1)S(1)}, u32[]{:S(2)}, u32[]{:S(2)}) collective-permute-start(bf16[256,384]{1,0:T(8,128)(2,1)S(1)} %collective-permute-done.2.a_4_), channel_id=1, source_target_pairs={{0,4},{1,5},{2,6},{3,7},{4,0},{5,1},{6,2},{7,3},{8,12},{9,13},{10,... | collective-permute-start | bytes 589832 | tf_op jit(solution)/shard_map/ppermute | solution.py:336
  18.4 13.4 %collective-permute-start.6 = (bf16[256,384]{1,0:T(8,128)(2,1)S(1)}, bf16[256,384]{1,0:T(8,128)(2,1)S(1)}, u32[]{:S(2)}, u32[]{:S(2)}) collective-permute-start(bf16[256,384]{1,0:T(8,128)(2,1)S(1)} %get-tuple-element.87.a_1_), channel_id=1, source_target_pairs={{0,2},{1,3},{2,0},{3,1},{4,6},{5,7},{6,4},{7,5},{8,10},{9,11},{10,... | collective-permute-start | bytes 589832 | tf_op jit(solution)/shard_map/ppermute | solution.py:336
  19.4 12.4 %collective-permute-start.7 = (bf16[256,384]{1,0:T(8,128)(2,1)S(1)}, bf16[256,384]{1,0:T(8,128)(2,1)S(1)}, u32[]{:S(2)}, u32[]{:S(2)}) collective-permute-start(bf16[256,384]{1,0:T(8,128)(2,1)S(1)} %collective-permute-done.3.a_2_), channel_id=1, source_target_pairs={{0,2},{1,3},{2,0},{3,1},{4,6},{5,7},{6,4},{7,5},{8,10},{9,11},{10,... | collective-permute-start | bytes 589832 | tf_op jit(solution)/shard_map/ppermute | solution.py:336
  24.4 7.3 %collective-permute-start.8 = (bf16[192,256]{1,0:T(8,128)(2,1)S(1)}, bf16[192,256]{1,0:T(8,128)(2,1)S(1)}, u32[]{:S(2)}, u32[]{:S(2)}) collective-permute-start(bf16[192,256]{1,0:T(8,128)(2,1)S(1)} %collective-permute-done), channel_id=1, source_target_pairs={{0,4},{1,5},{2,6},{3,7},{4,0},{5,1},{6,2},{7,3},{8,12},{9,13},{10,... | collective-permute-start | bytes 294920 | tf_op jit(solution)/shard_map/ppermute | solution.py:336
  37.0 1.7 %collective-permute-start.9 = (bf16[256,512]{1,0:T(8,128)(2,1)}, bf16[256,512]{1,0:T(8,128)(2,1)S(1)}, u32[]{:S(2)}, u32[]{:S(2)}) collective-permute-start(bf16[256,512]{1,0:T(8,128)(2,1)} %get-tuple-element.115.refs_2_), channel_id=1, source_target_pairs={{0,8},{8,0},{16,24},{24,16},{32,40},{40,32},{48,56},{56,48},{64,72... | collective-permute-start | bytes 786440 | tf_op jit(solution)/shard_map/ppermute | solution.py:339
  38.8 4.9 %collective-permute-start.11 = (bf16[8,192,256]{2,1,0:T(8,128)(2,1)S(1)}, bf16[8,192,256]{2,1,0:T(8,128)(2,1)S(1)}, u32[]{:S(2)}, u32[]{:S(2)}) collective-permute-start(bf16[8,192,256]{2,1,0:T(8,128)(2,1)S(1)} %get-tuple-element.144), channel_id=1, source_target_pairs={{0,8},{8,0},{16,24},{24,16},{32,40},{40,32},{48,56},{56,48},{64,72... | collective-permute-start | bytes 2359304 | tf_op jit(solution)/shard_map/ppermute | solution.py:339
  38.9 18.1 %collective-permute-start.15 = (bf16[256,512]{1,0:T(8,128)(2,1)S(1)}, bf16[256,512]{1,0:T(8,128)(2,1)}, u32[]{:S(2)}, u32[]{:S(2)}) collective-permute-start(bf16[256,512]{1,0:T(8,128)(2,1)S(1)} %get-tuple-element.128.refs_0_), channel_id=1, source_target_pairs={{0,16},{8,24},{16,0},{24,8},{32,48},{40,56},{48,32},{56,40},{64,80... | collective-permute-start | bytes 786440 | tf_op jit(solution)/shard_map/ppermute | solution.py:339
  39.5 17.5 %collective-permute-start.16 = (bf16[256,512]{1,0:T(8,128)(2,1)}, bf16[256,512]{1,0:T(8,128)(2,1)}, u32[]{:S(2)}, u32[]{:S(2)}) collective-permute-start(bf16[256,512]{1,0:T(8,128)(2,1)} %get-tuple-element.115.refs_2_), channel_id=1, source_target_pairs={{0,24},{8,16},{16,8},{24,0},{32,56},{40,48},{48,40},{56,32},{64,88... | collective-permute-start | bytes 786440 | tf_op jit(solution)/shard_map/ppermute | solution.py:339
  42.1 11.9 %collective-permute-start.10 = (bf16[2,192,256]{2,1,0:T(8,128)(2,1)S(1)}, bf16[2,192,256]{2,1,0:T(8,128)(2,1)S(1)}, u32[]{:S(2)}, u32[]{:S(2)}) collective-permute-start(bf16[2,192,256]{2,1,0:T(8,128)(2,1)S(1)} %pad_maximum_fusion.a_1_), channel_id=1, source_target_pairs={{0,1},{1,0},{2,3},{3,2},{4,5},{5,4},{6,7},{7,6},{8,9},{9,8},{10,11... | collective-permute-start | bytes 589832 | tf_op jit(solution)/shard_map/ppermute | solution.py:336
  42.8 12.4 %collective-permute-start.13 = (bf16[2,192,256]{2,1,0:T(8,128)(2,1)S(1)}, bf16[2,192,256]{2,1,0:T(8,128)(2,1)S(1)}, u32[]{:S(2)}, u32[]{:S(2)}) collective-permute-start(bf16[2,192,256]{2,1,0:T(8,128)(2,1)S(1)} %pad_maximum_fusion.a_1_), channel_id=1, source_target_pairs={{0,3},{1,2},{2,1},{3,0},{4,7},{5,6},{6,5},{7,4},{8,11},{9,10},{10,... | collective-permute-start | bytes 589832 | tf_op jit(solution)/shard_map/ppermute | solution.py:336
  43.7 0.9 copy-start.5
  44.6 10.6 %collective-permute-start.12 = (bf16[2,192,256]{2,1,0:T(8,128)(2,1)S(1)}, bf16[2,192,256]{2,1,0:T(8,128)(2,1)S(1)}, u32[]{:S(2)}, u32[]{:S(2)}) collective-permute-start(bf16[2,192,256]{2,1,0:T(8,128)(2,1)S(1)} %pad_maximum_fusion.a_1_), channel_id=1, source_target_pairs={{0,2},{1,3},{2,0},{3,1},{4,6},{5,7},{6,4},{7,5},{8,10},{9,11},{10,... | collective-permute-start | bytes 589832 | tf_op jit(solution)/shard_map/ppermute | solution.py:336
  54.0 1.8 %copy-start = (bf16[2,384,256]{2,1,0:T(8,128)(2,1)}, bf16[2,384,256]{2,1,0:T(8,128)(2,1)S(1)}, u32[]{:S(2)}) copy-start(bf16[2,384,256]{2,1,0:T(8,128)(2,1)S(1)} %get-tuple-element.140.value) | copy-start | bytes 1179652
  54.0 1.8 %copy-start.3 = (bf16[2,384,256]{2,1,0:T(8,128)(2,1)}, bf16[2,384,256]{2,1,0:T(8,128)(2,1)S(1)}, u32[]{:S(2)}) copy-start(bf16[2,384,256]{2,1,0:T(8,128)(2,1)S(1)} %get-tuple-element.122) | copy-start | bytes 1179652
  55.8 7.8 %collective-permute-start.17 = (bf16[8,192,256]{2,1,0:T(8,128)(2,1)S(1)}, bf16[8,192,256]{2,1,0:T(8,128)(2,1)}, u32[]{:S(2)}, u32[]{:S(2)}) collective-permute-start(bf16[8,192,256]{2,1,0:T(8,128)(2,1)S(1)} %shard_map.98), channel_id=1, source_target_pairs={{0,8},{8,0},{16,24},{24,16},{32,40},{40,32},{48,56},{56,48},{64,72... | collective-permute-start | bytes 2359304 | tf_op jit(solution)/shard_map/ppermute | solution.py:339
  57.0 17.4 %collective-permute-start.30 = (bf16[256,512]{1,0:T(8,128)(2,1)S(1)}, bf16[256,512]{1,0:T(8,128)(2,1)S(1)}, u32[]{:S(2)}, u32[]{:S(2)}) collective-permute-start(bf16[256,512]{1,0:T(8,128)(2,1)S(1)} %get-tuple-element.147.refs_3_), channel_id=1, source_target_pairs={{0,24},{8,16},{16,8},{24,0},{32,56},{40,48},{48,40},{56,32},{64,88... | collective-permute-start | bytes 786440 | tf_op jit(solution)/shard_map/ppermute | solution.py:339
  57.7 11.5 %collective-permute-start.28 = (bf16[256,512]{1,0:T(8,128)(2,1)S(1)}, bf16[256,512]{1,0:T(8,128)(2,1)S(1)}, u32[]{:S(2)}, u32[]{:S(2)}) collective-permute-start(bf16[256,512]{1,0:T(8,128)(2,1)S(1)} %get-tuple-element.147.refs_3_), channel_id=1, source_target_pairs={{0,8},{8,0},{16,24},{24,16},{32,40},{40,32},{48,56},{56,48},{64,72... | collective-permute-start | bytes 786440 | tf_op jit(solution)/shard_map/ppermute | solution.py:339
  59.5 1.0 copy-start.4
  60.5 57.8 %collective-permute-start.14 = (bf16[2,384,256]{2,1,0:T(8,128)(2,1)S(1)}, bf16[2,384,256]{2,1,0:T(8,128)(2,1)S(1)}, u32[]{:S(2)}, u32[]{:S(2)}) collective-permute-start(bf16[2,384,256]{2,1,0:T(8,128)(2,1)S(1)} %copy-done.4), channel_id=1, source_target_pairs={{0,1},{1,0},{2,3},{3,2},{4,5},{5,4},{6,7},{7,6},{8,9},{9,8},{10,11... | collective-permute-start | bytes 1179656 | tf_op jit(solution)/shard_map/ppermute | solution.py:336
  60.6 15.5 %collective-permute-start.29 = (bf16[256,512]{1,0:T(8,128)(2,1)S(1)}, bf16[256,512]{1,0:T(8,128)(2,1)S(1)}, u32[]{:S(2)}, u32[]{:S(2)}) collective-permute-start(bf16[256,512]{1,0:T(8,128)(2,1)S(1)} %get-tuple-element.146.refs_1_), channel_id=1, source_target_pairs={{0,16},{8,24},{16,0},{24,8},{32,48},{40,56},{48,32},{56,40},{64,80... | collective-permute-start | bytes 786440 | tf_op jit(solution)/shard_map/ppermute | solution.py:339
  66.9 6.3 %copy-start.6 = (bf16[8,192,256]{2,1,0:T(8,128)(2,1)S(1)}, bf16[8,192,256]{2,1,0:T(8,128)(2,1)}, u32[]{:S(2)}) copy-start(bf16[8,192,256]{2,1,0:T(8,128)(2,1)} %copy-done.5) | copy-start | bytes 2359300
  67.2 12.4 %collective-permute-start.18 = (bf16[192,512]{1,0:T(8,128)(2,1)S(1)}, bf16[192,512]{1,0:T(8,128)(2,1)S(1)}, u32[]{:S(2)}, u32[]{:S(2)}) collective-permute-start(bf16[192,512]{1,0:T(8,128)(2,1)S(1)} %get-tuple-element.137), channel_id=1, source_target_pairs={{0,32},{8,40},{16,48},{24,56},{32,64},{40,72},{48,80},{56,88},{64,... | collective-permute-start | bytes 589832 | tf_op jit(solution)/shard_map/ppermute | solution.py:342
  69.2 11.6 %collective-permute-start.19 = (bf16[192,512]{1,0:T(8,128)(2,1)S(1)}, bf16[192,512]{1,0:T(8,128)(2,1)S(1)}, u32[]{:S(2)}, u32[]{:S(2)}) collective-permute-start(bf16[192,512]{1,0:T(8,128)(2,1)S(1)} %get-tuple-element.138), channel_id=1, source_target_pairs={{0,224},{8,232},{16,240},{24,248},{32,0},{40,8},{48,16},{56,24},{6... | collective-permute-start | bytes 589832 | tf_op jit(solution)/shard_map/ppermute | solution.py:342
  76.7 2.9 %copy-start.1 = (bf16[2,384,256]{2,1,0:T(8,128)(2,1)S(1)}, bf16[2,384,256]{2,1,0:T(8,128)(2,1)}, u32[]{:S(2)}) copy-start(bf16[2,384,256]{2,1,0:T(8,128)(2,1)} %copy-done) | copy-start | bytes 1179652
  77.0 6.7 %collective-permute-start.32 = (bf16[192,512]{1,0:T(8,128)(2,1)S(1)}, bf16[192,512]{1,0:T(8,128)(2,1)S(1)}, u32[]{:S(2)}, u32[]{:S(2)}) collective-permute-start(bf16[192,512]{1,0:T(8,128)(2,1)S(1)} %get-tuple-element.150), channel_id=1, source_target_pairs={{0,224},{8,232},{16,240},{24,248},{32,0},{40,8},{48,16},{56,24},{6... | collective-permute-start | bytes 589832 | tf_op jit(solution)/shard_map/ppermute | solution.py:342
  79.6 9.1 %collective-permute-start.31 = (bf16[192,512]{1,0:T(8,128)(2,1)S(1)}, bf16[192,512]{1,0:T(8,128)(2,1)S(1)}, u32[]{:S(2)}, u32[]{:S(2)}) collective-permute-start(bf16[192,512]{1,0:T(8,128)(2,1)S(1)} %get-tuple-element.149), channel_id=1, source_target_pairs={{0,32},{8,40},{16,48},{24,56},{32,64},{40,72},{48,80},{56,88},{64,... | collective-permute-start | bytes 589832 | tf_op jit(solution)/shard_map/ppermute | solution.py:342
  79.7 39.5 %collective-permute-start.22 = (bf16[2,384,256]{2,1,0:T(8,128)(2,1)S(1)}, bf16[2,384,256]{2,1,0:T(8,128)(2,1)S(1)}, u32[]{:S(2)}, u32[]{:S(2)}) collective-permute-start(bf16[2,384,256]{2,1,0:T(8,128)(2,1)S(1)} %shard_map.100), channel_id=1, source_target_pairs={{0,3},{1,2},{2,1},{3,0},{4,7},{5,6},{6,5},{7,4},{8,11},{9,10},{10,... | collective-permute-start | bytes 1179656 | tf_op jit(solution)/shard_map/ppermute | solution.py:336
  81.0 11.3 %collective-permute-start.20 = (bf16[192,512]{1,0:T(8,128)(2,1)S(1)}, bf16[192,512]{1,0:T(8,128)(2,1)S(1)}, u32[]{:S(2)}, u32[]{:S(2)}) collective-permute-start(bf16[192,512]{1,0:T(8,128)(2,1)S(1)} %get-tuple-element.139), channel_id=1, source_target_pairs={{0,32},{8,40},{16,48},{24,56},{32,64},{40,72},{48,80},{56,88},{64,... | collective-permute-start | bytes 589832 | tf_op jit(solution)/shard_map/ppermute | solution.py:342
  83.7 10.7 %collective-permute-start.24 = (bf16[192,512]{1,0:T(8,128)(2,1)S(1)}, bf16[192,512]{1,0:T(8,128)(2,1)S(1)}, u32[]{:S(2)}, u32[]{:S(2)}) collective-permute-start(bf16[192,512]{1,0:T(8,128)(2,1)S(1)} %get-tuple-element.141), channel_id=1, source_target_pairs={{0,224},{8,232},{16,240},{24,248},{32,0},{40,8},{48,16},{56,24},{6... | collective-permute-start | bytes 589832 | tf_op jit(solution)/shard_map/ppermute | solution.py:342
  88.7 3.6 %collective-permute-start.39 = (f32[1,256]{1,0:T(1,128)S(1)}, f32[1,256]{1,0:T(1,128)S(1)}, u32[]{:S(2)}, u32[]{:S(2)}) collective-permute-start(f32[1,256]{1,0:T(1,128)S(1)} %shard_map.101), channel_id=1, source_target_pairs={{0,1},{1,0},{2,3},{3,2},{4,5},{5,4},{6,7},{7,6},{8,9},{9,8},{10,11... | collective-permute-start | bytes 3080 | tf_op jit(solution)/shard_map/ppermute | solution.py:336
  92.2 5.7 %collective-permute-start.34 = (bf16[192,512]{1,0:T(8,128)(2,1)S(1)}, bf16[192,512]{1,0:T(8,128)(2,1)S(1)}, u32[]{:S(2)}, u32[]{:S(2)}) collective-permute-start(bf16[192,512]{1,0:T(8,128)(2,1)S(1)} %get-tuple-element.152), channel_id=1, source_target_pairs={{0,224},{8,232},{16,240},{24,248},{32,0},{40,8},{48,16},{56,24},{6... | collective-permute-start | bytes 589832 | tf_op jit(solution)/shard_map/ppermute | solution.py:342
  92.3 8.8 %collective-permute-start.33 = (bf16[192,512]{1,0:T(8,128)(2,1)S(1)}, bf16[192,512]{1,0:T(8,128)(2,1)S(1)}, u32[]{:S(2)}, u32[]{:S(2)}) collective-permute-start(bf16[192,512]{1,0:T(8,128)(2,1)S(1)} %get-tuple-element.151), channel_id=1, source_target_pairs={{0,32},{8,40},{16,48},{24,56},{32,64},{40,72},{48,80},{56,88},{64,... | collective-permute-start | bytes 589832 | tf_op jit(solution)/shard_map/ppermute | solution.py:342
  94.3 27.3 %collective-permute-start.21 = (bf16[2,384,256]{2,1,0:T(8,128)(2,1)S(1)}, bf16[2,384,256]{2,1,0:T(8,128)(2,1)S(1)}, u32[]{:S(2)}, u32[]{:S(2)}) collective-permute-start(bf16[2,384,256]{2,1,0:T(8,128)(2,1)S(1)} %shard_map.99), channel_id=1, source_target_pairs={{0,2},{1,3},{2,0},{3,1},{4,6},{5,7},{6,4},{7,5},{8,10},{9,11},{10,... | collective-permute-start | bytes 1179656 | tf_op jit(solution)/shard_map/ppermute | solution.py:336
  97.9 8.3 %collective-permute-start.25 = (bf16[192,512]{1,0:T(8,128)(2,1)S(1)}, bf16[192,512]{1,0:T(8,128)(2,1)S(1)}, u32[]{:S(2)}, u32[]{:S(2)}) collective-permute-start(bf16[192,512]{1,0:T(8,128)(2,1)S(1)} %get-tuple-element.142), channel_id=1, source_target_pairs={{0,32},{8,40},{16,48},{24,56},{32,64},{40,72},{48,80},{56,88},{64,... | collective-permute-start | bytes 589832 | tf_op jit(solution)/shard_map/ppermute | solution.py:342
  101.0 5.1 %collective-permute-start.40 = (f32[1,256]{1,0:T(1,128)S(1)}, f32[1,256]{1,0:T(1,128)S(1)}, u32[]{:S(2)}, u32[]{:S(2)}) collective-permute-start(f32[1,256]{1,0:T(1,128)S(1)} %shard_map.102), channel_id=1, source_target_pairs={{0,2},{1,3},{2,0},{3,1},{4,6},{5,7},{6,4},{7,5},{8,10},{9,11},{10,... | collective-permute-start | bytes 3080 | tf_op jit(solution)/shard_map/ppermute | solution.py:336
  106.1 16.0 %collective-permute-start.27 = (bf16[192,512]{1,0:T(8,128)(2,1)S(1)}, bf16[192,512]{1,0:T(8,128)(2,1)S(1)}, u32[]{:S(2)}, u32[]{:S(2)}) collective-permute-start(bf16[192,512]{1,0:T(8,128)(2,1)S(1)} %get-tuple-element.143), channel_id=1, source_target_pairs={{0,224},{8,232},{16,240},{24,248},{32,0},{40,8},{48,16},{56,24},{6... | collective-permute-start | bytes 589832 | tf_op jit(solution)/shard_map/ppermute | solution.py:342
  106.2 7.6 %collective-permute-start.36 = (bf16[192,512]{1,0:T(8,128)(2,1)S(1)}, bf16[192,512]{1,0:T(8,128)(2,1)S(1)}, u32[]{:S(2)}, u32[]{:S(2)}) collective-permute-start(bf16[192,512]{1,0:T(8,128)(2,1)S(1)} %get-tuple-element.154), channel_id=1, source_target_pairs={{0,224},{8,232},{16,240},{24,248},{32,0},{40,8},{48,16},{56,24},{6... | collective-permute-start | bytes 589832 | tf_op jit(solution)/shard_map/ppermute | solution.py:342
  113.9 3.6 %collective-permute-start.41 = (f32[1,256]{1,0:T(1,128)S(1)}, f32[1,256]{1,0:T(1,128)S(1)}, u32[]{:S(2)}, u32[]{:S(2)}) collective-permute-start(f32[1,256]{1,0:T(1,128)S(1)} %shard_map.103), channel_id=1, source_target_pairs={{0,4},{1,5},{2,6},{3,7},{4,0},{5,1},{6,2},{7,3},{8,12},{9,13},{10,... | collective-permute-start | bytes 3080 | tf_op jit(solution)/shard_map/ppermute | solution.py:336
  117.5 9.1 %collective-permute-start.35 = (bf16[192,512]{1,0:T(8,128)(2,1)S(1)}, bf16[192,512]{1,0:T(8,128)(2,1)S(1)}, u32[]{:S(2)}, u32[]{:S(2)}) collective-permute-start(bf16[192,512]{1,0:T(8,128)(2,1)S(1)} %get-tuple-element.153), channel_id=1, source_target_pairs={{0,32},{8,40},{16,48},{24,56},{32,64},{40,72},{48,80},{56,88},{64,... | collective-permute-start | bytes 589832 | tf_op jit(solution)/shard_map/ppermute | solution.py:342
  118.3 8.3 %collective-permute-start.26 = (bf16[192,512]{1,0:T(8,128)(2,1)S(1)}, bf16[192,512]{1,0:T(8,128)(2,1)S(1)}, u32[]{:S(2)}, u32[]{:S(2)}) collective-permute-start(bf16[192,512]{1,0:T(8,128)(2,1)S(1)} %fusion.15), channel_id=1, source_target_pairs={{0,32},{8,40},{16,48},{24,56},{32,64},{40,72},{48,80},{56,88},{64,... | collective-permute-start | bytes 589832 | tf_op jit(solution)/shard_map/ppermute | solution.py:342
  119.2 7.4 %collective-permute-start.37 = (bf16[192,512]{1,0:T(8,128)(2,1)S(1)}, bf16[192,512]{1,0:T(8,128)(2,1)S(1)}, u32[]{:S(2)}, u32[]{:S(2)}) collective-permute-start(bf16[192,512]{1,0:T(8,128)(2,1)S(1)} %fusion.6), channel_id=1, source_target_pairs={{0,224},{8,232},{16,240},{24,248},{32,0},{40,8},{48,16},{56,24},{6... | collective-permute-start | bytes 589832 | tf_op jit(solution)/shard_map/ppermute | solution.py:342
  121.8 5.8 %collective-permute-start.23 = (bf16[384,256]{1,0:T(8,128)(2,1)S(1)}, bf16[384,256]{1,0:T(8,128)(2,1)S(1)}, u32[]{:S(2)}, u32[]{:S(2)}) collective-permute-start(bf16[384,256]{1,0:T(8,128)(2,1)S(1)} %fusion.23), channel_id=1, source_target_pairs={{0,4},{1,5},{2,6},{3,7},{4,0},{5,1},{6,2},{7,3},{8,12},{9,13},{10,... | collective-permute-start | bytes 589832 | tf_op jit(solution)/shard_map/ppermute | solution.py:336
  126.7 1.9 %collective-permute-start.38 = (bf16[96,1024]{1,0:T(8,128)(2,1)S(1)}, bf16[96,1024]{1,0:T(8,128)(2,1)S(1)}, u32[]{:S(2)}, u32[]{:S(2)}) collective-permute-start(bf16[96,1024]{1,0:T(8,128)(2,1)S(1)} %fusion.25), channel_id=1, source_target_pairs={{0,8},{8,0},{16,24},{24,16},{32,40},{40,32},{48,56},{56,48},{64,72... | collective-permute-start | bytes 589832 | tf_op jit(solution)/shard_map/ppermute | solution.py:339
  (2 other events, 1.4 us)
where the time goes:
time: 130 us; the launch traced here: 129 us
  starting transfers between devices  50.6 us (39%)
  waiting for transfers between devices  38.1 us (29%)
  Pallas kernels  21.2 us (16%)
  matrix products  10.4 us (8%)
  other arithmetic  5.56 us (4%)
  local copies, waits for them, and re-layouts  2.57 us (2%)
    ppermute x18, starting transfers between devices, over_tensor(): return lax.ppermute(x, 'tensor', [(i, i ^ k) for i in range(n_tensor)])  22.9 us
    ppermute x14, waiting for transfers between devices, along_z(): return lax.ppermute(x, 'dp', [(i, (i + 4 * k) % n_dp) for i in range(n_dp)])  20.1 us
    ppermute x14, starting transfers between devices, along_z(): return lax.ppermute(x, 'dp', [(i, (i + 4 * k) % n_dp) for i in range(n_dp)])  18.4 us
    ppermute x18, waiting for transfers between devices, over_tensor(): return lax.ppermute(x, 'tensor', [(i, i ^ k) for i in range(n_tensor)])  13.8 us
    ppermute x10, starting transfers between devices, over_dp(): return lax.ppermute(x, 'dp', [(i, i ^ k) for i in range(n_dp)])  9.3 us
    dot_general x8, matrix products, product(): return jnp.dot(a.reshape(n_z * half, CAP), b, preferred_element_type=F32)  9.08 us
    pallas_call x1, Pallas kernels, token_parts(): pl.pallas_call(back_kernel, grid_spec=pltpu.PrefetchScalarGridSpec(num_sc...  6.84 us
    pallas_call x1, Pallas kernels, early(): pl.pallas_call(lambda *a: early_kernel(n, *a), grid_spec=pltpu.PrefetchSc...  5.53 us
  transfers between devices with their start and end apart: 42, of which 15 were waited for; matrix products, arithmetic and copies ran while one was open for 11% of the time, Pallas kernels for 11%

commit v1 on v0

--- a/solution.py
+++ b/solution.py
@@ -7,6 +7,7 @@
 
 CAP = 256
 CHUNKS = 2
+EXTRA = 16
 BF = jnp.bfloat16
 F32 = jnp.float32
 MIB = 2**20
@@ -142,7 +143,7 @@
         out_shape=[jax.ShapeDtypeStruct((cap, width), F32)] * 2
         + [jax.ShapeDtypeStruct((n, piece // 2, cap), BF)]
         + [pltpu.VMEM((2 * n * piece, width), BF)] * 2,
-        compiler_params=pltpu.CompilerParams(vmem_limit_bytes=28 * MIB),
+        compiler_params=pltpu.CompilerParams(vmem_limit_bytes=14 * MIB),
         cost_estimate=pl.CostEstimate(
             flops=4 * cap * n * piece * width,
             bytes_accessed=8 * n * piece * width,
@@ -155,7 +156,7 @@
     pieces = refs[:n]
     wg, wu, gate_in, up_in, near_in, cot, share = refs[n : n + 7]
     mine, other = refs[n + 7 : n + 7 + CHUNKS], refs[n + 7 + CHUNKS : n + 7 + 2 * CHUNKS]
-    near_left, route_out, held, turned = refs[n + 7 + 2 * CHUNKS :]
+    near_left, route_out, held, turned, route = refs[n + 7 + 2 * CHUNKS :]
     step = pl.program_id(0)
     piece, cap = turned.shape
     half, block = near_left.shape[1], cot.shape[1]
@@ -163,7 +164,7 @@
 
     @pl.when(step == 0)
     def _():
-        route_out[...] = jnp.zeros_like(route_out)
+        route[...] = jnp.zeros_like(route)
         for i in range(n):
             held[:, i * piece : (i + 1) * piece] = pieces[i][...]
 
@@ -174,7 +175,7 @@
     activated = gate * sig
     hidden = (activated * up).astype(BF).astype(F32)
     cot_wide = cot[...].astype(F32)
-    route_out[...] += jnp.sum(hidden * cot_wide, axis=1, keepdims=True)
+    route[...] += jnp.sum(hidden * cot_wide, axis=1, keepdims=True)
     scaled = share[...] * cot_wide
     gate_cot = scaled * up * sig * (1.0 + gate * (1.0 - sig))
     up_cot = scaled * activated
@@ -190,6 +191,7 @@
 
     @pl.when(step == CHUNKS - 1)
     def _():
+        route_out[...] = jnp.broadcast_to(route[...], (cap, 128)).T[:1, :]
         for i, k in enumerate(soon):
             near_left[at(k)] = near_in[i]
         for i, k in enumerate(late):
@@ -205,7 +207,7 @@
     block = width // CHUNKS
     cols = pl.BlockSpec((cap, block), lambda j, *_: (0, j))
     near_left = (n_z, piece // 2, cap)
-    outs = [((cap, block), BF)] * (2 * CHUNKS) + [(near_left, BF), ((cap, 1), F32)]
+    outs = [((cap, block), BF)] * (2 * CHUNKS) + [(near_left, BF), ((1, cap), F32)]
     held = pl.BlockSpec(memory_space=pltpu.VMEM)
     return pl.pallas_call(
         lambda *a: forward_kernel(n, soon, late, n_z, *a),
@@ -215,10 +217,14 @@
             in_specs=[whole((cap, piece))] * n
             + [held, held, cols, cols, whole(near.shape), cols, whole((cap, 1))],
             out_specs=[whole(shape) for shape, _ in outs],
-            scratch_shapes=[pltpu.VMEM((cap, n * piece), BF), pltpu.VMEM((piece, cap), BF)],
+            scratch_shapes=[
+                pltpu.VMEM((cap, n * piece), BF),
+                pltpu.VMEM((piece, cap), BF),
+                pltpu.VMEM((cap, 1), F32),
+            ],
         ),
         out_shape=[jax.ShapeDtypeStruct(shape, kind) for shape, kind in outs],
-        compiler_params=pltpu.CompilerParams(vmem_limit_bytes=24 * MIB),
+        compiler_params=pltpu.CompilerParams(vmem_limit_bytes=20 * MIB),
         cost_estimate=pl.CostEstimate(
             flops=4 * cap * n * piece * width,
             bytes_accessed=16 * cap * width,
@@ -227,9 +233,22 @@
     )(info, *pieces, w_gate, w_up, gate, up, near, cot_rows, share)
 
 
+def in_terms(row):
+    high = row.astype(BF).astype(F32)
+    middle = (row - high).astype(BF).astype(F32)
+    low = row - high - middle
+    at = lax.broadcasted_iota(jnp.int32, (EXTRA, row.shape[1]), 0)
+    terms = jnp.where(at == 0, high, jnp.where(at == 1, middle, jnp.where(at == 2, low, 0.0)))
+    return terms.astype(BF)
+
+
+def row_of(terms):
+    return jnp.sum(terms.astype(F32), axis=0, keepdims=True)
+
+
 def back_kernel(info, *refs):
     mine, other = refs[:CHUNKS], refs[CHUNKS : 2 * CHUNKS]
-    wg, wu, own, first_out, third_out, second_out, gt, ut = refs[2 * CHUNKS :]
+    route, _, wg, wu, own, first_out, third_out, second_out, gt, ut = refs[2 * CHUNKS :]
     piece = own.shape[1]
     chunk = mine[0].shape[1]
     first = info[3] == 0
@@ -249,33 +268,38 @@
 
             @pl.when(i == j)
             def _(ref=ref, at=at):
-                ref[at] = out.astype(ref.dtype)
+                ref[at, :piece, :] = out.astype(ref.dtype)
 
         return 0
 
     lax.fori_loop(0, len(targets), block, 0)
-
-
-def token_parts(info, mine, other, weights, piece):
+    terms = in_terms(route[...])
+    for ref in (first_out, third_out, second_out):
+        for at in range(2):
+            ref[at, piece:, :] = terms
+
+
+def token_parts(info, mine, other, route, waited, weights, piece):
     cap, chunk = mine[0].shape
     depth, width = weights[0].shape
-    pair = (2, piece, cap)
+    pair, message = (2, piece, cap), (2, piece + EXTRA, cap)
     return pl.pallas_call(
         back_kernel,
         grid_spec=pltpu.PrefetchScalarGridSpec(
             num_scalar_prefetch=1,
             grid=(1,),
             in_specs=[whole((cap, chunk))] * (2 * CHUNKS)
+            + [whole((1, cap)), pl.BlockSpec(memory_space=pl.ANY)]
             + [pl.BlockSpec(memory_space=pltpu.VMEM)] * 2,
-            out_specs=[whole(pair)] * 4,
+            out_specs=[whole(pair)] + [whole(message)] * 3,
             scratch_shapes=[pltpu.VMEM((width, cap), BF), pltpu.VMEM((width, cap), BF)],
         ),
-        out_shape=[jax.ShapeDtypeStruct(pair, F32)] + [jax.ShapeDtypeStruct(pair, BF)] * 3,
-        compiler_params=pltpu.CompilerParams(vmem_limit_bytes=16 * MIB),
+        out_shape=[jax.ShapeDtypeStruct(pair, F32)] + [jax.ShapeDtypeStruct(message, BF)] * 3,
+        compiler_params=pltpu.CompilerParams(vmem_limit_bytes=14 * MIB),
         cost_estimate=pl.CostEstimate(
             flops=4 * cap * depth * width, bytes_accessed=4 * depth * width, transcendentals=0
         ),
-    )(info, *mine, *other, *weights)
+    )(info, *mine, *other, route, waited, *weights)
 
 
 def after(x, waited):
@@ -290,6 +314,67 @@
         out_shape=jax.ShapeDtypeStruct(x.shape, x.dtype),
         compiler_params=pltpu.CompilerParams(vmem_limit_bytes=4 * MIB),
     )(x, waited)
+
+
+def combine_kernel(own, route, first, third, second, kept, kept_route, sent):
+    piece = own.shape[1]
+    rows = [row_of(ref[0, piece:, :]) for ref in (first, third, second)]
+    kept_route[...] = (route[...] + rows[0]) + (rows[1] + rows[2])
+    for at in range(2):
+        total = own[at]
+        for ref in (first, third, second):
+            total += ref[at, :piece, :].astype(F32)
+        if at == 0:
+            kept[...] = total
+        else:
+            sent[:piece, :] = total.astype(BF)
+    sent[piece:, :] = in_terms(kept_route[...])
+
+
+def combine(own, route, parts):
+    _, piece, cap = own.shape
+    shapes = [((piece, cap), F32), ((1, cap), F32), ((piece + EXTRA, cap), BF)]
+    return pl.pallas_call(
+        combine_kernel,
+        out_shape=[jax.ShapeDtypeStruct(shape, kind) for shape, kind in shapes],
+        compiler_params=pltpu.CompilerParams(vmem_limit_bytes=6 * MIB),
+        cost_estimate=pl.CostEstimate(
+            flops=8 * piece * cap, bytes_accessed=30 * piece * cap, transcendentals=0
+        ),
+    )(own, route, *parts)
+
+
+def hop_kernel(has, n_waits, *refs):
+    n = len(has)
+    parts, refs = refs[:n], refs[n:]
+    got, outs = refs[: sum(has)], refs[sum(has) + n_waits :]
+    taken = 0
+    for i in range(n):
+        total = parts[i][0]
+        if has[i]:
+            total += got[taken][...].astype(F32)
+            taken += 1
+        outs[i][...] = total.astype(BF)
+
+
+def hop_sums(base, places, arrived, waited):
+    _, rows, cols = base.shape
+    got = [a for a in arrived if a is not None]
+    n = len(places)
+    block = lambda j: pl.BlockSpec((1, rows, cols), lambda i: (j, 0, 0))
+    return pl.pallas_call(
+        lambda *a: hop_kernel([x is not None for x in arrived], len(waited), *a),
+        grid=(1,),
+        in_specs=[block(j) for j in places]
+        + [whole((rows, cols))] * len(got)
+        + [pl.BlockSpec(memory_space=pl.ANY)] * len(waited),
+        out_specs=[whole((rows, cols))] * n,
+        out_shape=[jax.ShapeDtypeStruct((rows, cols), BF)] * n,
+        compiler_params=pltpu.CompilerParams(vmem_limit_bytes=6 * MIB),
+        cost_estimate=pl.CostEstimate(
+            flops=2 * n * rows * cols, bytes_accessed=8 * n * rows * cols, transcendentals=0
+        ),
+    )(*[base] * n, *got, *waited)
 
 
 def far_kernel(n, n_z, info, *refs):
@@ -373,9 +458,9 @@
     soon, late = (0, xlo, 1, 3), (xlo + 1, xlo + 3, 2, xlo + 2)
     order = jnp.stack([t ^ k for k in soon + late] + [xh]).astype(jnp.int32)
     gate, up, near_soon, *weights = early(order, [near[k] for k in soon], w_gate, w_up)
-    far_piece, near[late[0]] = tie((far_piece, near[late[0]]))
+    far_piece, near[late[3]] = tie((far_piece, near[late[3]]))
     far_pair = jnp.stack([far_piece, over_tensor(far_piece, xlo)])
-    late_near, far_pair, gate, up = tie(([near[k] for k in late], far_pair, gate, up))
+    late_near, gate, up = tie(([near[k] for k in late], gate, up))
     outs = forward(
         info, late_near, soon, late, *weights, gate, up, near_soon, cot_rows, share, n_z
     )
@@ -386,87 +471,83 @@
         return [mine[c], over_dp(other[c], 1), over_dp(mine[c], 2), over_dp(other[c], 3)]
 
     cots = [to_partners(0)]
-    far_pair, near_left, mine, other, route_part, cots[0][1] = tie(
-        (far_pair, near_left, mine, other, route_part, cots[0][1])
-    )
     near_sib = over_dp(near_left, 1)
     far = [far_pair] + [over_tensor(far_pair, k) for k in (1, 3)]
     far_pair, near_sib = tie((far_pair, near_sib))
     far.insert(2, over_tensor(far_pair, 2))
-    own_part, *sent = token_parts(info, mine, other, weights, piece)
-    far, own_part, sent, mine, other = tie((far, own_part, sent, mine, other))
+    own_part, *sent = token_parts(info, mine, other, route_part, far_pair, weights, piece)
+
+    def product(a, b):
+        return jnp.dot(a.reshape(n_z * half, CAP), b, preferred_element_type=F32)
+
+    close = product(near_left, cots[0][0]) + product(near_sib, cots[0][1])
+    far, own_part, sent, mine, other, close = tie((far, own_part, sent, mine, other, close))
     far_left = far_operand(info, far, n_tensor, n_z)
     far_sib = over_dp(far_left, 1)
     for c in range(1, CHUNKS):
         mine, other, cots[-1] = tie((mine, other, cots[-1]))
         cots.append(to_partners(c))
-    sums = {1: over_tensor(sent[0], 1)}
-
-    def product(a, b):
-        return jnp.dot(a.reshape(n_z * half, CAP), b, preferred_element_type=F32)
+    step = width // CHUNKS
+
+    def sums_of(c, close):
+        base = tie(close) + product(far_left, cots[c][2])
+        base = tie(base + product(far_sib, cots[c][3]))
+        return base.reshape(n_z, half, step)
 
     class Ring:
-        def __init__(self, c):
-            base = product(lefts[0], cots[c][0]) + product(lefts[1], cots[c][1])
-            base = tie(base) + product(far_left, cots[c][2])
-            base = tie(base + product(far_sib, cots[c][3]))
-            self.base = base.reshape(n_z, half, width // CHUNKS)
+        def __init__(self, c, base):
+            self.base = base
             self.up_hops = n_z // 2 - c % 2
             self.down_hops = n_z - 1 - self.up_hops
             self.rising = self.falling = None
 
-        def part(self, j):
-            return self.base[j]
-
-        def hop(self, i):
-            up, down = i < self.up_hops, i < self.down_hops
-            if up:
-                out = self.part(self.up_hops - i)
-                rising = (out if i == 0 else out + self.rising.astype(F32)).astype(BF)
-            if down:
-                out = self.part((n_z - self.down_hops + i) % n_z)
-                falling = (out if i == 0 else out + self.falling.astype(F32)).astype(BF)
-            if up and down:
-                rising, falling = tie((rising, falling))
-            if up:
-                self.rising = along_z(rising, 1)
-            if down:
-                self.falling = along_z(falling, -1)
+        def hop(self, i, waited):
+            places, arrived = [], []
+            if i < self.up_hops:
+                places.append(self.up_hops - i)
+                arrived.append(self.rising)
+            if i < self.down_hops:
+                places.append((n_z - self.down_hops + i) % n_z)
+                arrived.append(self.falling)
+            out = hop_sums(self.base, places, arrived, waited)
+            if i < self.up_hops:
+                self.rising = along_z(out[0], 1)
+            if i < self.down_hops:
+                self.falling = along_z(out[-1], -1)
+            return out[0]
 
         def finish(self):
-            total = self.part(0) + self.rising.astype(F32) + self.falling.astype(F32)
-            total = total.astype(BF).reshape(2, half // 2, width // CHUNKS)
-            return total
-
-    lefts = [near_left, near_sib]
-    rings = []
-    for c in range(CHUNKS):
-        rings.append(Ring(c))
-        lefts, rings[c].base = tie((lefts, rings[c].base))
-    route_part = route_part.reshape(1, CAP)
-    for i in range(n_z // 2):
-        for ring in rings:
-            ring.hop(i)
-        waited = rings[0].rising
-        if i < 2:
-            sums[3 - i] = over_tensor(after(sent[1 + i], waited), 3 - i)
+            total = self.base[0] + self.rising.astype(F32) + self.falling.astype(F32)
+            return total.astype(BF).reshape(2, half // 2, step)
+
+    rings = [Ring(0, sums_of(0, close))]
+    waited = rings[0].hop(0, [])
+    sums = {1: over_tensor(after(sent[0], waited), 1)}
+    for c in range(1, CHUNKS):
+        lefts = [after(near_left, waited), near_sib]
+        close = product(lefts[0], cots[c][0]) + product(lefts[1], cots[c][1])
+        rings.append(Ring(c, sums_of(c, close)))
+        waited = rings[c].hop(0, [waited])
+    for i in range(1, n_z // 2):
+        waited = rings[0].hop(i, [waited])
         if i < 3:
-            route_part = after(route_part, waited)
-            route_part = route_part + over_tensor(route_part, 1 << i)
+            sums[4 - i] = over_tensor(after(sent[i], waited), 4 - i)
+        for ring in rings[1:]:
+            waited = ring.hop(i, [waited, sums[(1, 3, 2)[i - 1]]])
     whole_rows = jnp.concatenate([ring.finish() for ring in rings], axis=2)
     kept = lax.dynamic_index_in_dim(whole_rows, core, 0, keepdims=False)
     swapped = over_dp(lax.dynamic_index_in_dim(whole_rows, 1 - core, 0, keepdims=False), 1)
     gate_grad = jnp.where(core == 0, kept, swapped)
     up_grad = jnp.where(core == 0, swapped, kept)
 
-    total = own_part
-    for k in (1, 2, 3):
-        total = total + sums[k].astype(F32)
-    total = total[0] + over_tensor(total[1].astype(BF), xlo).astype(F32)
+    total, route_total, message = combine(own_part, route_part, [sums[1], sums[3], sums[2]])
+    message = over_tensor(message, xlo)
+    total = total + message[:piece].astype(F32)
+    route_total = route_total + row_of(message[piece:])
     token_grad = lax.dot_general(
         dispatch, total.astype(BF), (((0,), (1,)), ((), ())), preferred_element_type=F32
     ).astype(BF)
-    route_grad = jnp.sum(jnp.where(mask, route_part[0][:, None], 0.0), axis=0)
+    route_grad = jnp.sum(jnp.where(mask, route_total[0][:, None], 0.0), axis=0)
     return token_grad, gate_grad, up_grad, route_grad
 
 

time: 130 us -> 126 us (0.969)
  waiting for transfers between devices: 38.1 us -> 33.3 us
  matrix products: 10.4 us -> 5.8 us
  starting transfers between devices: 50.6 us -> 54.8 us
  Pallas kernels: 21.2 us -> 25.1 us
  local copies, waits for them, and re-layouts: 2.57 us -> 1.01 us
    ppermute x14, starting transfers between devices: 18.4 us -> 26.4 us  [along_z(): return lax.ppermute(x, 'dp', [(i, (i + 4 * k) % n_dp) for i in range(n_dp)])]
    ppermute x14, waiting for transfers between devices: 20.1 us -> 14.2 us  [along_z(): return lax.ppermute(x, 'dp', [(i, (i + 4 * k) % n_dp) for i in range(n_dp)])]
    pallas_call x0 -> x9, Pallas kernels: none -> 4.66 us  [the longest x8 3.39 us: hop_sums(): pl.pallas_call(lambda *a: hop_kernel([x is not None for x in arrived], le...]
    dot_general x8, matrix products: 9.08 us -> 4.53 us  [product(): return jnp.dot(a.reshape(n_z * half, CAP), b, preferred_element_type=F32)]
    ppermute x18 -> x15, starting transfers between devices: 22.9 us -> 18.7 us  [over_tensor(): return lax.ppermute(x, 'tensor', [(i, i ^ k) for i in range(n_tensor)])]
    ppermute x18 -> x15, waiting for transfers between devices: 13.8 us -> 16 us  [over_tensor(): return lax.ppermute(x, 'tensor', [(i, i ^ k) for i in range(n_tensor)])]
    unnamed x16 -> x20, local copies, waits for them, and re-layouts: 2.39 us -> 0.92 us
  transfers between devices with their start and end apart: 42 -> 39, of which waited for: 15 -> 13; matrix products, arithmetic and copies ran while one was open for 11% -> 7% of each run, Pallas kernels for 11% -> 15%
where the time goes in v1:
time: 126 us
  starting transfers between devices  54.8 us (43%)
  waiting for transfers between devices  33.3 us (26%)
  Pallas kernels  25.1 us (20%)
  matrix products  5.8 us (5%)
  other arithmetic  4.45 us (4%)
    ppermute x14, starting transfers between devices, along_z(): return lax.ppermute(x, 'dp', [(i, (i + 4 * k) % n_dp) for i in range(n_dp)])  26.4 us
    ppermute x15, starting transfers between devices, over_tensor(): return lax.ppermute(x, 'tensor', [(i, i ^ k) for i in range(n_tensor)])  18.7 us
    ppermute x15, waiting for transfers between devices, over_tensor(): return lax.ppermute(x, 'tensor', [(i, i ^ k) for i in range(n_tensor)])  16 us
    ppermute x14, waiting for transfers between devices, along_z(): return lax.ppermute(x, 'dp', [(i, (i + 4 * k) % n_dp) for i in range(n_dp)])  14.2 us
    ppermute x10, starting transfers between devices, over_dp(): return lax.ppermute(x, 'dp', [(i, i ^ k) for i in range(n_dp)])  9.71 us
    pallas_call x1, Pallas kernels, token_parts(): pl.pallas_call(back_kernel, grid_spec=pltpu.PrefetchScalarGridSpec(num_sc...  5.93 us
    pallas_call x1, Pallas kernels, early(): pl.pallas_call(lambda *a: early_kernel(n, *a), grid_spec=pltpu.PrefetchSc...  5.46 us
    dot_general x8, matrix products, product(): return jnp.dot(a.reshape(n_z * half, CAP), b, preferred_element_type=F32)  4.53 us
  transfers between devices with their start and end apart: 39, of which 13 were waited for; matrix products, arithmetic and copies ran while one was open for 7% of the time, Pallas kernels for 15%

profile of v1, /device:TPU:2, one launch (start us, length us, event | category | flops | bytes accessed | tf_op | source)
XLA Modules:
  0.0 125.5 jit_solution(16912114670060306682)
XLA Ops:
  1.7 1.9 %shard_map.93 = (bf16[256,384]{1,0:T(8,128)(2,1)S(1)}, bf16[192,256]{1,0:T(8,128)(2,1)S(1)}) custom-call(s32[4]{0:T(128)S(1)} %pad_add_fusion.info.a_0_, s32[1,512]{1,0:T(1,128)S(1)} %bitcast.70, bf16[512,384]{1,0:T(8,128)(2,1)} %tokens.1), custom_call_target="tpu_custom_call" | custom-call | flops 100663296 | bytes 786432 | tf_op jit(solution)/shard_map/pallas_call | solution.py:34
  3.6 1.7 %collective-permute-start.1 = (bf16[256,384]{1,0:T(8,128)(2,1)S(1)}, bf16[256,384]{1,0:T(8,128)(2,1)S(1)}, u32[]{:S(2)}, u32[]{:S(2)}) collective-permute-start(bf16[256,384]{1,0:T(8,128)(2,1)S(1)} %get-tuple-element.77.a_1_), channel_id=1, source_target_pairs={{0,1},{1,0},{2,3},{3,2},{4,5},{5,4},{6,7},{7,6},{8,9},{9,8},{10,11... | collective-permute-start | bytes 589832 | tf_op jit(solution)/shard_map/ppermute | solution.py:421
  5.3 2.2 %collective-permute-start.2 = (bf16[256,384]{1,0:T(8,128)(2,1)S(1)}, bf16[256,384]{1,0:T(8,128)(2,1)S(1)}, u32[]{:S(2)}, u32[]{:S(2)}) collective-permute-start(bf16[256,384]{1,0:T(8,128)(2,1)S(1)} %get-tuple-element.77.a_1_), channel_id=1, source_target_pairs={{0,3},{1,2},{2,1},{3,0},{4,7},{5,6},{6,5},{7,4},{8,11},{9,10},{10,... | collective-permute-start | bytes 589832 | tf_op jit(solution)/shard_map/ppermute | solution.py:421
  8.7 1.7 %shard_map.94 = (bf16[256,1024]{1,0:T(8,128)(2,1)S(1)}, f32[256,1]{1,0:T(8,128)S(1)}) custom-call(s32[1,512]{1,0:T(1,128)S(1)} %bitcast.71, f32[1,512]{1,0:T(1,128)S(1)} %bitcast.72, bf16[512,1024]{1,0:T(8,128)(2,1)} %cot.1), custom_call_target="tpu_custom_call" | custom-call | flops 268435456 | bytes 2097152 | tf_op jit(solution)/shard_map/pallas_call | solution.py:64
  10.4 2.4 %collective-permute-done.2.a_4_ = bf16[256,384]{1,0:T(8,128)(2,1)S(1)} collective-permute-done((bf16[256,384]{1,0:T(8,128)(2,1)S(1)}, bf16[256,384]{1,0:T(8,128)(2,1)S(1)}, u32[]{:S(2)}, u32[]{:S(2)}) %collective-permute-start.2) | collective-permute-done | bytes 196640 | tf_op jit(solution)/shard_map/ppermute | solution.py:421
  13.5 1.0 collective-permute-start.4
  14.5 1.2 collective-permute-start.7
  15.7 0.8 collective-permute-start.8
  16.5 2.5 %collective-permute-start.9 = (bf16[256,384]{1,0:T(8,128)(2,1)S(1)}, bf16[256,384]{1,0:T(8,128)(2,1)S(1)}, u32[]{:S(2)}, u32[]{:S(2)}) collective-permute-start(bf16[256,384]{1,0:T(8,128)(2,1)S(1)} %get-tuple-element.77.a_1_), channel_id=1, source_target_pairs={{0,2},{1,3},{2,0},{3,1},{4,6},{5,7},{6,4},{7,5},{8,10},{9,11},{10,... | collective-permute-start | bytes 589832 | tf_op jit(solution)/shard_map/ppermute | solution.py:421
  19.1 2.1 %collective-permute-start = (bf16[192,256]{1,0:T(8,128)(2,1)S(1)}, bf16[192,256]{1,0:T(8,128)(2,1)S(1)}, u32[]{:S(2)}, u32[]{:S(2)}) collective-permute-start(bf16[192,256]{1,0:T(8,128)(2,1)S(1)} %get-tuple-element.69), channel_id=1, source_target_pairs={{0,16},{8,24},{16,0},{24,8},{32,48},{40,56},{48,32},{56,40},{64,80... | collective-permute-start | bytes 294920 | tf_op jit(solution)/shard_map/ppermute | solution.py:424
  21.3 5.5 %shard_map.95 = (f32[256,1024]{1,0:T(8,128)S(1)}, f32[256,1024]{1,0:T(8,128)S(1)}, bf16[4,192,256]{2,1,0:T(8,128)(2,1)S(1)}, bf16[3072,1024]{1,0:T(8,128)(2,1)S(1)}, bf16[3072,1024]{1,0:T(8,128)(2,1)S(1)}) custom-call(s32[9]{0:T(128)S(1)} %stack.65.a_0_, bf16[256,384]{1,0:T(8,128)(2,1)S(1)} %get-tuple-element.77.a_1_, ...), custom_call_target="tpu_custom_call" | custom-call | flops 1610612736 | bytes 12582912 | tf_op jit(solution)/shard_map/pallas_call | solution.py:128
  27.0 3.9 %shard_map.96 = (bf16[256,512]{1,0:T(8,128)(2,1)S(1)}, bf16[256,512]{1,0:T(8,128)(2,1)S(1)}, bf16[256,512]{1,0:T(8,128)(2,1)S(1)}, bf16[256,512]{1,0:T(8,128)(2,...) custom-call(s32[4]{0:T(128)S(1)} %pad_add_fusion.info.a_0_, ...), custom_call_target="tpu_custom_call" | custom-call | flops 1610612736 | bytes 4194304 | tf_op jit(solution)/shard_map/pallas_call | solution.py:212
  31.5 1.0 collective-permute-start.15
  32.5 1.4 %collective-permute-start.5 = (bf16[192,256]{1,0:T(8,128)(2,1)S(1)}, bf16[192,256]{1,0:T(8,128)(2,1)S(1)}, u32[]{:S(2)}, u32[]{:S(2)}) collective-permute-start(bf16[192,256]{1,0:T(8,128)(2,1)S(1)} %collective-permute-done), channel_id=1, source_target_pairs={{0,4},{1,5},{2,6},{3,7},{4,0},{5,1},{6,2},{7,3},{8,12},{9,13},{10,... | collective-permute-start | bytes 294920 | tf_op jit(solution)/shard_map/ppermute | solution.py:421
  33.8 2.1 %collective-permute-start.14 = (bf16[256,512]{1,0:T(8,128)(2,1)S(1)}, bf16[256,512]{1,0:T(8,128)(2,1)S(1)}, u32[]{:S(2)}, u32[]{:S(2)}) collective-permute-start(bf16[256,512]{1,0:T(8,128)(2,1)S(1)} %get-tuple-element.94.refs_0_), channel_id=1, source_target_pairs={{0,16},{8,24},{16,0},{24,8},{32,48},{40,56},{48,32},{56,40},{64,80... | collective-permute-start | bytes 786440 | tf_op jit(solution)/shard_map/ppermute | solution.py:424
  36.5 6.6 %collective-permute-done.5 = bf16[192,256]{1,0:T(8,128)(2,1)S(1)} collective-permute-done((bf16[192,256]{1,0:T(8,128)(2,1)S(1)}, bf16[192,256]{1,0:T(8,128)(2,1)S(1)}, u32[]{:S(2)}, u32[]{:S(2)}) %collective-permute-start.5) | collective-permute-done | bytes 98336 | tf_op jit(solution)/shard_map/ppermute | solution.py:421
  43.1 1.4 %collective-permute-start.6 = (bf16[2,192,256]{2,1,0:T(8,128)(2,1)S(1)}, bf16[2,192,256]{2,1,0:T(8,128)(2,1)S(1)}, u32[]{:S(2)}, u32[]{:S(2)}) collective-permute-start(bf16[2,192,256]{2,1,0:T(8,128)(2,1)S(1)} %pad_maximum_fusion.refs_5_.a_1_), channel_id=1, source_target_pairs={{0,1},{1,0},{2,3},{3,2},{4,5},{5,4},{6,7},{7,6},{8,9},{9,8},{10,11... | collective-permute-start | bytes 589832 | tf_op jit(solution)/shard_map/ppermute | solution.py:421
  44.5 1.5 %collective-permute-start.12 = (bf16[2,192,256]{2,1,0:T(8,128)(2,1)S(1)}, bf16[2,192,256]{2,1,0:T(8,128)(2,1)S(1)}, u32[]{:S(2)}, u32[]{:S(2)}) collective-permute-start(bf16[2,192,256]{2,1,0:T(8,128)(2,1)S(1)} %pad_maximum_fusion.refs_5_.a_1_), channel_id=1, source_target_pairs={{0,3},{1,2},{2,1},{3,0},{4,7},{5,6},{6,5},{7,4},{8,11},{9,10},{10,... | collective-permute-start | bytes 589832 | tf_op jit(solution)/shard_map/ppermute | solution.py:421
  46.0 1.3 %collective-permute-start.11 = (bf16[2,192,256]{2,1,0:T(8,128)(2,1)S(1)}, bf16[2,192,256]{2,1,0:T(8,128)(2,1)S(1)}, u32[]{:S(2)}, u32[]{:S(2)}) collective-permute-start(bf16[2,192,256]{2,1,0:T(8,128)(2,1)S(1)} %pad_maximum_fusion.refs_5_.a_1_), channel_id=1, source_target_pairs={{0,2},{1,3},{2,0},{3,1},{4,6},{5,7},{6,4},{7,5},{8,10},{9,11},{10,... | collective-permute-start | bytes 589832 | tf_op jit(solution)/shard_map/ppermute | solution.py:421
  47.9 5.9 %shard_map.97 = (f32[2,384,256]{2,1,0:T(8,128)S(1)}, bf16[2,400,256]{2,1,0:T(8,128)(2,1)S(1)}, bf16[2,400,256]{2,1,0:T(8,128)(2,1)S(1)}, bf16[2,400,256]{2,1,0:T(8,128)(2,1)S(1)}) custom-call(s32[4]{0:T(128)S(1)} %pad_add_fusion.info.a_0_, bf16[256,512]{1,0:T(8,128)(2,1)S(1)} %get-tuple-element.94.refs_0_, bf16[256,512]{1,0:T(8,128)(2,1)S(1)} %get-tuple-element.118.refs_1_, ...), custom_call_target="tpu_custom_call" | custom-call | flops 3221225472 | bytes 12582912 | tf_op jit(solution)/shard_map/pallas_call | solution.py:286
  53.8 0.9 copy-done.3
  54.7 1.4 %collective-permute-done.12.a_4_ = bf16[2,192,256]{2,1,0:T(8,128)(2,1)S(1)} collective-permute-done((bf16[2,192,256]{2,1,0:T(8,128)(2,1)S(1)}, bf16[2,192,256]{2,1,0:T(8,128)(2,1)S(1)}, u32[]{:S(2)}, u32[]{:S(2)}) %collective-permute-start.12) | collective-permute-done | bytes 196640 | tf_op jit(solution)/shard_map/ppermute | solution.py:421
  56.8 2.2 %collective-permute-start.22 = (bf16[256,512]{1,0:T(8,128)(2,1)S(1)}, bf16[256,512]{1,0:T(8,128)(2,1)S(1)}, u32[]{:S(2)}, u32[]{:S(2)}) collective-permute-start(bf16[256,512]{1,0:T(8,128)(2,1)S(1)} %get-tuple-element.119.refs_3_), channel_id=1, source_target_pairs={{0,24},{8,16},{16,8},{24,0},{32,56},{40,48},{48,40},{56,32},{64,88... | collective-permute-start | bytes 786440 | tf_op jit(solution)/shard_map/ppermute | solution.py:424
  59.1 1.4 %collective-permute-start.21 = (bf16[256,512]{1,0:T(8,128)(2,1)S(1)}, bf16[256,512]{1,0:T(8,128)(2,1)S(1)}, u32[]{:S(2)}, u32[]{:S(2)}) collective-permute-start(bf16[256,512]{1,0:T(8,128)(2,1)S(1)} %get-tuple-element.118.refs_1_), channel_id=1, source_target_pairs={{0,16},{8,24},{16,0},{24,8},{32,48},{40,56},{48,32},{56,40},{64,80... | collective-permute-start | bytes 786440 | tf_op jit(solution)/shard_map/ppermute | solution.py:424
  62.3 2.0 %collective-permute-start.18 = (bf16[192,512]{1,0:T(8,128)(2,1)S(1)}, bf16[192,512]{1,0:T(8,128)(2,1)S(1)}, u32[]{:S(2)}, u32[]{:S(2)}) collective-permute-start(bf16[192,512]{1,0:T(8,128)(2,1)S(1)} %get-tuple-element.115._.a_2_), channel_id=1, source_target_pairs={{0,32},{8,40},{16,48},{24,56},{32,64},{40,72},{48,80},{56,88},{64,... | collective-permute-start | bytes 589832 | tf_op jit(solution)/shard_map/ppermute | solution.py:427
  64.5 4.0 %collective-permute-start.19 = (bf16[192,512]{1,0:T(8,128)(2,1)S(1)}, bf16[192,512]{1,0:T(8,128)(2,1)S(1)}, u32[]{:S(2)}, u32[]{:S(2)}) collective-permute-start(bf16[192,512]{1,0:T(8,128)(2,1)S(1)} %get-tuple-element.117), channel_id=1, source_target_pairs={{0,224},{8,232},{16,240},{24,248},{32,0},{40,8},{48,16},{56,24},{6... | collective-permute-start | bytes 589832 | tf_op jit(solution)/shard_map/ppermute | solution.py:427
  69.7 2.9 %collective-permute-done.21 = bf16[256,512]{1,0:T(8,128)(2,1)S(1)} collective-permute-done((bf16[256,512]{1,0:T(8,128)(2,1)S(1)}, bf16[256,512]{1,0:T(8,128)(2,1)S(1)}, u32[]{:S(2)}, u32[]{:S(2)}) %collective-permute-start.21) | collective-permute-done | bytes 262176 | tf_op jit(solution)/shard_map/ppermute | solution.py:424
  73.2 2.0 %collective-permute-start.26 = (bf16[192,512]{1,0:T(8,128)(2,1)S(1)}, bf16[192,512]{1,0:T(8,128)(2,1)S(1)}, u32[]{:S(2)}, u32[]{:S(2)}) collective-permute-start(bf16[192,512]{1,0:T(8,128)(2,1)S(1)} %get-tuple-element.120.a_4_), channel_id=1, source_target_pairs={{0,32},{8,40},{16,48},{24,56},{32,64},{40,72},{48,80},{56,88},{64,... | collective-permute-start | bytes 589832 | tf_op jit(solution)/shard_map/ppermute | solution.py:427
  75.2 4.0 %collective-permute-start.27 = (bf16[192,512]{1,0:T(8,128)(2,1)S(1)}, bf16[192,512]{1,0:T(8,128)(2,1)S(1)}, u32[]{:S(2)}, u32[]{:S(2)}) collective-permute-start(bf16[192,512]{1,0:T(8,128)(2,1)S(1)} %get-tuple-element.124), channel_id=1, source_target_pairs={{0,224},{8,232},{16,240},{24,248},{32,0},{40,8},{48,16},{56,24},{6... | collective-permute-start | bytes 589832 | tf_op jit(solution)/shard_map/ppermute | solution.py:427
  79.5 1.5 %collective-permute-start.23 = (bf16[2,400,256]{2,1,0:T(8,128)(2,1)S(1)}, bf16[2,400,256]{2,1,0:T(8,128)(2,1)S(1)}, u32[]{:S(2)}, u32[]{:S(2)}) collective-permute-start(bf16[2,400,256]{2,1,0:T(8,128)(2,1)S(1)} %shard_map.104), channel_id=1, source_target_pairs={{0,3},{1,2},{2,1},{3,0},{4,7},{5,6},{6,5},{7,4},{8,11},{9,10},{10,... | collective-permute-start | bytes 1228808 | tf_op jit(solution)/shard_map/ppermute | solution.py:421
  81.0 3.9 %collective-permute-done.26.a_2_ = bf16[192,512]{1,0:T(8,128)(2,1)S(1)} collective-permute-done((bf16[192,512]{1,0:T(8,128)(2,1)S(1)}, bf16[192,512]{1,0:T(8,128)(2,1)S(1)}, u32[]{:S(2)}, u32[]{:S(2)}) %collective-permute-start.26) | collective-permute-done | bytes 196640 | tf_op jit(solution)/shard_map/ppermute | solution.py:427
  84.9 2.1 %collective-permute-start.25 = (bf16[192,512]{1,0:T(8,128)(2,1)S(1)}, bf16[192,512]{1,0:T(8,128)(2,1)S(1)}, u32[]{:S(2)}, u32[]{:S(2)}) collective-permute-start(bf16[192,512]{1,0:T(8,128)(2,1)S(1)} %get-tuple-element.123), channel_id=1, source_target_pairs={{0,224},{8,232},{16,240},{24,248},{32,0},{40,8},{48,16},{56,24},{6... | collective-permute-start | bytes 589832 | tf_op jit(solution)/shard_map/ppermute | solution.py:427
  87.1 0.9 collective-permute-done.24.a_2_
  88.0 2.6 %collective-permute-done.25.a_3_ = bf16[192,512]{1,0:T(8,128)(2,1)S(1)} collective-permute-done((bf16[192,512]{1,0:T(8,128)(2,1)S(1)}, bf16[192,512]{1,0:T(8,128)(2,1)S(1)}, u32[]{:S(2)}, u32[]{:S(2)}) %collective-permute-start.25) | collective-permute-done | bytes 196640 | tf_op jit(solution)/shard_map/ppermute | solution.py:427
  92.1 1.0 collective-permute-start.28
  93.1 3.3 %collective-permute-start.32 = (bf16[192,512]{1,0:T(8,128)(2,1)S(1)}, bf16[192,512]{1,0:T(8,128)(2,1)S(1)}, u32[]{:S(2)}, u32[]{:S(2)}) collective-permute-start(bf16[192,512]{1,0:T(8,128)(2,1)S(1)} %get-tuple-element.129), channel_id=1, source_target_pairs={{0,224},{8,232},{16,240},{24,248},{32,0},{40,8},{48,16},{56,24},{6... | collective-permute-start | bytes 589832 | tf_op jit(solution)/shard_map/ppermute | solution.py:427
  96.4 4.1 %collective-permute-done.31.a_2_ = bf16[192,512]{1,0:T(8,128)(2,1)S(1)} collective-permute-done((bf16[192,512]{1,0:T(8,128)(2,1)S(1)}, bf16[192,512]{1,0:T(8,128)(2,1)S(1)}, u32[]{:S(2)}, u32[]{:S(2)}) %collective-permute-start.31) | collective-permute-done | bytes 196640 | tf_op jit(solution)/shard_map/ppermute | solution.py:427
  101.2 2.9 %collective-permute-start.36 = (bf16[192,512]{1,0:T(8,128)(2,1)}, bf16[192,512]{1,0:T(8,128)(2,1)}, u32[]{:S(2)}, u32[]{:S(2)}) collective-permute-start(bf16[192,512]{1,0:T(8,128)(2,1)} %get-tuple-element.132), channel_id=1, source_target_pairs={{0,224},{8,232},{16,240},{24,248},{32,0},{40,8},{48,16},{56,24},{6... | collective-permute-start | bytes 589832 | tf_op jit(solution)/shard_map/ppermute | solution.py:427
  104.1 2.5 %collective-permute-start.34 = (bf16[192,512]{1,0:T(8,128)(2,1)}, bf16[192,512]{1,0:T(8,128)(2,1)}, u32[]{:S(2)}, u32[]{:S(2)}) collective-permute-start(bf16[192,512]{1,0:T(8,128)(2,1)} %get-tuple-element.131), channel_id=1, source_target_pairs={{0,224},{8,232},{16,240},{24,248},{32,0},{40,8},{48,16},{56,24},{6... | collective-permute-start | bytes 589832 | tf_op jit(solution)/shard_map/ppermute | solution.py:427
  107.4 1.4 %collective-permute-done.36.a_1_ = bf16[192,512]{1,0:T(8,128)(2,1)} collective-permute-done((bf16[192,512]{1,0:T(8,128)(2,1)}, bf16[192,512]{1,0:T(8,128)(2,1)}, u32[]{:S(2)}, u32[]{:S(2)}) %collective-permute-start.36) | collective-permute-done | bytes 196640 | tf_op jit(solution)/shard_map/ppermute | solution.py:427
  108.8 1.0 shard_map.111
  109.8 3.5 %collective-permute-start.37 = (bf16[192,512]{1,0:T(8,128)(2,1)S(1)}, bf16[192,512]{1,0:T(8,128)(2,1)S(1)}, u32[]{:S(2)}, u32[]{:S(2)}) collective-permute-start(bf16[192,512]{1,0:T(8,128)(2,1)S(1)} %shard_map.111), channel_id=1, source_target_pairs={{0,224},{8,232},{16,240},{24,248},{32,0},{40,8},{48,16},{56,24},{6... | collective-permute-start | bytes 589832 | tf_op jit(solution)/shard_map/ppermute | solution.py:427
  113.3 1.2 collective-permute-done.33
  114.5 1.2 fusion.6
  115.7 1.3 %shard_map.108 = (f32[384,256]{1,0:T(8,128)S(1)}, f32[1,256]{1,0:T(1,128)S(1)}, bf16[400,256]{1,0:T(8,128)(2,1)S(1)}) custom-call(f32[2,384,256]{2,1,0:T(8,128)S(1)} %copy-done.4, f32[1,256]{1,0:T(1,128)S(1)} %copy-done.9, bf16[2,400,256]{2,1,0:T(8,128)(2,1)S(1)} %collective-permute-done.17.a_5_.first, bf16[2,400,256]{2,1,0:T(8,128)(2,1)S(1)} %copy-done.2, ...), custom_call_target="tpu_custom_call" | custom-call | flops 786432 | bytes 2949120 | tf_op jit(solution)/shard_map/pallas_call | solution.py:337
  117.9 5.0 %collective-permute-done.29 = bf16[400,256]{1,0:T(8,128)(2,1)S(1)} collective-permute-done((bf16[400,256]{1,0:T(8,128)(2,1)S(1)}, bf16[400,256]{1,0:T(8,128)(2,1)S(1)}, u32[]{:S(2)}, u32[]{:S(2)}) %collective-permute-start.29) | collective-permute-done | bytes 204832 | tf_op jit(solution)/shard_map/ppermute | solution.py:421
  123.6 1.1 convolution_convert_fusion
  124.7 0.8 broadcast_select_fusion
  (94 shorter events, 14.4 us)
Async XLA Ops:
  1.6 11.9 %copy-start.6 = (s32[512]{0:T(512)}, s32[512]{0:T(512)S(1)}, u32[]{:S(2)}) copy-start(s32[512]{0:T(512)S(1)} %convert_select_fusion) | copy-start | bytes 6148
  3.6 6.8 %collective-permute-start.1 = (bf16[256,384]{1,0:T(8,128)(2,1)S(1)}, bf16[256,384]{1,0:T(8,128)(2,1)S(1)}, u32[]{:S(2)}, u32[]{:S(2)}) collective-permute-start(bf16[256,384]{1,0:T(8,128)(2,1)S(1)} %get-tuple-element.77.a_1_), channel_id=1, source_target_pairs={{0,1},{1,0},{2,3},{3,2},{4,5},{5,4},{6,7},{7,6},{8,9},{9,8},{10,11... | collective-permute-start | bytes 589832 | tf_op jit(solution)/shard_map/ppermute | solution.py:421
  5.3 7.6 %collective-permute-start.2 = (bf16[256,384]{1,0:T(8,128)(2,1)S(1)}, bf16[256,384]{1,0:T(8,128)(2,1)S(1)}, u32[]{:S(2)}, u32[]{:S(2)}) collective-permute-start(bf16[256,384]{1,0:T(8,128)(2,1)S(1)} %get-tuple-element.77.a_1_), channel_id=1, source_target_pairs={{0,3},{1,2},{2,1},{3,0},{4,7},{5,6},{6,5},{7,4},{8,11},{9,10},{10,... | collective-permute-start | bytes 589832 | tf_op jit(solution)/shard_map/ppermute | solution.py:421
  7.4 6.1 %collective-permute-start.3 = (bf16[256,384]{1,0:T(8,128)(2,1)S(1)}, bf16[256,384]{1,0:T(8,128)(2,1)S(1)}, u32[]{:S(2)}, u32[]{:S(2)}) collective-permute-start(bf16[256,384]{1,0:T(8,128)(2,1)S(1)} %get-tuple-element.77.a_1_), channel_id=1, source_target_pairs={{0,4},{1,5},{2,6},{3,7},{4,0},{5,1},{6,2},{7,3},{8,12},{9,13},{10,... | collective-permute-start | bytes 589832 | tf_op jit(solution)/shard_map/ppermute | solution.py:421
  13.5 13.4 %collective-permute-start.4 = (bf16[256,384]{1,0:T(8,128)(2,1)S(1)}, bf16[256,384]{1,0:T(8,128)(2,1)S(1)}, u32[]{:S(2)}, u32[]{:S(2)}) collective-permute-start(bf16[256,384]{1,0:T(8,128)(2,1)S(1)} %collective-permute-done.3.a_2_), channel_id=1, source_target_pairs={{0,2},{1,3},{2,0},{3,1},{4,6},{5,7},{6,4},{7,5},{8,10},{9,11},{10,... | collective-permute-start | bytes 589832 | tf_op jit(solution)/shard_map/ppermute | solution.py:421
  14.5 12.4 %collective-permute-start.7 = (bf16[256,384]{1,0:T(8,128)(2,1)S(1)}, bf16[256,384]{1,0:T(8,128)(2,1)S(1)}, u32[]{:S(2)}, u32[]{:S(2)}) collective-permute-start(bf16[256,384]{1,0:T(8,128)(2,1)S(1)} %collective-permute-done.1.a_3_), channel_id=1, source_target_pairs={{0,4},{1,5},{2,6},{3,7},{4,0},{5,1},{6,2},{7,3},{8,12},{9,13},{10,... | collective-permute-start | bytes 589832 | tf_op jit(solution)/shard_map/ppermute | solution.py:421
  15.7 11.2 %collective-permute-start.8 = (bf16[256,384]{1,0:T(8,128)(2,1)S(1)}, bf16[256,384]{1,0:T(8,128)(2,1)S(1)}, u32[]{:S(2)}, u32[]{:S(2)}) collective-permute-start(bf16[256,384]{1,0:T(8,128)(2,1)S(1)} %collective-permute-done.2.a_4_), channel_id=1, source_target_pairs={{0,4},{1,5},{2,6},{3,7},{4,0},{5,1},{6,2},{7,3},{8,12},{9,13},{10,... | collective-permute-start | bytes 589832 | tf_op jit(solution)/shard_map/ppermute | solution.py:421
  16.5 10.4 %collective-permute-start.9 = (bf16[256,384]{1,0:T(8,128)(2,1)S(1)}, bf16[256,384]{1,0:T(8,128)(2,1)S(1)}, u32[]{:S(2)}, u32[]{:S(2)}) collective-permute-start(bf16[256,384]{1,0:T(8,128)(2,1)S(1)} %get-tuple-element.77.a_1_), channel_id=1, source_target_pairs={{0,2},{1,3},{2,0},{3,1},{4,6},{5,7},{6,4},{7,5},{8,10},{9,11},{10,... | collective-permute-start | bytes 589832 | tf_op jit(solution)/shard_map/ppermute | solution.py:421
  19.1 7.9 %collective-permute-start = (bf16[192,256]{1,0:T(8,128)(2,1)S(1)}, bf16[192,256]{1,0:T(8,128)(2,1)S(1)}, u32[]{:S(2)}, u32[]{:S(2)}) collective-permute-start(bf16[192,256]{1,0:T(8,128)(2,1)S(1)} %get-tuple-element.69), channel_id=1, source_target_pairs={{0,16},{8,24},{16,0},{24,8},{32,48},{40,56},{48,32},{56,40},{64,80... | collective-permute-start | bytes 294920 | tf_op jit(solution)/shard_map/ppermute | solution.py:424
  30.9 17.0 %copy-start.8 = (f32[1,256]{1,0:T(1,128)}, f32[1,256]{1,0:T(1,128)S(1)}, u32[]{:S(2)}) copy-start(f32[1,256]{1,0:T(1,128)S(1)} %get-tuple-element.98.refs_4_.route) | copy-start | bytes 3076
  30.9 13.6 %collective-permute-start.10 = (bf16[8,192,256]{2,1,0:T(8,128)(2,1)S(1)}, bf16[8,192,256]{2,1,0:T(8,128)(2,1)S(1)}, u32[]{:S(2)}, u32[]{:S(2)}) collective-permute-start(bf16[8,192,256]{2,1,0:T(8,128)(2,1)S(1)} %get-tuple-element.92.value), channel_id=1, source_target_pairs={{0,8},{8,0},{16,24},{24,16},{32,40},{40,32},{48,56},{56,48},{64,72... | collective-permute-start | bytes 2359304 | tf_op jit(solution)/shard_map/ppermute | solution.py:424
  31.0 15.0 %collective-permute-start.13 = (bf16[256,512]{1,0:T(8,128)(2,1)S(1)}, bf16[256,512]{1,0:T(8,128)(2,1)S(1)}, u32[]{:S(2)}, u32[]{:S(2)}) collective-permute-start(bf16[256,512]{1,0:T(8,128)(2,1)S(1)} %get-tuple-element.96.refs_2_), channel_id=1, source_target_pairs={{0,8},{8,0},{16,24},{24,16},{32,40},{40,32},{48,56},{56,48},{64,72... | collective-permute-start | bytes 786440 | tf_op jit(solution)/shard_map/ppermute | solution.py:424
  31.5 25.3 %collective-permute-start.15 = (bf16[256,512]{1,0:T(8,128)(2,1)S(1)}, bf16[256,512]{1,0:T(8,128)(2,1)S(1)}, u32[]{:S(2)}, u32[]{:S(2)}) collective-permute-start(bf16[256,512]{1,0:T(8,128)(2,1)S(1)} %get-tuple-element.96.refs_2_), channel_id=1, source_target_pairs={{0,24},{8,16},{16,8},{24,0},{32,56},{40,48},{48,40},{56,32},{64,88... | collective-permute-start | bytes 786440 | tf_op jit(solution)/shard_map/ppermute | solution.py:424
  32.5 10.6 %collective-permute-start.5 = (bf16[192,256]{1,0:T(8,128)(2,1)S(1)}, bf16[192,256]{1,0:T(8,128)(2,1)S(1)}, u32[]{:S(2)}, u32[]{:S(2)}) collective-permute-start(bf16[192,256]{1,0:T(8,128)(2,1)S(1)} %collective-permute-done), channel_id=1, source_target_pairs={{0,4},{1,5},{2,6},{3,7},{4,0},{5,1},{6,2},{7,3},{8,12},{9,13},{10,... | collective-permute-start | bytes 294920 | tf_op jit(solution)/shard_map/ppermute | solution.py:421
  33.8 22.9 %collective-permute-start.14 = (bf16[256,512]{1,0:T(8,128)(2,1)S(1)}, bf16[256,512]{1,0:T(8,128)(2,1)S(1)}, u32[]{:S(2)}, u32[]{:S(2)}) collective-permute-start(bf16[256,512]{1,0:T(8,128)(2,1)S(1)} %get-tuple-element.94.refs_0_), channel_id=1, source_target_pairs={{0,16},{8,24},{16,0},{24,8},{32,48},{40,56},{48,32},{56,40},{64,80... | collective-permute-start | bytes 786440 | tf_op jit(solution)/shard_map/ppermute | solution.py:424
  43.1 11.6 %collective-permute-start.6 = (bf16[2,192,256]{2,1,0:T(8,128)(2,1)S(1)}, bf16[2,192,256]{2,1,0:T(8,128)(2,1)S(1)}, u32[]{:S(2)}, u32[]{:S(2)}) collective-permute-start(bf16[2,192,256]{2,1,0:T(8,128)(2,1)S(1)} %pad_maximum_fusion.refs_5_.a_1_), channel_id=1, source_target_pairs={{0,1},{1,0},{2,3},{3,2},{4,5},{5,4},{6,7},{7,6},{8,9},{9,8},{10,11... | collective-permute-start | bytes 589832 | tf_op jit(solution)/shard_map/ppermute | solution.py:421
  44.5 11.5 %collective-permute-start.12 = (bf16[2,192,256]{2,1,0:T(8,128)(2,1)S(1)}, bf16[2,192,256]{2,1,0:T(8,128)(2,1)S(1)}, u32[]{:S(2)}, u32[]{:S(2)}) collective-permute-start(bf16[2,192,256]{2,1,0:T(8,128)(2,1)S(1)} %pad_maximum_fusion.refs_5_.a_1_), channel_id=1, source_target_pairs={{0,3},{1,2},{2,1},{3,0},{4,7},{5,6},{6,5},{7,4},{8,11},{9,10},{10,... | collective-permute-start | bytes 589832 | tf_op jit(solution)/shard_map/ppermute | solution.py:421
  46.0 10.1 %collective-permute-start.11 = (bf16[2,192,256]{2,1,0:T(8,128)(2,1)S(1)}, bf16[2,192,256]{2,1,0:T(8,128)(2,1)S(1)}, u32[]{:S(2)}, u32[]{:S(2)}) collective-permute-start(bf16[2,192,256]{2,1,0:T(8,128)(2,1)S(1)} %pad_maximum_fusion.refs_5_.a_1_), channel_id=1, source_target_pairs={{0,2},{1,3},{2,0},{3,1},{4,6},{5,7},{6,4},{7,5},{8,10},{9,11},{10,... | collective-permute-start | bytes 589832 | tf_op jit(solution)/shard_map/ppermute | solution.py:421
  56.7 5.0 %collective-permute-start.16 = (bf16[8,192,256]{2,1,0:T(8,128)(2,1)S(1)}, bf16[8,192,256]{2,1,0:T(8,128)(2,1)S(1)}, u32[]{:S(2)}, u32[]{:S(2)}) collective-permute-start(bf16[8,192,256]{2,1,0:T(8,128)(2,1)S(1)} %shard_map.98), channel_id=1, source_target_pairs={{0,8},{8,0},{16,24},{24,16},{32,40},{40,32},{48,56},{56,48},{64,72... | collective-permute-start | bytes 2359304 | tf_op jit(solution)/shard_map/ppermute | solution.py:424
  56.8 12.3 %collective-permute-start.22 = (bf16[256,512]{1,0:T(8,128)(2,1)S(1)}, bf16[256,512]{1,0:T(8,128)(2,1)S(1)}, u32[]{:S(2)}, u32[]{:S(2)}) collective-permute-start(bf16[256,512]{1,0:T(8,128)(2,1)S(1)} %get-tuple-element.119.refs_3_), channel_id=1, source_target_pairs={{0,24},{8,16},{16,8},{24,0},{32,56},{40,48},{48,40},{56,32},{64,88... | collective-permute-start | bytes 786440 | tf_op jit(solution)/shard_map/ppermute | solution.py:424
  59.0 2.1 %collective-permute-start.20 = (bf16[256,512]{1,0:T(8,128)(2,1)S(1)}, bf16[256,512]{1,0:T(8,128)(2,1)S(1)}, u32[]{:S(2)}, u32[]{:S(2)}) collective-permute-start(bf16[256,512]{1,0:T(8,128)(2,1)S(1)} %get-tuple-element.119.refs_3_), channel_id=1, source_target_pairs={{0,8},{8,0},{16,24},{24,16},{32,40},{40,32},{48,56},{56,48},{64,72... | collective-permute-start | bytes 786440 | tf_op jit(solution)/shard_map/ppermute | solution.py:424
  59.1 13.5 %collective-permute-start.21 = (bf16[256,512]{1,0:T(8,128)(2,1)S(1)}, bf16[256,512]{1,0:T(8,128)(2,1)S(1)}, u32[]{:S(2)}, u32[]{:S(2)}) collective-permute-start(bf16[256,512]{1,0:T(8,128)(2,1)S(1)} %get-tuple-element.118.refs_1_), channel_id=1, source_target_pairs={{0,16},{8,24},{16,0},{24,8},{32,48},{40,56},{48,32},{56,40},{64,80... | collective-permute-start | bytes 786440 | tf_op jit(solution)/shard_map/ppermute | solution.py:424
  62.3 44.3 %copy-start = (f32[1536,512]{1,0:T(8,128)}, f32[1536,512]{1,0:T(8,128)S(1)}, u32[]{:S(2)}) copy-start(f32[1536,512]{1,0:T(8,128)S(1)} %add_add_fusion) | copy-start | bytes 9437188
  62.3 16.9 %collective-permute-start.18 = (bf16[192,512]{1,0:T(8,128)(2,1)S(1)}, bf16[192,512]{1,0:T(8,128)(2,1)S(1)}, u32[]{:S(2)}, u32[]{:S(2)}) collective-permute-start(bf16[192,512]{1,0:T(8,128)(2,1)S(1)} %get-tuple-element.115._.a_2_), channel_id=1, source_target_pairs={{0,32},{8,40},{16,48},{24,56},{32,64},{40,72},{48,80},{56,88},{64,... | collective-permute-start | bytes 589832 | tf_op jit(solution)/shard_map/ppermute | solution.py:427
  64.4 22.6 %collective-permute-start.17 = (bf16[2,400,256]{2,1,0:T(8,128)(2,1)S(1)}, bf16[2,400,256]{2,1,0:T(8,128)(2,1)S(1)}, u32[]{:S(2)}, u32[]{:S(2)}) collective-permute-start(bf16[2,400,256]{2,1,0:T(8,128)(2,1)S(1)} %shard_map.100), channel_id=1, source_target_pairs={{0,1},{1,0},{2,3},{3,2},{4,5},{5,4},{6,7},{7,6},{8,9},{9,8},{10,11... | collective-permute-start | bytes 1228808 | tf_op jit(solution)/shard_map/ppermute | solution.py:421
  64.5 14.8 %collective-permute-start.19 = (bf16[192,512]{1,0:T(8,128)(2,1)S(1)}, bf16[192,512]{1,0:T(8,128)(2,1)S(1)}, u32[]{:S(2)}, u32[]{:S(2)}) collective-permute-start(bf16[192,512]{1,0:T(8,128)(2,1)S(1)} %get-tuple-element.117), channel_id=1, source_target_pairs={{0,224},{8,232},{16,240},{24,248},{32,0},{40,8},{48,16},{56,24},{6... | collective-permute-start | bytes 589832 | tf_op jit(solution)/shard_map/ppermute | solution.py:427
  73.2 11.7 %collective-permute-start.26 = (bf16[192,512]{1,0:T(8,128)(2,1)S(1)}, bf16[192,512]{1,0:T(8,128)(2,1)S(1)}, u32[]{:S(2)}, u32[]{:S(2)}) collective-permute-start(bf16[192,512]{1,0:T(8,128)(2,1)S(1)} %get-tuple-element.120.a_4_), channel_id=1, source_target_pairs={{0,32},{8,40},{16,48},{24,56},{32,64},{40,72},{48,80},{56,88},{64,... | collective-permute-start | bytes 589832 | tf_op jit(solution)/shard_map/ppermute | solution.py:427
  75.2 11.8 %collective-permute-start.27 = (bf16[192,512]{1,0:T(8,128)(2,1)S(1)}, bf16[192,512]{1,0:T(8,128)(2,1)S(1)}, u32[]{:S(2)}, u32[]{:S(2)}) collective-permute-start(bf16[192,512]{1,0:T(8,128)(2,1)S(1)} %get-tuple-element.124), channel_id=1, source_target_pairs={{0,224},{8,232},{16,240},{24,248},{32,0},{40,8},{48,16},{56,24},{6... | collective-permute-start | bytes 589832 | tf_op jit(solution)/shard_map/ppermute | solution.py:427
  79.3 8.7 %collective-permute-start.24 = (bf16[192,512]{1,0:T(8,128)(2,1)S(1)}, bf16[192,512]{1,0:T(8,128)(2,1)S(1)}, u32[]{:S(2)}, u32[]{:S(2)}) collective-permute-start(bf16[192,512]{1,0:T(8,128)(2,1)S(1)} %get-tuple-element.121._.a_4_), channel_id=1, source_target_pairs={{0,32},{8,40},{16,48},{24,56},{32,64},{40,72},{48,80},{56,88},{64,... | collective-permute-start | bytes 589832 | tf_op jit(solution)/shard_map/ppermute | solution.py:427
  79.5 16.9 %collective-permute-start.23 = (bf16[2,400,256]{2,1,0:T(8,128)(2,1)S(1)}, bf16[2,400,256]{2,1,0:T(8,128)(2,1)S(1)}, u32[]{:S(2)}, u32[]{:S(2)}) collective-permute-start(bf16[2,400,256]{2,1,0:T(8,128)(2,1)S(1)} %shard_map.104), channel_id=1, source_target_pairs={{0,3},{1,2},{2,1},{3,0},{4,7},{5,6},{6,5},{7,4},{8,11},{9,10},{10,... | collective-permute-start | bytes 1228808 | tf_op jit(solution)/shard_map/ppermute | solution.py:421
  84.9 5.7 %collective-permute-start.25 = (bf16[192,512]{1,0:T(8,128)(2,1)S(1)}, bf16[192,512]{1,0:T(8,128)(2,1)S(1)}, u32[]{:S(2)}, u32[]{:S(2)}) collective-permute-start(bf16[192,512]{1,0:T(8,128)(2,1)S(1)} %get-tuple-element.123), channel_id=1, source_target_pairs={{0,224},{8,232},{16,240},{24,248},{32,0},{40,8},{48,16},{56,24},{6... | collective-permute-start | bytes 589832 | tf_op jit(solution)/shard_map/ppermute | solution.py:427
  92.1 16.7 %collective-permute-start.28 = (bf16[2,400,256]{2,1,0:T(8,128)(2,1)}, bf16[2,400,256]{2,1,0:T(8,128)(2,1)}, u32[]{:S(2)}, u32[]{:S(2)}) collective-permute-start(bf16[2,400,256]{2,1,0:T(8,128)(2,1)} %shard_map.107), channel_id=1, source_target_pairs={{0,2},{1,3},{2,0},{3,1},{4,6},{5,7},{6,4},{7,5},{8,10},{9,11},{10,... | collective-permute-start | bytes 1228808 | tf_op jit(solution)/shard_map/ppermute | solution.py:421
  93.1 7.4 %collective-permute-start.31 = (bf16[192,512]{1,0:T(8,128)(2,1)S(1)}, bf16[192,512]{1,0:T(8,128)(2,1)S(1)}, u32[]{:S(2)}, u32[]{:S(2)}) collective-permute-start(bf16[192,512]{1,0:T(8,128)(2,1)S(1)} %get-tuple-element.125.a_4_), channel_id=1, source_target_pairs={{0,32},{8,40},{16,48},{24,56},{32,64},{40,72},{48,80},{56,88},{64,... | collective-permute-start | bytes 589832 | tf_op jit(solution)/shard_map/ppermute | solution.py:427
  93.1 7.4 %collective-permute-start.32 = (bf16[192,512]{1,0:T(8,128)(2,1)S(1)}, bf16[192,512]{1,0:T(8,128)(2,1)S(1)}, u32[]{:S(2)}, u32[]{:S(2)}) collective-permute-start(bf16[192,512]{1,0:T(8,128)(2,1)S(1)} %get-tuple-element.129), channel_id=1, source_target_pairs={{0,224},{8,232},{16,240},{24,248},{32,0},{40,8},{48,16},{56,24},{6... | collective-permute-start | bytes 589832 | tf_op jit(solution)/shard_map/ppermute | solution.py:427
  96.4 10.2 %collective-permute-start.30 = (bf16[192,512]{1,0:T(8,128)(2,1)S(1)}, bf16[192,512]{1,0:T(8,128)(2,1)S(1)}, u32[]{:S(2)}, u32[]{:S(2)}) collective-permute-start(bf16[192,512]{1,0:T(8,128)(2,1)S(1)} %get-tuple-element.126._.a_4_), channel_id=1, source_target_pairs={{0,32},{8,40},{16,48},{24,56},{32,64},{40,72},{48,80},{56,88},{64,... | collective-permute-start | bytes 589832 | tf_op jit(solution)/shard_map/ppermute | solution.py:427
  96.4 4.8 %copy-start.1 = (bf16[2,400,256]{2,1,0:T(8,128)(2,1)}, bf16[2,400,256]{2,1,0:T(8,128)(2,1)S(1)}, u32[]{:S(2)}) copy-start(bf16[2,400,256]{2,1,0:T(8,128)(2,1)S(1)} %collective-permute-done.23.third.a_5_) | copy-start | bytes 1228804
  101.2 6.1 %copy-start.5 = (bf16[192,512]{1,0:T(8,128)(2,1)}, bf16[192,512]{1,0:T(8,128)(2,1)S(1)}, u32[]{:S(2)}) copy-start(bf16[192,512]{1,0:T(8,128)(2,1)S(1)} %get-tuple-element.130.a_2_) | copy-start | bytes 589828
  101.2 7.6 %collective-permute-start.36 = (bf16[192,512]{1,0:T(8,128)(2,1)}, bf16[192,512]{1,0:T(8,128)(2,1)}, u32[]{:S(2)}, u32[]{:S(2)}) collective-permute-start(bf16[192,512]{1,0:T(8,128)(2,1)} %get-tuple-element.132), channel_id=1, source_target_pairs={{0,224},{8,232},{16,240},{24,248},{32,0},{40,8},{48,16},{56,24},{6... | collective-permute-start | bytes 589832 | tf_op jit(solution)/shard_map/ppermute | solution.py:427
  104.1 9.3 %collective-permute-start.34 = (bf16[192,512]{1,0:T(8,128)(2,1)}, bf16[192,512]{1,0:T(8,128)(2,1)}, u32[]{:S(2)}, u32[]{:S(2)}) collective-permute-start(bf16[192,512]{1,0:T(8,128)(2,1)} %get-tuple-element.131), channel_id=1, source_target_pairs={{0,224},{8,232},{16,240},{24,248},{32,0},{40,8},{48,16},{56,24},{6... | collective-permute-start | bytes 589832 | tf_op jit(solution)/shard_map/ppermute | solution.py:427
  107.3 7.2 %collective-permute-start.33 = (bf16[192,512]{1,0:T(8,128)(2,1)}, bf16[192,512]{1,0:T(8,128)(2,1)}, u32[]{:S(2)}, u32[]{:S(2)}) collective-permute-start(bf16[192,512]{1,0:T(8,128)(2,1)} %shard_map.110.a_2_), channel_id=1, source_target_pairs={{0,32},{8,40},{16,48},{24,56},{32,64},{40,72},{48,80},{56,88},{64,... | collective-permute-start | bytes 589832 | tf_op jit(solution)/shard_map/ppermute | solution.py:427
  107.3 8.4 %copy-start.2 = (bf16[2,400,256]{2,1,0:T(8,128)(2,1)S(1)}, bf16[2,400,256]{2,1,0:T(8,128)(2,1)}, u32[]{:S(2)}) copy-start(bf16[2,400,256]{2,1,0:T(8,128)(2,1)} %copy-done.1) | copy-start | bytes 1228804
  107.3 8.4 %copy-start.4 = (f32[2,384,256]{2,1,0:T(8,128)S(1)}, f32[2,384,256]{2,1,0:T(8,128)}, u32[]{:S(2)}) copy-start(f32[2,384,256]{2,1,0:T(8,128)} %copy-done.3) | copy-start | bytes 2359300
  107.3 8.4 %copy-start.9 = (f32[1,256]{1,0:T(1,128)S(1)}, f32[1,256]{1,0:T(1,128)}, u32[]{:S(2)}) copy-start(f32[1,256]{1,0:T(1,128)} %copy-done.8) | copy-start | bytes 3076
  107.3 10.3 %collective-permute-start.35 = (bf16[192,512]{1,0:T(8,128)(2,1)}, bf16[192,512]{1,0:T(8,128)(2,1)S(1)}, u32[]{:S(2)}, u32[]{:S(2)}) collective-permute-start(bf16[192,512]{1,0:T(8,128)(2,1)} %copy-done.5), channel_id=1, source_target_pairs={{0,32},{8,40},{16,48},{24,56},{32,64},{40,72},{48,80},{56,88},{64,... | collective-permute-start | bytes 589832 | tf_op jit(solution)/shard_map/ppermute | solution.py:427
  109.8 13.1 %copy-start.7 = (s32[512]{0:T(512)S(1)}, s32[512]{0:T(512)}, u32[]{:S(2)}) copy-start(s32[512]{0:T(512)} %copy-done.6) | copy-start | bytes 6148
  109.8 7.8 %collective-permute-start.37 = (bf16[192,512]{1,0:T(8,128)(2,1)S(1)}, bf16[192,512]{1,0:T(8,128)(2,1)S(1)}, u32[]{:S(2)}, u32[]{:S(2)}) collective-permute-start(bf16[192,512]{1,0:T(8,128)(2,1)S(1)} %shard_map.111), channel_id=1, source_target_pairs={{0,224},{8,232},{16,240},{24,248},{32,0},{40,8},{48,16},{56,24},{6... | collective-permute-start | bytes 589832 | tf_op jit(solution)/shard_map/ppermute | solution.py:427
  117.0 5.8 %collective-permute-start.29 = (bf16[400,256]{1,0:T(8,128)(2,1)S(1)}, bf16[400,256]{1,0:T(8,128)(2,1)S(1)}, u32[]{:S(2)}, u32[]{:S(2)}) collective-permute-start(bf16[400,256]{1,0:T(8,128)(2,1)S(1)} %get-tuple-element.128), channel_id=1, source_target_pairs={{0,4},{1,5},{2,6},{3,7},{4,0},{5,1},{6,2},{7,3},{8,12},{9,13},{10,... | collective-permute-start | bytes 614408 | tf_op jit(solution)/shard_map/ppermute | solution.py:421
  117.8 6.9 %collective-permute-start.38 = (bf16[96,1024]{1,0:T(8,128)(2,1)S(1)}, bf16[96,1024]{1,0:T(8,128)(2,1)S(1)}, u32[]{:S(2)}, u32[]{:S(2)}) collective-permute-start(bf16[96,1024]{1,0:T(8,128)(2,1)S(1)} %fusion.10), channel_id=1, source_target_pairs={{0,8},{8,0},{16,24},{24,16},{32,40},{40,32},{48,56},{56,48},{64,72... | collective-permute-start | bytes 589832 | tf_op jit(solution)/shard_map/ppermute | solution.py:424
  (1 other events, 0.9 us)

commit v2 on v1

--- a/solution.py
+++ b/solution.py
@@ -15,6 +15,13 @@
 
 def whole(shape):
     return pl.BlockSpec(shape, lambda *_: (0,) * len(shape))
+
+
+def placed(info, k, n_z):
+    ahead = lax.rem((info[0] ^ k) - info[1] + n_z, n_z)
+    behind = lax.rem(n_z - ahead, n_z)
+    first = info[3] == 0
+    return jnp.where(first, ahead, behind), jnp.where(first, behind, ahead)
 
 
 def dispatch_kernel(info, slots, tokens, picked, far, turned):
@@ -156,11 +163,10 @@
     pieces = refs[:n]
     wg, wu, gate_in, up_in, near_in, cot, share = refs[n : n + 7]
     mine, other = refs[n + 7 : n + 7 + CHUNKS], refs[n + 7 + CHUNKS : n + 7 + 2 * CHUNKS]
-    near_left, route_out, held, turned, route = refs[n + 7 + 2 * CHUNKS :]
+    near_left, near_send, route_out, held, turned, route = refs[n + 7 + 2 * CHUNKS :]
     step = pl.program_id(0)
     piece, cap = turned.shape
     half, block = near_left.shape[1], cot.shape[1]
-    at = lambda k: lax.rem((info[0] ^ k) - info[1] + n_z, n_z)
 
     @pl.when(step == 0)
     def _():
@@ -193,11 +199,15 @@
     def _():
         route_out[...] = jnp.broadcast_to(route[...], (cap, 128)).T[:1, :]
         for i, k in enumerate(soon):
-            near_left[at(k)] = near_in[i]
+            at, there = placed(info, k, n_z)
+            near_left[at] = near_in[i]
+            near_send[there] = near_in[i]
         for i, k in enumerate(late):
             turned[...] = held[:, i * piece : (i + 1) * piece].T
             start = pl.multiple_of(info[2] * half, half)
-            near_left[at(k)] = turned[pl.ds(start, half), :]
+            at, there = placed(info, k, n_z)
+            near_left[at] = turned[pl.ds(start, half), :]
+            near_send[there] = turned[pl.ds(start, half), :]
 
 
 def forward(info, pieces, soon, late, w_gate, w_up, gate, up, near, cot_rows, share, n_z):
@@ -207,7 +217,7 @@
     block = width // CHUNKS
     cols = pl.BlockSpec((cap, block), lambda j, *_: (0, j))
     near_left = (n_z, piece // 2, cap)
-    outs = [((cap, block), BF)] * (2 * CHUNKS) + [(near_left, BF), ((1, cap), F32)]
+    outs = [((cap, block), BF)] * (2 * CHUNKS) + [(near_left, BF)] * 2 + [((1, cap), F32)]
     held = pl.BlockSpec(memory_space=pltpu.VMEM)
     return pl.pallas_call(
         lambda *a: forward_kernel(n, soon, late, n_z, *a),
@@ -378,11 +388,12 @@
 
 
 def far_kernel(n, n_z, info, *refs):
-    out = refs[-1]
+    out, send = refs[-2:]
     for y in range(n // 2):
         for x in range(2):
-            at = lax.rem((info[0] ^ (y + x * (n // 2))) - info[1] + n_z, n_z)
+            at, there = placed(info, y + x * (n // 2), n_z)
             out[at] = refs[y][x]
+            send[there] = refs[y][x]
 
 
 def far_operand(info, arrays, n, n_z):
@@ -393,9 +404,9 @@
             num_scalar_prefetch=1,
             grid=(1,),
             in_specs=[whole(a.shape) for a in arrays],
-            out_specs=whole((n_z, rows, cap)),
-        ),
-        out_shape=jax.ShapeDtypeStruct((n_z, rows, cap), BF),
+            out_specs=[whole((n_z, rows, cap))] * 2,
+        ),
+        out_shape=[jax.ShapeDtypeStruct((n_z, rows, cap), BF)] * 2,
         compiler_params=pltpu.CompilerParams(vmem_limit_bytes=8 * MIB),
         cost_estimate=pl.CostEstimate(
             flops=0, bytes_accessed=4 * n * rows * cap, transcendentals=0
@@ -424,7 +435,13 @@
         return lax.ppermute(x, "dp", [(i, i ^ k) for i in range(n_dp)])
 
     def along_z(x, k):
-        return lax.ppermute(x, "dp", [(i, (i + 4 * k) % n_dp) for i in range(n_dp)])
+        pairs = [(i, (i + 4 * (k if i % 2 == 0 else -k)) % n_dp) for i in range(n_dp)]
+        return lax.ppermute(x, "dp", pairs)
+
+    def over_both(x, k, m):
+        n_all = n_dp * n_tensor
+        pairs = [(i, i ^ (k * n_tensor + m)) for i in range(n_all)]
+        return lax.ppermute(x, ("dp", "tensor"), pairs)
 
     selected = expert_ids == 0
     flag = jnp.any(selected, axis=1)
@@ -446,10 +463,11 @@
     near[xlo] = over_tensor(picked, xlo)
     near[1] = over_tensor(picked, 1)
     near[3] = over_tensor(picked, 3)
+    far_other = over_both(far_piece, 2, xlo)
+    picked, near[1], near[3], near[xlo], cot_rows, share, far_other, far_piece = tie(
+        (picked, near[1], near[3], near[xlo], cot_rows, share, far_other, far_piece)
+    )
     far_piece = over_dp(far_piece, 2)
-    picked, near[1], near[3], near[xlo], cot_rows, share = tie(
-        (picked, near[1], near[3], near[xlo], cot_rows, share)
-    )
     near[0] = picked
     near[xlo + 1] = over_tensor(near[1], xlo)
     near[xlo + 3] = over_tensor(near[3], xlo)
@@ -458,23 +476,21 @@
     soon, late = (0, xlo, 1, 3), (xlo + 1, xlo + 3, 2, xlo + 2)
     order = jnp.stack([t ^ k for k in soon + late] + [xh]).astype(jnp.int32)
     gate, up, near_soon, *weights = early(order, [near[k] for k in soon], w_gate, w_up)
-    far_piece, near[late[3]] = tie((far_piece, near[late[3]]))
-    far_pair = jnp.stack([far_piece, over_tensor(far_piece, xlo)])
-    late_near, gate, up = tie(([near[k] for k in late], gate, up))
+    far_pair = jnp.stack([far_piece, far_other])
+    late_near, gate, up, far_pair = tie(([near[k] for k in late], gate, up, far_pair))
     outs = forward(
         info, late_near, soon, late, *weights, gate, up, near_soon, cot_rows, share, n_z
     )
     mine, other = outs[:CHUNKS], outs[CHUNKS : 2 * CHUNKS]
-    near_left, route_part = outs[2 * CHUNKS :]
+    near_left, near_send, route_part = outs[2 * CHUNKS :]
 
     def to_partners(c):
         return [mine[c], over_dp(other[c], 1), over_dp(mine[c], 2), over_dp(other[c], 3)]
 
     cots = [to_partners(0)]
-    near_sib = over_dp(near_left, 1)
-    far = [far_pair] + [over_tensor(far_pair, k) for k in (1, 3)]
+    near_sib = over_dp(near_send, 1)
     far_pair, near_sib = tie((far_pair, near_sib))
-    far.insert(2, over_tensor(far_pair, 2))
+    far = [far_pair] + [over_tensor(far_pair, k) for k in (1, 2, 3)]
     own_part, *sent = token_parts(info, mine, other, route_part, far_pair, weights, piece)
 
     def product(a, b):
@@ -482,8 +498,8 @@
 
     close = product(near_left, cots[0][0]) + product(near_sib, cots[0][1])
     far, own_part, sent, mine, other, close = tie((far, own_part, sent, mine, other, close))
-    far_left = far_operand(info, far, n_tensor, n_z)
-    far_sib = over_dp(far_left, 1)
+    far_left, far_send = far_operand(info, far, n_tensor, n_z)
+    far_sib = over_dp(far_send, 1)
     for c in range(1, CHUNKS):
         mine, other, cots[-1] = tie((mine, other, cots[-1]))
         cots.append(to_partners(c))
@@ -532,15 +548,17 @@
         waited = rings[0].hop(i, [waited])
         if i < 3:
             sums[4 - i] = over_tensor(after(sent[i], waited), 4 - i)
+        else:
+            parts = [sums[1], sums[3], sums[2]]
+            total, route_total, message = combine(own_part, route_part, parts)
         for ring in rings[1:]:
-            waited = ring.hop(i, [waited, sums[(1, 3, 2)[i - 1]]])
+            waited = ring.hop(i, [waited, message if i == 3 else sums[(1, 3)[i - 1]]])
     whole_rows = jnp.concatenate([ring.finish() for ring in rings], axis=2)
     kept = lax.dynamic_index_in_dim(whole_rows, core, 0, keepdims=False)
     swapped = over_dp(lax.dynamic_index_in_dim(whole_rows, 1 - core, 0, keepdims=False), 1)
     gate_grad = jnp.where(core == 0, kept, swapped)
     up_grad = jnp.where(core == 0, swapped, kept)
 
-    total, route_total, message = combine(own_part, route_part, [sums[1], sums[3], sums[2]])
     message = over_tensor(message, xlo)
     total = total + message[:piece].astype(F32)
     route_total = route_total + row_of(message[piece:])

time: 126 us -> 123 us (0.976)
  waiting for transfers between devices: 33.3 us -> 20.5 us
  starting transfers between devices: 54.8 us -> 62.7 us
  local copies, waits for them, and re-layouts: 1.01 us -> 2.92 us
    ppermute x15 -> x14, waiting for transfers between devices: 16 us -> 8.06 us  [over_tensor(): return lax.ppermute(x, 'tensor', [(i, i ^ k) for i in range(n_tensor)])]
    ppermute x14 -> x15, starting transfers between devices: 26.4 us -> 33.4 us  [the longest x14 31.2 us: along_z(): return lax.ppermute(x, 'dp', pairs)]
    ppermute x14 -> x15, waiting for transfers between devices: 14.2 us -> 9.5 us  [the longest x14 9.42 us: along_z(): return lax.ppermute(x, 'dp', pairs)]
    unnamed x20, local copies, waits for them, and re-layouts: 0.92 us -> 2.83 us
    ppermute x15 -> x14, starting transfers between devices: 18.7 us -> 18.8 us  [over_tensor(): return lax.ppermute(x, 'tensor', [(i, i ^ k) for i in range(n_tensor)])]
  transfers between devices with their start and end apart: 39 -> 39, of which waited for: 13 -> 12; matrix products, arithmetic and copies ran while one was open for 7% -> 7% of each run, Pallas kernels for 15% -> 16%
where the time goes in v2:
time: 123 us
  starting transfers between devices  62.7 us (51%)
  Pallas kernels  25.1 us (20%)
  waiting for transfers between devices  20.5 us (17%)
  matrix products  5.81 us (5%)
  other arithmetic  4.44 us (4%)
  local copies, waits for them, and re-layouts  2.92 us (2%)
    ppermute x14, starting transfers between devices, along_z(): return lax.ppermute(x, 'dp', pairs)  31.2 us
    ppermute x14, starting transfers between devices, over_tensor(): return lax.ppermute(x, 'tensor', [(i, i ^ k) for i in range(n_tensor)])  18.8 us
    ppermute x10, starting transfers between devices, over_dp(): return lax.ppermute(x, 'dp', [(i, i ^ k) for i in range(n_dp)])  10.5 us
    ppermute x14, waiting for transfers between devices, along_z(): return lax.ppermute(x, 'dp', pairs)  9.42 us
    ppermute x14, waiting for transfers between devices, over_tensor(): return lax.ppermute(x, 'tensor', [(i, i ^ k) for i in range(n_tensor)])  8.06 us
    pallas_call x1, Pallas kernels, token_parts(): pl.pallas_call(back_kernel, grid_spec=pltpu.PrefetchScalarGridSpec(num_sc...  5.93 us
    pallas_call x1, Pallas kernels, early(): pl.pallas_call(lambda *a: early_kernel(n, *a), grid_spec=pltpu.PrefetchSc...  5.45 us
    dot_general x8, matrix products, product(): return jnp.dot(a.reshape(n_z * half, CAP), b, preferred_element_type=F32)  4.54 us
  transfers between devices with their start and end apart: 39, of which 12 were waited for; matrix products, arithmetic and copies ran while one was open for 7% of the time, Pallas kernels for 16%

profile of v2, /device:TPU:2, one launch (start us, length us, event | category | flops | bytes accessed | tf_op | source)
XLA Modules:
  0.0 122.6 jit_solution(7585326442982089059)
XLA Ops:
  1.7 1.9 %shard_map.93 = (bf16[256,384]{1,0:T(8,128)(2,1)S(1)}, bf16[192,256]{1,0:T(8,128)(2,1)S(1)}) custom-call(s32[4]{0:T(128)S(1)} %pad_add_fusion.info.a_0_, s32[1,512]{1,0:T(1,128)S(1)} %bitcast.70, bf16[512,384]{1,0:T(8,128)(2,1)} %tokens.1), custom_call_target="tpu_custom_call" | custom-call | flops 100663296 | bytes 786432 | tf_op jit(solution)/shard_map/pallas_call | solution.py:41
  3.6 1.7 %collective-permute-start = (bf16[256,384]{1,0:T(8,128)(2,1)S(1)}, bf16[256,384]{1,0:T(8,128)(2,1)S(1)}, u32[]{:S(2)}, u32[]{:S(2)}) collective-permute-start(bf16[256,384]{1,0:T(8,128)(2,1)S(1)} %get-tuple-element.79.a_1_), channel_id=1, source_target_pairs={{0,1},{1,0},{2,3},{3,2},{4,5},{5,4},{6,7},{7,6},{8,9},{9,8},{10,11... | collective-permute-start | bytes 589832 | tf_op jit(solution)/shard_map/ppermute | solution.py:432
  5.3 2.2 %collective-permute-start.1 = (bf16[256,384]{1,0:T(8,128)(2,1)S(1)}, bf16[256,384]{1,0:T(8,128)(2,1)S(1)}, u32[]{:S(2)}, u32[]{:S(2)}) collective-permute-start(bf16[256,384]{1,0:T(8,128)(2,1)S(1)} %get-tuple-element.79.a_1_), channel_id=1, source_target_pairs={{0,3},{1,2},{2,1},{3,0},{4,7},{5,6},{6,5},{7,4},{8,11},{9,10},{10,... | collective-permute-start | bytes 589832 | tf_op jit(solution)/shard_map/ppermute | solution.py:432
  8.0 2.2 %collective-permute-start.3 = (bf16[192,256]{1,0:T(8,128)(2,1)S(1)}, bf16[192,256]{1,0:T(8,128)(2,1)S(1)}, u32[]{:S(2)}, u32[]{:S(2)}) collective-permute-start(bf16[192,256]{1,0:T(8,128)(2,1)S(1)} %get-tuple-element.83), channel_id=1, source_target_pairs={{0,20},{1,21},{2,22},{3,23},{4,16},{5,17},{6,18},{7,19},{8,28},{9,... | collective-permute-start | bytes 294920 | tf_op jit(solution)/shard_map/ppermute | solution.py:444
  10.1 0.7 select_reduce_fusion.1
  10.9 1.7 %shard_map.94 = (bf16[256,1024]{1,0:T(8,128)(2,1)S(1)}, f32[256,1]{1,0:T(8,128)S(1)}) custom-call(s32[1,512]{1,0:T(1,128)S(1)} %bitcast.71, f32[1,512]{1,0:T(1,128)S(1)} %bitcast.72, bf16[512,1024]{1,0:T(8,128)(2,1)} %cot.1), custom_call_target="tpu_custom_call" | custom-call | flops 268435456 | bytes 2097152 | tf_op jit(solution)/shard_map/pallas_call | solution.py:71
  13.5 1.9 %collective-permute-start.4 = (bf16[256,384]{1,0:T(8,128)(2,1)S(1)}, bf16[256,384]{1,0:T(8,128)(2,1)S(1)}, u32[]{:S(2)}, u32[]{:S(2)}) collective-permute-start(bf16[256,384]{1,0:T(8,128)(2,1)S(1)} %collective-permute-done.a_3_), channel_id=1, source_target_pairs={{0,4},{1,5},{2,6},{3,7},{4,0},{5,1},{6,2},{7,3},{8,12},{9,13},{10,... | collective-permute-start | bytes 589832 | tf_op jit(solution)/shard_map/ppermute | solution.py:432
  15.5 1.2 %collective-permute-start.6 = (bf16[256,384]{1,0:T(8,128)(2,1)S(1)}, bf16[256,384]{1,0:T(8,128)(2,1)S(1)}, u32[]{:S(2)}, u32[]{:S(2)}) collective-permute-start(bf16[256,384]{1,0:T(8,128)(2,1)S(1)} %get-tuple-element.79.a_1_), channel_id=1, source_target_pairs={{0,2},{1,3},{2,0},{3,1},{4,6},{5,7},{6,4},{7,5},{8,10},{9,11},{10,... | collective-permute-start | bytes 589832 | tf_op jit(solution)/shard_map/ppermute | solution.py:432
  16.8 2.3 %collective-permute-start.7 = (bf16[256,384]{1,0:T(8,128)(2,1)S(1)}, bf16[256,384]{1,0:T(8,128)(2,1)S(1)}, u32[]{:S(2)}, u32[]{:S(2)}) collective-permute-start(bf16[256,384]{1,0:T(8,128)(2,1)S(1)} %collective-permute-done.2.a_2_), channel_id=1, source_target_pairs={{0,2},{1,3},{2,0},{3,1},{4,6},{5,7},{6,4},{7,5},{8,10},{9,11},{10,... | collective-permute-start | bytes 589832 | tf_op jit(solution)/shard_map/ppermute | solution.py:432
  19.1 2.8 %collective-permute-start.8 = (bf16[192,256]{1,0:T(8,128)(2,1)S(1)}, bf16[192,256]{1,0:T(8,128)(2,1)S(1)}, u32[]{:S(2)}, u32[]{:S(2)}) collective-permute-start(bf16[192,256]{1,0:T(8,128)(2,1)S(1)} %get-tuple-element.83), channel_id=1, source_target_pairs={{0,16},{8,24},{16,0},{24,8},{32,48},{40,56},{48,32},{56,40},{64,80... | collective-permute-start | bytes 294920 | tf_op jit(solution)/shard_map/ppermute | solution.py:435
  21.9 5.5 %shard_map.95 = (f32[256,1024]{1,0:T(8,128)S(1)}, f32[256,1024]{1,0:T(8,128)S(1)}, bf16[4,192,256]{2,1,0:T(8,128)(2,1)S(1)}, bf16[3072,1024]{1,0:T(8,128)(2,1)S(1)}, bf16[3072,1024]{1,0:T(8,128)(2,1)S(1)}) custom-call(s32[9]{0:T(128)S(1)} %stack.62.a_0_, bf16[256,384]{1,0:T(8,128)(2,1)S(1)} %get-tuple-element.79.a_1_, ...), custom_call_target="tpu_custom_call" | custom-call | flops 1610612736 | bytes 12582912 | tf_op jit(solution)/shard_map/pallas_call | solution.py:135
  27.4 4.0 %shard_map.96 = (bf16[256,512]{1,0:T(8,128)(2,1)S(1)}, bf16[256,512]{1,0:T(8,128)(2,1)S(1)}, bf16[256,512]{1,0:T(8,128)(2,1)S(1)}, bf16[256,512]{1,0:T(8,128)(2,...) custom-call(s32[4]{0:T(128)S(1)} %pad_add_fusion.info.a_0_, ...), custom_call_target="tpu_custom_call" | custom-call | flops 1610612736 | bytes 4194304 | tf_op jit(solution)/shard_map/pallas_call | solution.py:222
  32.0 0.7 collective-permute-start.15
  32.7 2.5 %collective-permute-start.14 = (bf16[256,512]{1,0:T(8,128)(2,1)S(1)}, bf16[256,512]{1,0:T(8,128)(2,1)S(1)}, u32[]{:S(2)}, u32[]{:S(2)}) collective-permute-start(bf16[256,512]{1,0:T(8,128)(2,1)S(1)} %get-tuple-element.99.refs_0_), channel_id=1, source_target_pairs={{0,16},{8,24},{16,0},{24,8},{32,48},{40,56},{48,32},{56,40},{64,80... | collective-permute-start | bytes 786440 | tf_op jit(solution)/shard_map/ppermute | solution.py:435
  35.8 0.8 collective-permute-start.10
  36.6 1.8 %collective-permute-start.11 = (bf16[2,192,256]{2,1,0:T(8,128)(2,1)S(1)}, bf16[2,192,256]{2,1,0:T(8,128)(2,1)S(1)}, u32[]{:S(2)}, u32[]{:S(2)}) collective-permute-start(bf16[2,192,256]{2,1,0:T(8,128)(2,1)S(1)} %pad_maximum_fusion.refs_5_.a_1_), channel_id=1, source_target_pairs={{0,2},{1,3},{2,0},{3,1},{4,6},{5,7},{6,4},{7,5},{8,10},{9,11},{10,... | collective-permute-start | bytes 589832 | tf_op jit(solution)/shard_map/ppermute | solution.py:432
  38.4 2.2 %collective-permute-start.12 = (bf16[2,192,256]{2,1,0:T(8,128)(2,1)S(1)}, bf16[2,192,256]{2,1,0:T(8,128)(2,1)S(1)}, u32[]{:S(2)}, u32[]{:S(2)}) collective-permute-start(bf16[2,192,256]{2,1,0:T(8,128)(2,1)S(1)} %pad_maximum_fusion.refs_5_.a_1_), channel_id=1, source_target_pairs={{0,3},{1,2},{2,1},{3,0},{4,7},{5,6},{6,5},{7,4},{8,11},{9,10},{10,... | collective-permute-start | bytes 589832 | tf_op jit(solution)/shard_map/ppermute | solution.py:432
  41.2 5.9 %shard_map.97 = (f32[2,384,256]{2,1,0:T(8,128)S(1)}, bf16[2,400,256]{2,1,0:T(8,128)(2,1)S(1)}, bf16[2,400,256]{2,1,0:T(8,128)(2,1)S(1)}, bf16[2,400,256]{2,1,0:T(8,128)(2,1)S(1)}) custom-call(s32[4]{0:T(128)S(1)} %pad_add_fusion.info.a_0_, bf16[256,512]{1,0:T(8,128)(2,1)S(1)} %get-tuple-element.99.refs_0_, bf16[256,512]{1,0:T(8,128)(2,1)S(1)} %get-tuple-element.126.refs_1_, ...), custom_call_target="tpu_custom_call" | custom-call | flops 3221225472 | bytes 12582912 | tf_op jit(solution)/shard_map/pallas_call | solution.py:296
  47.7 2.6 %collective-permute-done.12.a_4_ = bf16[2,192,256]{2,1,0:T(8,128)(2,1)S(1)} collective-permute-done((bf16[2,192,256]{2,1,0:T(8,128)(2,1)S(1)}, bf16[2,192,256]{2,1,0:T(8,128)(2,1)S(1)}, u32[]{:S(2)}, u32[]{:S(2)}) %collective-permute-start.12) | collective-permute-done | bytes 196640 | tf_op jit(solution)/shard_map/ppermute | solution.py:432
  51.0 1.4 %collective-permute-start.22 = (bf16[256,512]{1,0:T(8,128)(2,1)S(1)}, bf16[256,512]{1,0:T(8,128)(2,1)S(1)}, u32[]{:S(2)}, u32[]{:S(2)}) collective-permute-start(bf16[256,512]{1,0:T(8,128)(2,1)S(1)} %get-tuple-element.127.refs_3_), channel_id=1, source_target_pairs={{0,24},{8,16},{16,8},{24,0},{32,56},{40,48},{48,40},{56,32},{64,88... | collective-permute-start | bytes 786440 | tf_op jit(solution)/shard_map/ppermute | solution.py:435
  52.5 2.3 %collective-permute-start.21 = (bf16[256,512]{1,0:T(8,128)(2,1)S(1)}, bf16[256,512]{1,0:T(8,128)(2,1)S(1)}, u32[]{:S(2)}, u32[]{:S(2)}) collective-permute-start(bf16[256,512]{1,0:T(8,128)(2,1)S(1)} %get-tuple-element.126.refs_1_), channel_id=1, source_target_pairs={{0,16},{8,24},{16,0},{24,8},{32,48},{40,56},{48,32},{56,40},{64,80... | collective-permute-start | bytes 786440 | tf_op jit(solution)/shard_map/ppermute | solution.py:435
  56.6 2.0 %collective-permute-start.18 = (bf16[192,512]{1,0:T(8,128)(2,1)S(1)}, bf16[192,512]{1,0:T(8,128)(2,1)S(1)}, u32[]{:S(2)}, u32[]{:S(2)}) collective-permute-start(bf16[192,512]{1,0:T(8,128)(2,1)S(1)} %get-tuple-element.123._.a_2_), channel_id=1, source_target_pairs={{0,32},{8,232},{16,48},{24,248},{32,64},{40,8},{48,80},{56,24},{64... | collective-permute-start | bytes 589832 | tf_op jit(solution)/shard_map/ppermute | solution.py:439
  58.7 4.0 %collective-permute-start.19 = (bf16[192,512]{1,0:T(8,128)(2,1)S(1)}, bf16[192,512]{1,0:T(8,128)(2,1)S(1)}, u32[]{:S(2)}, u32[]{:S(2)}) collective-permute-start(bf16[192,512]{1,0:T(8,128)(2,1)S(1)} %get-tuple-element.125), channel_id=1, source_target_pairs={{0,224},{8,40},{16,240},{24,56},{32,0},{40,72},{48,16},{56,88},{64... | collective-permute-start | bytes 589832 | tf_op jit(solution)/shard_map/ppermute | solution.py:439
  63.9 2.9 %collective-permute-done.21 = bf16[256,512]{1,0:T(8,128)(2,1)S(1)} collective-permute-done((bf16[256,512]{1,0:T(8,128)(2,1)S(1)}, bf16[256,512]{1,0:T(8,128)(2,1)S(1)}, u32[]{:S(2)}, u32[]{:S(2)}) %collective-permute-start.21) | collective-permute-done | bytes 262176 | tf_op jit(solution)/shard_map/ppermute | solution.py:435
  67.5 2.0 %collective-permute-start.26 = (bf16[192,512]{1,0:T(8,128)(2,1)S(1)}, bf16[192,512]{1,0:T(8,128)(2,1)S(1)}, u32[]{:S(2)}, u32[]{:S(2)}) collective-permute-start(bf16[192,512]{1,0:T(8,128)(2,1)S(1)} %get-tuple-element.128.a_4_), channel_id=1, source_target_pairs={{0,32},{8,232},{16,48},{24,248},{32,64},{40,8},{48,80},{56,24},{64... | collective-permute-start | bytes 589832 | tf_op jit(solution)/shard_map/ppermute | solution.py:439
  69.5 4.0 %collective-permute-start.27 = (bf16[192,512]{1,0:T(8,128)(2,1)S(1)}, bf16[192,512]{1,0:T(8,128)(2,1)S(1)}, u32[]{:S(2)}, u32[]{:S(2)}) collective-permute-start(bf16[192,512]{1,0:T(8,128)(2,1)S(1)} %get-tuple-element.132), channel_id=1, source_target_pairs={{0,224},{8,40},{16,240},{24,56},{32,0},{40,72},{48,16},{56,88},{64... | collective-permute-start | bytes 589832 | tf_op jit(solution)/shard_map/ppermute | solution.py:439
  73.7 3.2 %collective-permute-start.25 = (bf16[192,512]{1,0:T(8,128)(2,1)S(1)}, bf16[192,512]{1,0:T(8,128)(2,1)S(1)}, u32[]{:S(2)}, u32[]{:S(2)}) collective-permute-start(bf16[192,512]{1,0:T(8,128)(2,1)S(1)} %get-tuple-element.131), channel_id=1, source_target_pairs={{0,224},{8,40},{16,240},{24,56},{32,0},{40,72},{48,16},{56,88},{64... | collective-permute-start | bytes 589832 | tf_op jit(solution)/shard_map/ppermute | solution.py:439
  77.5 2.2 %collective-permute-start.23 = (bf16[2,400,256]{2,1,0:T(8,128)(2,1)S(1)}, bf16[2,400,256]{2,1,0:T(8,128)(2,1)S(1)}, u32[]{:S(2)}, u32[]{:S(2)}) collective-permute-start(bf16[2,400,256]{2,1,0:T(8,128)(2,1)S(1)} %shard_map.104), channel_id=1, source_target_pairs={{0,3},{1,2},{2,1},{3,0},{4,7},{5,6},{6,5},{7,4},{8,11},{9,10},{10,... | collective-permute-start | bytes 1228808 | tf_op jit(solution)/shard_map/ppermute | solution.py:432
  79.8 2.9 %collective-permute-done.24.a_2_ = bf16[192,512]{1,0:T(8,128)(2,1)S(1)} collective-permute-done((bf16[192,512]{1,0:T(8,128)(2,1)S(1)}, bf16[192,512]{1,0:T(8,128)(2,1)S(1)}, u32[]{:S(2)}, u32[]{:S(2)}) %collective-permute-start.24) | collective-permute-done | bytes 196640 | tf_op jit(solution)/shard_map/ppermute | solution.py:439
  82.7 0.7 shard_map.106
  83.4 0.8 shard_map.107
  84.7 3.2 %collective-permute-start.32 = (bf16[192,512]{1,0:T(8,128)(2,1)S(1)}, bf16[192,512]{1,0:T(8,128)(2,1)S(1)}, u32[]{:S(2)}, u32[]{:S(2)}) collective-permute-start(bf16[192,512]{1,0:T(8,128)(2,1)S(1)} %get-tuple-element.137), channel_id=1, source_target_pairs={{0,224},{8,40},{16,240},{24,56},{32,0},{40,72},{48,16},{56,88},{64... | collective-permute-start | bytes 589832 | tf_op jit(solution)/shard_map/ppermute | solution.py:439
  88.4 5.2 %collective-permute-done.31.a_2_ = bf16[192,512]{1,0:T(8,128)(2,1)S(1)} collective-permute-done((bf16[192,512]{1,0:T(8,128)(2,1)S(1)}, bf16[192,512]{1,0:T(8,128)(2,1)S(1)}, u32[]{:S(2)}, u32[]{:S(2)}) %collective-permute-start.31) | collective-permute-done | bytes 196640 | tf_op jit(solution)/shard_map/ppermute | solution.py:439
  93.6 0.7 shard_map.109
  94.4 7.3 %collective-permute-start.36 = (bf16[192,512]{1,0:T(8,128)(2,1)}, bf16[192,512]{1,0:T(8,128)(2,1)}, u32[]{:S(2)}, u32[]{:S(2)}) collective-permute-start(bf16[192,512]{1,0:T(8,128)(2,1)} %get-tuple-element.140), channel_id=1, source_target_pairs={{0,224},{8,40},{16,240},{24,56},{32,0},{40,72},{48,16},{56,88},{64... | collective-permute-start | bytes 589832 | tf_op jit(solution)/shard_map/ppermute | solution.py:439
  101.8 0.7 shard_map.110.a_2_
  102.5 2.0 %collective-permute-start.33 = (bf16[192,512]{1,0:T(8,128)(2,1)}, bf16[192,512]{1,0:T(8,128)(2,1)}, u32[]{:S(2)}, u32[]{:S(2)}) collective-permute-start(bf16[192,512]{1,0:T(8,128)(2,1)} %shard_map.110.a_2_), channel_id=1, source_target_pairs={{0,32},{8,232},{16,48},{24,248},{32,64},{40,8},{48,80},{56,24},{64... | collective-permute-start | bytes 589832 | tf_op jit(solution)/shard_map/ppermute | solution.py:439
  104.5 1.0 copy-done.2
  105.5 1.1 copy-done.4
  107.3 1.3 %shard_map.108 = (f32[384,256]{1,0:T(8,128)S(1)}, f32[1,256]{1,0:T(1,128)S(1)}, bf16[400,256]{1,0:T(8,128)(2,1)S(1)}) custom-call(f32[2,384,256]{2,1,0:T(8,128)S(1)} %copy-done.4, f32[1,256]{1,0:T(1,128)S(1)} %copy-done.9, bf16[2,400,256]{2,1,0:T(8,128)(2,1)S(1)} %collective-permute-done.17.a_5_.first, bf16[2,400,256]{2,1,0:T(8,128)(2,1)S(1)} %copy-done.2, ...), custom_call_target="tpu_custom_call" | custom-call | flops 786432 | bytes 2949120 | tf_op jit(solution)/shard_map/pallas_call | solution.py:347
  108.6 1.0 shard_map.111
  109.5 3.3 %collective-permute-start.37 = (bf16[192,512]{1,0:T(8,128)(2,1)S(1)}, bf16[192,512]{1,0:T(8,128)(2,1)S(1)}, u32[]{:S(2)}, u32[]{:S(2)}) collective-permute-start(bf16[192,512]{1,0:T(8,128)(2,1)S(1)} %shard_map.111), channel_id=1, source_target_pairs={{0,224},{8,40},{16,240},{24,56},{32,0},{40,72},{48,16},{56,88},{64... | collective-permute-start | bytes 589832 | tf_op jit(solution)/shard_map/ppermute | solution.py:439
  112.8 1.2 fusion.6
  114.1 1.3 %collective-permute-start.29 = (bf16[400,256]{1,0:T(8,128)(2,1)S(1)}, bf16[400,256]{1,0:T(8,128)(2,1)S(1)}, u32[]{:S(2)}, u32[]{:S(2)}) collective-permute-start(bf16[400,256]{1,0:T(8,128)(2,1)S(1)} %get-tuple-element.136.a_3_), channel_id=1, source_target_pairs={{0,4},{1,5},{2,6},{3,7},{4,0},{5,1},{6,2},{7,3},{8,12},{9,13},{10,... | collective-permute-start | bytes 614408 | tf_op jit(solution)/shard_map/ppermute | solution.py:432
  116.2 3.7 %collective-permute-done.29 = bf16[400,256]{1,0:T(8,128)(2,1)S(1)} collective-permute-done((bf16[400,256]{1,0:T(8,128)(2,1)S(1)}, bf16[400,256]{1,0:T(8,128)(2,1)S(1)}, u32[]{:S(2)}, u32[]{:S(2)}) %collective-permute-start.29) | collective-permute-done | bytes 204832 | tf_op jit(solution)/shard_map/ppermute | solution.py:432
  119.9 0.7 select_reduce_fusion
  120.7 1.1 convolution_convert_fusion
  121.8 0.8 broadcast_select_fusion
  (94 shorter events, 13.0 us)
Async XLA Ops:
  1.6 25.8 %copy-start.6 = (s32[512]{0:T(512)}, s32[512]{0:T(512)S(1)}, u32[]{:S(2)}) copy-start(s32[512]{0:T(512)S(1)} %convert_select_fusion) | copy-start | bytes 6148
  3.6 9.1 %collective-permute-start = (bf16[256,384]{1,0:T(8,128)(2,1)S(1)}, bf16[256,384]{1,0:T(8,128)(2,1)S(1)}, u32[]{:S(2)}, u32[]{:S(2)}) collective-permute-start(bf16[256,384]{1,0:T(8,128)(2,1)S(1)} %get-tuple-element.79.a_1_), channel_id=1, source_target_pairs={{0,1},{1,0},{2,3},{3,2},{4,5},{5,4},{6,7},{7,6},{8,9},{9,8},{10,11... | collective-permute-start | bytes 589832 | tf_op jit(solution)/shard_map/ppermute | solution.py:432
  5.3 7.6 %collective-permute-start.1 = (bf16[256,384]{1,0:T(8,128)(2,1)S(1)}, bf16[256,384]{1,0:T(8,128)(2,1)S(1)}, u32[]{:S(2)}, u32[]{:S(2)}) collective-permute-start(bf16[256,384]{1,0:T(8,128)(2,1)S(1)} %get-tuple-element.79.a_1_), channel_id=1, source_target_pairs={{0,3},{1,2},{2,1},{3,0},{4,7},{5,6},{6,5},{7,4},{8,11},{9,10},{10,... | collective-permute-start | bytes 589832 | tf_op jit(solution)/shard_map/ppermute | solution.py:432
  7.4 6.1 %collective-permute-start.2 = (bf16[256,384]{1,0:T(8,128)(2,1)S(1)}, bf16[256,384]{1,0:T(8,128)(2,1)S(1)}, u32[]{:S(2)}, u32[]{:S(2)}) collective-permute-start(bf16[256,384]{1,0:T(8,128)(2,1)S(1)} %get-tuple-element.79.a_1_), channel_id=1, source_target_pairs={{0,4},{1,5},{2,6},{3,7},{4,0},{5,1},{6,2},{7,3},{8,12},{9,13},{10,... | collective-permute-start | bytes 589832 | tf_op jit(solution)/shard_map/ppermute | solution.py:432
  8.0 4.7 %collective-permute-start.3 = (bf16[192,256]{1,0:T(8,128)(2,1)S(1)}, bf16[192,256]{1,0:T(8,128)(2,1)S(1)}, u32[]{:S(2)}, u32[]{:S(2)}) collective-permute-start(bf16[192,256]{1,0:T(8,128)(2,1)S(1)} %get-tuple-element.83), channel_id=1, source_target_pairs={{0,20},{1,21},{2,22},{3,23},{4,16},{5,17},{6,18},{7,19},{8,28},{9,... | collective-permute-start | bytes 294920 | tf_op jit(solution)/shard_map/ppermute | solution.py:444
  13.5 13.9 %collective-permute-start.4 = (bf16[256,384]{1,0:T(8,128)(2,1)S(1)}, bf16[256,384]{1,0:T(8,128)(2,1)S(1)}, u32[]{:S(2)}, u32[]{:S(2)}) collective-permute-start(bf16[256,384]{1,0:T(8,128)(2,1)S(1)} %collective-permute-done.a_3_), channel_id=1, source_target_pairs={{0,4},{1,5},{2,6},{3,7},{4,0},{5,1},{6,2},{7,3},{8,12},{9,13},{10,... | collective-permute-start | bytes 589832 | tf_op jit(solution)/shard_map/ppermute | solution.py:432
  15.4 12.0 %collective-permute-start.5 = (bf16[256,384]{1,0:T(8,128)(2,1)S(1)}, bf16[256,384]{1,0:T(8,128)(2,1)S(1)}, u32[]{:S(2)}, u32[]{:S(2)}) collective-permute-start(bf16[256,384]{1,0:T(8,128)(2,1)S(1)} %collective-permute-done.1.a_4_), channel_id=1, source_target_pairs={{0,4},{1,5},{2,6},{3,7},{4,0},{5,1},{6,2},{7,3},{8,12},{9,13},{10,... | collective-permute-start | bytes 589832 | tf_op jit(solution)/shard_map/ppermute | solution.py:432
  15.5 11.9 %collective-permute-start.6 = (bf16[256,384]{1,0:T(8,128)(2,1)S(1)}, bf16[256,384]{1,0:T(8,128)(2,1)S(1)}, u32[]{:S(2)}, u32[]{:S(2)}) collective-permute-start(bf16[256,384]{1,0:T(8,128)(2,1)S(1)} %get-tuple-element.79.a_1_), channel_id=1, source_target_pairs={{0,2},{1,3},{2,0},{3,1},{4,6},{5,7},{6,4},{7,5},{8,10},{9,11},{10,... | collective-permute-start | bytes 589832 | tf_op jit(solution)/shard_map/ppermute | solution.py:432
  16.8 10.6 %collective-permute-start.7 = (bf16[256,384]{1,0:T(8,128)(2,1)S(1)}, bf16[256,384]{1,0:T(8,128)(2,1)S(1)}, u32[]{:S(2)}, u32[]{:S(2)}) collective-permute-start(bf16[256,384]{1,0:T(8,128)(2,1)S(1)} %collective-permute-done.2.a_2_), channel_id=1, source_target_pairs={{0,2},{1,3},{2,0},{3,1},{4,6},{5,7},{6,4},{7,5},{8,10},{9,11},{10,... | collective-permute-start | bytes 589832 | tf_op jit(solution)/shard_map/ppermute | solution.py:432
  19.1 8.3 %collective-permute-start.8 = (bf16[192,256]{1,0:T(8,128)(2,1)S(1)}, bf16[192,256]{1,0:T(8,128)(2,1)S(1)}, u32[]{:S(2)}, u32[]{:S(2)}) collective-permute-start(bf16[192,256]{1,0:T(8,128)(2,1)S(1)} %get-tuple-element.83), channel_id=1, source_target_pairs={{0,16},{8,24},{16,0},{24,8},{32,48},{40,56},{48,32},{56,40},{64,80... | collective-permute-start | bytes 294920 | tf_op jit(solution)/shard_map/ppermute | solution.py:435
  31.4 9.8 %copy-start.8 = (f32[1,256]{1,0:T(1,128)}, f32[1,256]{1,0:T(1,128)S(1)}, u32[]{:S(2)}) copy-start(f32[1,256]{1,0:T(1,128)S(1)} %get-tuple-element.103.refs_4_.route) | copy-start | bytes 3076
  31.4 4.4 %collective-permute-start.9 = (bf16[8,192,256]{2,1,0:T(8,128)(2,1)S(1)}, bf16[8,192,256]{2,1,0:T(8,128)(2,1)S(1)}, u32[]{:S(2)}, u32[]{:S(2)}) collective-permute-start(bf16[8,192,256]{2,1,0:T(8,128)(2,1)S(1)} %get-tuple-element.97), channel_id=1, source_target_pairs={{0,8},{8,0},{16,24},{24,16},{32,40},{40,32},{48,56},{56,48},{64,72... | collective-permute-start | bytes 2359304 | tf_op jit(solution)/shard_map/ppermute | solution.py:435
  31.5 6.9 %collective-permute-start.13 = (bf16[256,512]{1,0:T(8,128)(2,1)S(1)}, bf16[256,512]{1,0:T(8,128)(2,1)S(1)}, u32[]{:S(2)}, u32[]{:S(2)}) collective-permute-start(bf16[256,512]{1,0:T(8,128)(2,1)S(1)} %get-tuple-element.101.refs_2_), channel_id=1, source_target_pairs={{0,8},{8,0},{16,24},{24,16},{32,40},{40,32},{48,56},{56,48},{64,72... | collective-permute-start | bytes 786440 | tf_op jit(solution)/shard_map/ppermute | solution.py:435
  32.0 19.0 %collective-permute-start.15 = (bf16[256,512]{1,0:T(8,128)(2,1)S(1)}, bf16[256,512]{1,0:T(8,128)(2,1)S(1)}, u32[]{:S(2)}, u32[]{:S(2)}) collective-permute-start(bf16[256,512]{1,0:T(8,128)(2,1)S(1)} %get-tuple-element.101.refs_2_), channel_id=1, source_target_pairs={{0,24},{8,16},{16,8},{24,0},{32,56},{40,48},{48,40},{56,32},{64,88... | collective-permute-start | bytes 786440 | tf_op jit(solution)/shard_map/ppermute | solution.py:435
  32.7 18.3 %collective-permute-start.14 = (bf16[256,512]{1,0:T(8,128)(2,1)S(1)}, bf16[256,512]{1,0:T(8,128)(2,1)S(1)}, u32[]{:S(2)}, u32[]{:S(2)}) collective-permute-start(bf16[256,512]{1,0:T(8,128)(2,1)S(1)} %get-tuple-element.99.refs_0_), channel_id=1, source_target_pairs={{0,16},{8,24},{16,0},{24,8},{32,48},{40,56},{48,32},{56,40},{64,80... | collective-permute-start | bytes 786440 | tf_op jit(solution)/shard_map/ppermute | solution.py:435
  35.8 11.3 %collective-permute-start.10 = (bf16[2,192,256]{2,1,0:T(8,128)(2,1)S(1)}, bf16[2,192,256]{2,1,0:T(8,128)(2,1)S(1)}, u32[]{:S(2)}, u32[]{:S(2)}) collective-permute-start(bf16[2,192,256]{2,1,0:T(8,128)(2,1)S(1)} %pad_maximum_fusion.refs_5_.a_1_), channel_id=1, source_target_pairs={{0,1},{1,0},{2,3},{3,2},{4,5},{5,4},{6,7},{7,6},{8,9},{9,8},{10,11... | collective-permute-start | bytes 589832 | tf_op jit(solution)/shard_map/ppermute | solution.py:432
  36.6 11.1 %collective-permute-start.11 = (bf16[2,192,256]{2,1,0:T(8,128)(2,1)S(1)}, bf16[2,192,256]{2,1,0:T(8,128)(2,1)S(1)}, u32[]{:S(2)}, u32[]{:S(2)}) collective-permute-start(bf16[2,192,256]{2,1,0:T(8,128)(2,1)S(1)} %pad_maximum_fusion.refs_5_.a_1_), channel_id=1, source_target_pairs={{0,2},{1,3},{2,0},{3,1},{4,6},{5,7},{6,4},{7,5},{8,10},{9,11},{10,... | collective-permute-start | bytes 589832 | tf_op jit(solution)/shard_map/ppermute | solution.py:432
  38.4 11.8 %collective-permute-start.12 = (bf16[2,192,256]{2,1,0:T(8,128)(2,1)S(1)}, bf16[2,192,256]{2,1,0:T(8,128)(2,1)S(1)}, u32[]{:S(2)}, u32[]{:S(2)}) collective-permute-start(bf16[2,192,256]{2,1,0:T(8,128)(2,1)S(1)} %pad_maximum_fusion.refs_5_.a_1_), channel_id=1, source_target_pairs={{0,3},{1,2},{2,1},{3,0},{4,7},{5,6},{6,5},{7,4},{8,11},{9,10},{10,... | collective-permute-start | bytes 589832 | tf_op jit(solution)/shard_map/ppermute | solution.py:432
  47.1 8.8 %copy-start.3 = (f32[2,384,256]{2,1,0:T(8,128)}, f32[2,384,256]{2,1,0:T(8,128)S(1)}, u32[]{:S(2)}) copy-start(f32[2,384,256]{2,1,0:T(8,128)S(1)} %get-tuple-element.110.own) | copy-start | bytes 2359300
  50.9 5.0 %collective-permute-start.16 = (bf16[8,192,256]{2,1,0:T(8,128)(2,1)S(1)}, bf16[8,192,256]{2,1,0:T(8,128)(2,1)S(1)}, u32[]{:S(2)}, u32[]{:S(2)}) collective-permute-start(bf16[8,192,256]{2,1,0:T(8,128)(2,1)S(1)} %get-tuple-element.121), channel_id=1, source_target_pairs={{0,8},{8,0},{16,24},{24,16},{32,40},{40,32},{48,56},{56,48},{64,72... | collective-permute-start | bytes 2359304 | tf_op jit(solution)/shard_map/ppermute | solution.py:435
  51.0 12.3 %collective-permute-start.22 = (bf16[256,512]{1,0:T(8,128)(2,1)S(1)}, bf16[256,512]{1,0:T(8,128)(2,1)S(1)}, u32[]{:S(2)}, u32[]{:S(2)}) collective-permute-start(bf16[256,512]{1,0:T(8,128)(2,1)S(1)} %get-tuple-element.127.refs_3_), channel_id=1, source_target_pairs={{0,24},{8,16},{16,8},{24,0},{32,56},{40,48},{48,40},{56,32},{64,88... | collective-permute-start | bytes 786440 | tf_op jit(solution)/shard_map/ppermute | solution.py:435
  52.4 2.9 %collective-permute-start.20 = (bf16[256,512]{1,0:T(8,128)(2,1)S(1)}, bf16[256,512]{1,0:T(8,128)(2,1)S(1)}, u32[]{:S(2)}, u32[]{:S(2)}) collective-permute-start(bf16[256,512]{1,0:T(8,128)(2,1)S(1)} %get-tuple-element.127.refs_3_), channel_id=1, source_target_pairs={{0,8},{8,0},{16,24},{24,16},{32,40},{40,32},{48,56},{56,48},{64,72... | collective-permute-start | bytes 786440 | tf_op jit(solution)/shard_map/ppermute | solution.py:435
  52.5 14.3 %collective-permute-start.21 = (bf16[256,512]{1,0:T(8,128)(2,1)S(1)}, bf16[256,512]{1,0:T(8,128)(2,1)S(1)}, u32[]{:S(2)}, u32[]{:S(2)}) collective-permute-start(bf16[256,512]{1,0:T(8,128)(2,1)S(1)} %get-tuple-element.126.refs_1_), channel_id=1, source_target_pairs={{0,16},{8,24},{16,0},{24,8},{32,48},{40,56},{48,32},{56,40},{64,80... | collective-permute-start | bytes 786440 | tf_op jit(solution)/shard_map/ppermute | solution.py:435
  56.5 45.3 %copy-start = (f32[1536,512]{1,0:T(8,128)}, f32[1536,512]{1,0:T(8,128)S(1)}, u32[]{:S(2)}) copy-start(f32[1536,512]{1,0:T(8,128)S(1)} %add_add_fusion) | copy-start | bytes 9437188
  56.6 16.9 %collective-permute-start.18 = (bf16[192,512]{1,0:T(8,128)(2,1)S(1)}, bf16[192,512]{1,0:T(8,128)(2,1)S(1)}, u32[]{:S(2)}, u32[]{:S(2)}) collective-permute-start(bf16[192,512]{1,0:T(8,128)(2,1)S(1)} %get-tuple-element.123._.a_2_), channel_id=1, source_target_pairs={{0,32},{8,232},{16,48},{24,248},{32,64},{40,8},{48,80},{56,24},{64... | collective-permute-start | bytes 589832 | tf_op jit(solution)/shard_map/ppermute | solution.py:439
  58.6 21.1 %collective-permute-start.17 = (bf16[2,400,256]{2,1,0:T(8,128)(2,1)S(1)}, bf16[2,400,256]{2,1,0:T(8,128)(2,1)S(1)}, u32[]{:S(2)}, u32[]{:S(2)}) collective-permute-start(bf16[2,400,256]{2,1,0:T(8,128)(2,1)S(1)} %shard_map.100), channel_id=1, source_target_pairs={{0,1},{1,0},{2,3},{3,2},{4,5},{5,4},{6,7},{7,6},{8,9},{9,8},{10,11... | collective-permute-start | bytes 1228808 | tf_op jit(solution)/shard_map/ppermute | solution.py:432
  58.7 14.7 %collective-permute-start.19 = (bf16[192,512]{1,0:T(8,128)(2,1)S(1)}, bf16[192,512]{1,0:T(8,128)(2,1)S(1)}, u32[]{:S(2)}, u32[]{:S(2)}) collective-permute-start(bf16[192,512]{1,0:T(8,128)(2,1)S(1)} %get-tuple-element.125), channel_id=1, source_target_pairs={{0,224},{8,40},{16,240},{24,56},{32,0},{40,72},{48,16},{56,88},{64... | collective-permute-start | bytes 589832 | tf_op jit(solution)/shard_map/ppermute | solution.py:439
  67.5 10.1 %collective-permute-start.26 = (bf16[192,512]{1,0:T(8,128)(2,1)S(1)}, bf16[192,512]{1,0:T(8,128)(2,1)S(1)}, u32[]{:S(2)}, u32[]{:S(2)}) collective-permute-start(bf16[192,512]{1,0:T(8,128)(2,1)S(1)} %get-tuple-element.128.a_4_), channel_id=1, source_target_pairs={{0,32},{8,232},{16,48},{24,248},{32,64},{40,8},{48,80},{56,24},{64... | collective-permute-start | bytes 589832 | tf_op jit(solution)/shard_map/ppermute | solution.py:439
  69.5 10.3 %collective-permute-start.27 = (bf16[192,512]{1,0:T(8,128)(2,1)S(1)}, bf16[192,512]{1,0:T(8,128)(2,1)S(1)}, u32[]{:S(2)}, u32[]{:S(2)}) collective-permute-start(bf16[192,512]{1,0:T(8,128)(2,1)S(1)} %get-tuple-element.132), channel_id=1, source_target_pairs={{0,224},{8,40},{16,240},{24,56},{32,0},{40,72},{48,16},{56,88},{64... | collective-permute-start | bytes 589832 | tf_op jit(solution)/shard_map/ppermute | solution.py:439
  73.6 9.1 %collective-permute-start.24 = (bf16[192,512]{1,0:T(8,128)(2,1)S(1)}, bf16[192,512]{1,0:T(8,128)(2,1)S(1)}, u32[]{:S(2)}, u32[]{:S(2)}) collective-permute-start(bf16[192,512]{1,0:T(8,128)(2,1)S(1)} %get-tuple-element.129._.a_4_), channel_id=1, source_target_pairs={{0,32},{8,232},{16,48},{24,248},{32,64},{40,8},{48,80},{56,24},{64... | collective-permute-start | bytes 589832 | tf_op jit(solution)/shard_map/ppermute | solution.py:439
  73.7 9.0 %collective-permute-start.25 = (bf16[192,512]{1,0:T(8,128)(2,1)S(1)}, bf16[192,512]{1,0:T(8,128)(2,1)S(1)}, u32[]{:S(2)}, u32[]{:S(2)}) collective-permute-start(bf16[192,512]{1,0:T(8,128)(2,1)S(1)} %get-tuple-element.131), channel_id=1, source_target_pairs={{0,224},{8,40},{16,240},{24,56},{32,0},{40,72},{48,16},{56,88},{64... | collective-permute-start | bytes 589832 | tf_op jit(solution)/shard_map/ppermute | solution.py:439
  77.5 10.9 %collective-permute-start.23 = (bf16[2,400,256]{2,1,0:T(8,128)(2,1)S(1)}, bf16[2,400,256]{2,1,0:T(8,128)(2,1)S(1)}, u32[]{:S(2)}, u32[]{:S(2)}) collective-permute-start(bf16[2,400,256]{2,1,0:T(8,128)(2,1)S(1)} %shard_map.104), channel_id=1, source_target_pairs={{0,3},{1,2},{2,1},{3,0},{4,7},{5,6},{6,5},{7,4},{8,11},{9,10},{10,... | collective-permute-start | bytes 1228808 | tf_op jit(solution)/shard_map/ppermute | solution.py:432
  84.2 20.3 %collective-permute-start.28 = (bf16[2,400,256]{2,1,0:T(8,128)(2,1)}, bf16[2,400,256]{2,1,0:T(8,128)(2,1)}, u32[]{:S(2)}, u32[]{:S(2)}) collective-permute-start(bf16[2,400,256]{2,1,0:T(8,128)(2,1)} %shard_map.107), channel_id=1, source_target_pairs={{0,2},{1,3},{2,0},{3,1},{4,6},{5,7},{6,4},{7,5},{8,10},{9,11},{10,... | collective-permute-start | bytes 1228808 | tf_op jit(solution)/shard_map/ppermute | solution.py:432
  84.7 8.9 %collective-permute-start.31 = (bf16[192,512]{1,0:T(8,128)(2,1)S(1)}, bf16[192,512]{1,0:T(8,128)(2,1)S(1)}, u32[]{:S(2)}, u32[]{:S(2)}) collective-permute-start(bf16[192,512]{1,0:T(8,128)(2,1)S(1)} %get-tuple-element.133.a_4_), channel_id=1, source_target_pairs={{0,32},{8,232},{16,48},{24,248},{32,64},{40,8},{48,80},{56,24},{64... | collective-permute-start | bytes 589832 | tf_op jit(solution)/shard_map/ppermute | solution.py:439
  84.7 8.9 %collective-permute-start.32 = (bf16[192,512]{1,0:T(8,128)(2,1)S(1)}, bf16[192,512]{1,0:T(8,128)(2,1)S(1)}, u32[]{:S(2)}, u32[]{:S(2)}) collective-permute-start(bf16[192,512]{1,0:T(8,128)(2,1)S(1)} %get-tuple-element.137), channel_id=1, source_target_pairs={{0,224},{8,40},{16,240},{24,56},{32,0},{40,72},{48,16},{56,88},{64... | collective-permute-start | bytes 589832 | tf_op jit(solution)/shard_map/ppermute | solution.py:439
  87.9 13.8 %collective-permute-start.30 = (bf16[192,512]{1,0:T(8,128)(2,1)S(1)}, bf16[192,512]{1,0:T(8,128)(2,1)S(1)}, u32[]{:S(2)}, u32[]{:S(2)}) collective-permute-start(bf16[192,512]{1,0:T(8,128)(2,1)S(1)} %get-tuple-element.134._.a_4_), channel_id=1, source_target_pairs={{0,32},{8,232},{16,48},{24,248},{32,64},{40,8},{48,80},{56,24},{64... | collective-permute-start | bytes 589832 | tf_op jit(solution)/shard_map/ppermute | solution.py:439
  88.4 6.0 %copy-start.1 = (bf16[2,400,256]{2,1,0:T(8,128)(2,1)}, bf16[2,400,256]{2,1,0:T(8,128)(2,1)S(1)}, u32[]{:S(2)}) copy-start(bf16[2,400,256]{2,1,0:T(8,128)(2,1)S(1)} %collective-permute-done.23.third.a_5_) | copy-start | bytes 1228804
  94.4 8.1 %copy-start.5 = (bf16[192,512]{1,0:T(8,128)(2,1)}, bf16[192,512]{1,0:T(8,128)(2,1)S(1)}, u32[]{:S(2)}) copy-start(bf16[192,512]{1,0:T(8,128)(2,1)S(1)} %get-tuple-element.138.a_2_) | copy-start | bytes 589828
  94.4 14.2 %collective-permute-start.36 = (bf16[192,512]{1,0:T(8,128)(2,1)}, bf16[192,512]{1,0:T(8,128)(2,1)}, u32[]{:S(2)}, u32[]{:S(2)}) collective-permute-start(bf16[192,512]{1,0:T(8,128)(2,1)} %get-tuple-element.140), channel_id=1, source_target_pairs={{0,224},{8,40},{16,240},{24,56},{32,0},{40,72},{48,16},{56,88},{64... | collective-permute-start | bytes 589832 | tf_op jit(solution)/shard_map/ppermute | solution.py:439
  101.7 11.1 %collective-permute-start.34 = (bf16[192,512]{1,0:T(8,128)(2,1)}, bf16[192,512]{1,0:T(8,128)(2,1)}, u32[]{:S(2)}, u32[]{:S(2)}) collective-permute-start(bf16[192,512]{1,0:T(8,128)(2,1)} %get-tuple-element.139), channel_id=1, source_target_pairs={{0,224},{8,40},{16,240},{24,56},{32,0},{40,72},{48,16},{56,88},{64... | collective-permute-start | bytes 589832 | tf_op jit(solution)/shard_map/ppermute | solution.py:439
  102.5 10.3 %collective-permute-start.33 = (bf16[192,512]{1,0:T(8,128)(2,1)}, bf16[192,512]{1,0:T(8,128)(2,1)}, u32[]{:S(2)}, u32[]{:S(2)}) collective-permute-start(bf16[192,512]{1,0:T(8,128)(2,1)} %shard_map.110.a_2_), channel_id=1, source_target_pairs={{0,32},{8,232},{16,48},{24,248},{32,64},{40,8},{48,80},{56,24},{64... | collective-permute-start | bytes 589832 | tf_op jit(solution)/shard_map/ppermute | solution.py:439
  104.5 10.9 %collective-permute-start.35 = (bf16[192,512]{1,0:T(8,128)(2,1)}, bf16[192,512]{1,0:T(8,128)(2,1)S(1)}, u32[]{:S(2)}, u32[]{:S(2)}) collective-permute-start(bf16[192,512]{1,0:T(8,128)(2,1)} %copy-done.5), channel_id=1, source_target_pairs={{0,32},{8,232},{16,48},{24,248},{32,64},{40,8},{48,80},{56,24},{64... | collective-permute-start | bytes 589832 | tf_op jit(solution)/shard_map/ppermute | solution.py:439
  104.5 1.0 copy-start.2
  105.5 1.1 copy-start.4
  108.6 11.4 %copy-start.7 = (s32[512]{0:T(512)S(1)}, s32[512]{0:T(512)}, u32[]{:S(2)}) copy-start(s32[512]{0:T(512)} %copy-done.6) | copy-start | bytes 6148
  109.5 6.5 %collective-permute-start.37 = (bf16[192,512]{1,0:T(8,128)(2,1)S(1)}, bf16[192,512]{1,0:T(8,128)(2,1)S(1)}, u32[]{:S(2)}, u32[]{:S(2)}) collective-permute-start(bf16[192,512]{1,0:T(8,128)(2,1)S(1)} %shard_map.111), channel_id=1, source_target_pairs={{0,224},{8,40},{16,240},{24,56},{32,0},{40,72},{48,16},{56,88},{64... | collective-permute-start | bytes 589832 | tf_op jit(solution)/shard_map/ppermute | solution.py:439
  114.1 5.8 %collective-permute-start.29 = (bf16[400,256]{1,0:T(8,128)(2,1)S(1)}, bf16[400,256]{1,0:T(8,128)(2,1)S(1)}, u32[]{:S(2)}, u32[]{:S(2)}) collective-permute-start(bf16[400,256]{1,0:T(8,128)(2,1)S(1)} %get-tuple-element.136.a_3_), channel_id=1, source_target_pairs={{0,4},{1,5},{2,6},{3,7},{4,0},{5,1},{6,2},{7,3},{8,12},{9,13},{10,... | collective-permute-start | bytes 614408 | tf_op jit(solution)/shard_map/ppermute | solution.py:432
  116.1 5.6 %collective-permute-start.38 = (bf16[96,1024]{1,0:T(8,128)(2,1)S(1)}, bf16[96,1024]{1,0:T(8,128)(2,1)S(1)}, u32[]{:S(2)}, u32[]{:S(2)}) collective-permute-start(bf16[96,1024]{1,0:T(8,128)(2,1)S(1)} %fusion.10), channel_id=1, source_target_pairs={{0,8},{8,0},{16,24},{24,16},{32,40},{40,32},{48,56},{56,48},{64,72... | collective-permute-start | bytes 589832 | tf_op jit(solution)/shard_map/ppermute | solution.py:435
  (1 other events, 0.7 us)

commit v3 on v2

--- a/solution.py
+++ b/solution.py
@@ -488,18 +488,18 @@
         return [mine[c], over_dp(other[c], 1), over_dp(mine[c], 2), over_dp(other[c], 3)]
 
     cots = [to_partners(0)]
+    far = [far_pair] + [over_tensor(far_pair, k) for k in (1, 2, 3)]
+    far_left, far_send = far_operand(info, far, n_tensor, n_z)
+    far_send, near_send = tie((far_send, near_send))
+    far_sib = over_dp(far_send, 1)
     near_sib = over_dp(near_send, 1)
-    far_pair, near_sib = tie((far_pair, near_sib))
-    far = [far_pair] + [over_tensor(far_pair, k) for k in (1, 2, 3)]
-    own_part, *sent = token_parts(info, mine, other, route_part, far_pair, weights, piece)
+    own_part, *sent = token_parts(info, mine, other, route_part, far_left, weights, piece)
 
     def product(a, b):
         return jnp.dot(a.reshape(n_z * half, CAP), b, preferred_element_type=F32)
 
     close = product(near_left, cots[0][0]) + product(near_sib, cots[0][1])
-    far, own_part, sent, mine, other, close = tie((far, own_part, sent, mine, other, close))
-    far_left, far_send = far_operand(info, far, n_tensor, n_z)
-    far_sib = over_dp(far_send, 1)
+    own_part, sent, mine, other, close = tie((own_part, sent, mine, other, close))
     for c in range(1, CHUNKS):
         mine, other, cots[-1] = tie((mine, other, cots[-1]))
         cots.append(to_partners(c))
@@ -550,7 +550,10 @@
             sums[4 - i] = over_tensor(after(sent[i], waited), 4 - i)
         else:
             parts = [sums[1], sums[3], sums[2]]
-            total, route_total, message = combine(own_part, route_part, parts)
+            in_hbm = lambda a: pltpu.with_memory_space_constraint(a, pltpu.HBM)
+            total, route_total, message = combine(
+                in_hbm(own_part), in_hbm(route_part), [in_hbm(a) for a in parts]
+            )
         for ring in rings[1:]:
             waited = ring.hop(i, [waited, message if i == 3 else sums[(1, 3)[i - 1]]])
     whole_rows = jnp.concatenate([ring.finish() for ring in rings], axis=2)

time: 123 us -> 124 us (level); the launches traced: 123 us -> 121 us
  waiting for transfers between devices: 20.5 us -> 28.7 us
  starting transfers between devices: 62.7 us -> 55.8 us
  local copies, waits for them, and re-layouts: 2.92 us -> 0.4 us
    ppermute x14, starting transfers between devices: 31.2 us -> 22.5 us  [along_z(): return lax.ppermute(x, 'dp', pairs)]
    ppermute x10, waiting for transfers between devices: 2.93 us -> 10.6 us  [over_dp(): return lax.ppermute(x, 'dp', [(i, i ^ k) for i in range(n_dp)])]
    ppermute x14, waiting for transfers between devices: 9.42 us -> 15.2 us  [along_z(): return lax.ppermute(x, 'dp', pairs)]
    ppermute x14, waiting for transfers between devices: 8.06 us -> 2.76 us  [over_tensor(): return lax.ppermute(x, 'tensor', [(i, i ^ k) for i in range(n_tensor)])]
    unnamed x20 -> x14, local copies, waits for them, and re-layouts: 2.83 us -> 0.3 us
    ppermute x14, starting transfers between devices: 18.8 us -> 20.7 us  [over_tensor(): return lax.ppermute(x, 'tensor', [(i, i ^ k) for i in range(n_tensor)])]
  transfers between devices with their start and end apart: 39 -> 39, of which waited for: 12 -> 10; matrix products, arithmetic and copies ran while one was open for 7% -> 7% of each run, Pallas kernels for 16% -> 19%
where the time goes in v3:
time: 124 us; the launch traced here: 121 us
  starting transfers between devices  55.8 us (45%)
  waiting for transfers between devices  28.7 us (23%)
  Pallas kernels  25.1 us (20%)
  matrix products  5.83 us (5%)
  other arithmetic  4.44 us (4%)
    ppermute x14, starting transfers between devices, along_z(): return lax.ppermute(x, 'dp', pairs)  22.5 us
    ppermute x14, starting transfers between devices, over_tensor(): return lax.ppermute(x, 'tensor', [(i, i ^ k) for i in range(n_tensor)])  20.7 us
    ppermute x14, waiting for transfers between devices, along_z(): return lax.ppermute(x, 'dp', pairs)  15.2 us
    ppermute x10, waiting for transfers between devices, over_dp(): return lax.ppermute(x, 'dp', [(i, i ^ k) for i in range(n_dp)])  10.6 us
    ppermute x10, starting transfers between devices, over_dp(): return lax.ppermute(x, 'dp', [(i, i ^ k) for i in range(n_dp)])  10.5 us
    pallas_call x1, Pallas kernels, token_parts(): pl.pallas_call(back_kernel, grid_spec=pltpu.PrefetchScalarGridSpec(num_sc...  5.93 us
    pallas_call x1, Pallas kernels, early(): pl.pallas_call(lambda *a: early_kernel(n, *a), grid_spec=pltpu.PrefetchSc...  5.45 us
    dot_general x8, matrix products, product(): return jnp.dot(a.reshape(n_z * half, CAP), b, preferred_element_type=F32)  4.55 us
  transfers between devices with their start and end apart: 39, of which 10 were waited for; matrix products, arithmetic and copies ran while one was open for 7% of the time, Pallas kernels for 19%

profile of v3, /device:TPU:2, one launch (start us, length us, event | category | flops | bytes accessed | tf_op | source)
XLA Modules:
  0.0 121.4 jit_solution(16186163879173052423)
XLA Ops:
  0.7 0.7 fusion.15
  1.7 1.9 %shard_map.93 = (bf16[256,384]{1,0:T(8,128)(2,1)S(1)}, bf16[192,256]{1,0:T(8,128)(2,1)S(1)}) custom-call(s32[4]{0:T(128)S(1)} %pad_add_fusion.info.a_0_, s32[1,512]{1,0:T(1,128)S(1)} %bitcast.70, bf16[512,384]{1,0:T(8,128)(2,1)} %tokens.1), custom_call_target="tpu_custom_call" | custom-call | flops 100663296 | bytes 786432 | tf_op jit(solution)/shard_map/pallas_call | solution.py:41
  3.6 1.7 %collective-permute-start = (bf16[256,384]{1,0:T(8,128)(2,1)S(1)}, bf16[256,384]{1,0:T(8,128)(2,1)S(1)}, u32[]{:S(2)}, u32[]{:S(2)}) collective-permute-start(bf16[256,384]{1,0:T(8,128)(2,1)S(1)} %get-tuple-element.75.a_1_), channel_id=1, source_target_pairs={{0,1},{1,0},{2,3},{3,2},{4,5},{5,4},{6,7},{7,6},{8,9},{9,8},{10,11... | collective-permute-start | bytes 589832 | tf_op jit(solution)/shard_map/ppermute | solution.py:432
  5.3 2.2 %collective-permute-start.1 = (bf16[256,384]{1,0:T(8,128)(2,1)S(1)}, bf16[256,384]{1,0:T(8,128)(2,1)S(1)}, u32[]{:S(2)}, u32[]{:S(2)}) collective-permute-start(bf16[256,384]{1,0:T(8,128)(2,1)S(1)} %get-tuple-element.75.a_1_), channel_id=1, source_target_pairs={{0,3},{1,2},{2,1},{3,0},{4,7},{5,6},{6,5},{7,4},{8,11},{9,10},{10,... | collective-permute-start | bytes 589832 | tf_op jit(solution)/shard_map/ppermute | solution.py:432
  8.0 2.2 %collective-permute-start.3 = (bf16[192,256]{1,0:T(8,128)(2,1)S(1)}, bf16[192,256]{1,0:T(8,128)(2,1)S(1)}, u32[]{:S(2)}, u32[]{:S(2)}) collective-permute-start(bf16[192,256]{1,0:T(8,128)(2,1)S(1)} %get-tuple-element.79), channel_id=1, source_target_pairs={{0,20},{1,21},{2,22},{3,23},{4,16},{5,17},{6,18},{7,19},{8,28},{9,... | collective-permute-start | bytes 294920 | tf_op jit(solution)/shard_map/ppermute | solution.py:444
  10.1 0.7 select_reduce_fusion.1
  10.9 1.7 %shard_map.94 = (bf16[256,1024]{1,0:T(8,128)(2,1)S(1)}, f32[256,1]{1,0:T(8,128)S(1)}) custom-call(s32[1,512]{1,0:T(1,128)S(1)} %bitcast.71, f32[1,512]{1,0:T(1,128)S(1)} %bitcast.72, bf16[512,1024]{1,0:T(8,128)(2,1)} %cot.1), custom_call_target="tpu_custom_call" | custom-call | flops 268435456 | bytes 2097152 | tf_op jit(solution)/shard_map/pallas_call | solution.py:71
  12.8 0.7 collective-permute-done.2.a_2_
  13.5 1.9 %collective-permute-start.4 = (bf16[256,384]{1,0:T(8,128)(2,1)S(1)}, bf16[256,384]{1,0:T(8,128)(2,1)S(1)}, u32[]{:S(2)}, u32[]{:S(2)}) collective-permute-start(bf16[256,384]{1,0:T(8,128)(2,1)S(1)} %collective-permute-done.a_3_), channel_id=1, source_target_pairs={{0,4},{1,5},{2,6},{3,7},{4,0},{5,1},{6,2},{7,3},{8,12},{9,13},{10,... | collective-permute-start | bytes 589832 | tf_op jit(solution)/shard_map/ppermute | solution.py:432
  15.5 1.2 %collective-permute-start.6 = (bf16[256,384]{1,0:T(8,128)(2,1)S(1)}, bf16[256,384]{1,0:T(8,128)(2,1)S(1)}, u32[]{:S(2)}, u32[]{:S(2)}) collective-permute-start(bf16[256,384]{1,0:T(8,128)(2,1)S(1)} %get-tuple-element.75.a_1_), channel_id=1, source_target_pairs={{0,2},{1,3},{2,0},{3,1},{4,6},{5,7},{6,4},{7,5},{8,10},{9,11},{10,... | collective-permute-start | bytes 589832 | tf_op jit(solution)/shard_map/ppermute | solution.py:432
  16.8 2.3 %collective-permute-start.7 = (bf16[256,384]{1,0:T(8,128)(2,1)S(1)}, bf16[256,384]{1,0:T(8,128)(2,1)S(1)}, u32[]{:S(2)}, u32[]{:S(2)}) collective-permute-start(bf16[256,384]{1,0:T(8,128)(2,1)S(1)} %collective-permute-done.2.a_2_), channel_id=1, source_target_pairs={{0,2},{1,3},{2,0},{3,1},{4,6},{5,7},{6,4},{7,5},{8,10},{9,11},{10,... | collective-permute-start | bytes 589832 | tf_op jit(solution)/shard_map/ppermute | solution.py:432
  19.1 2.8 %collective-permute-start.8 = (bf16[192,256]{1,0:T(8,128)(2,1)S(1)}, bf16[192,256]{1,0:T(8,128)(2,1)S(1)}, u32[]{:S(2)}, u32[]{:S(2)}) collective-permute-start(bf16[192,256]{1,0:T(8,128)(2,1)S(1)} %get-tuple-element.79), channel_id=1, source_target_pairs={{0,16},{8,24},{16,0},{24,8},{32,48},{40,56},{48,32},{56,40},{64,80... | collective-permute-start | bytes 294920 | tf_op jit(solution)/shard_map/ppermute | solution.py:435
  21.9 5.5 %shard_map.95 = (f32[256,1024]{1,0:T(8,128)S(1)}, f32[256,1024]{1,0:T(8,128)S(1)}, bf16[4,192,256]{2,1,0:T(8,128)(2,1)S(1)}, bf16[3072,1024]{1,0:T(8,128)(2,1)S(1)}, bf16[3072,1024]{1,0:T(8,128)(2,1)S(1)}) custom-call(s32[9]{0:T(128)S(1)} %stack.62.a_0_, bf16[256,384]{1,0:T(8,128)(2,1)S(1)} %get-tuple-element.75.a_1_, ...), custom_call_target="tpu_custom_call" | custom-call | flops 1610612736 | bytes 12582912 | tf_op jit(solution)/shard_map/pallas_call | solution.py:135
  27.4 0.8 collective-permute-start.9
  28.2 1.8 %collective-permute-start.10 = (bf16[2,192,256]{2,1,0:T(8,128)(2,1)S(1)}, bf16[2,192,256]{2,1,0:T(8,128)(2,1)S(1)}, u32[]{:S(2)}, u32[]{:S(2)}) collective-permute-start(bf16[2,192,256]{2,1,0:T(8,128)(2,1)S(1)} %pad_maximum_fusion.a_1_), channel_id=1, source_target_pairs={{0,2},{1,3},{2,0},{3,1},{4,6},{5,7},{6,4},{7,5},{8,10},{9,11},{10,... | collective-permute-start | bytes 589832 | tf_op jit(solution)/shard_map/ppermute | solution.py:432
  30.0 2.2 %collective-permute-start.11 = (bf16[2,192,256]{2,1,0:T(8,128)(2,1)S(1)}, bf16[2,192,256]{2,1,0:T(8,128)(2,1)S(1)}, u32[]{:S(2)}, u32[]{:S(2)}) collective-permute-start(bf16[2,192,256]{2,1,0:T(8,128)(2,1)S(1)} %pad_maximum_fusion.a_1_), channel_id=1, source_target_pairs={{0,3},{1,2},{2,1},{3,0},{4,7},{5,6},{6,5},{7,4},{8,11},{9,10},{10,... | collective-permute-start | bytes 589832 | tf_op jit(solution)/shard_map/ppermute | solution.py:432
  32.2 3.9 %shard_map.96 = (bf16[256,512]{1,0:T(8,128)(2,1)S(1)}, bf16[256,512]{1,0:T(8,128)(2,1)S(1)}, bf16[256,512]{1,0:T(8,128)(2,1)S(1)}, bf16[256,512]{1,0:T(8,128)(2,...) custom-call(s32[4]{0:T(128)S(1)} %pad_add_fusion.info.a_0_, ...), custom_call_target="tpu_custom_call" | custom-call | flops 1610612736 | bytes 4194304 | tf_op jit(solution)/shard_map/pallas_call | solution.py:222
  36.2 1.9 %collective-permute-done.11.a_4_ = bf16[2,192,256]{2,1,0:T(8,128)(2,1)S(1)} collective-permute-done((bf16[2,192,256]{2,1,0:T(8,128)(2,1)S(1)}, bf16[2,192,256]{2,1,0:T(8,128)(2,1)S(1)}, u32[]{:S(2)}, u32[]{:S(2)}) %collective-permute-start.11) | collective-permute-done | bytes 196640 | tf_op jit(solution)/shard_map/ppermute | solution.py:432
  39.4 1.1 collective-permute-start.15
  40.5 2.1 %collective-permute-start.14 = (bf16[256,512]{1,0:T(8,128)(2,1)S(1)}, bf16[256,512]{1,0:T(8,128)(2,1)S(1)}, u32[]{:S(2)}, u32[]{:S(2)}) collective-permute-start(bf16[256,512]{1,0:T(8,128)(2,1)S(1)} %get-tuple-element.92.refs_0_), channel_id=1, source_target_pairs={{0,16},{8,24},{16,0},{24,8},{32,48},{40,56},{48,32},{56,40},{64,80... | collective-permute-start | bytes 786440 | tf_op jit(solution)/shard_map/ppermute | solution.py:435
  43.4 5.9 %shard_map.98 = (f32[2,384,256]{2,1,0:T(8,128)S(1)}, bf16[2,400,256]{2,1,0:T(8,128)(2,1)S(1)}, bf16[2,400,256]{2,1,0:T(8,128)(2,1)S(1)}, bf16[2,400,256]{2,1,0:T(8,128)(2,1)S(1)}) custom-call(s32[4]{0:T(128)S(1)} %pad_add_fusion.info.a_0_, bf16[256,512]{1,0:T(8,128)(2,1)S(1)} %get-tuple-element.92.refs_0_, bf16[256,512]{1,0:T(8,128)(2,1)S(1)} %get-tuple-element.118.refs_1_, ...), custom_call_target="tpu_custom_call" | custom-call | flops 3221225472 | bytes 12582912 | tf_op jit(solution)/shard_map/pallas_call | solution.py:296
  50.2 5.0 %collective-permute-done.14 = bf16[256,512]{1,0:T(8,128)(2,1)S(1)} collective-permute-done((bf16[256,512]{1,0:T(8,128)(2,1)S(1)}, bf16[256,512]{1,0:T(8,128)(2,1)S(1)}, u32[]{:S(2)}, u32[]{:S(2)}) %collective-permute-start.14) | collective-permute-done | bytes 262176 | tf_op jit(solution)/shard_map/ppermute | solution.py:435
  55.1 0.9 collective-permute-start.22
  57.9 2.0 %collective-permute-start.18 = (bf16[192,512]{1,0:T(8,128)(2,1)S(1)}, bf16[192,512]{1,0:T(8,128)(2,1)S(1)}, u32[]{:S(2)}, u32[]{:S(2)}) collective-permute-start(bf16[192,512]{1,0:T(8,128)(2,1)S(1)} %get-tuple-element.115._.a_2_), channel_id=1, source_target_pairs={{0,32},{8,232},{16,48},{24,248},{32,64},{40,8},{48,80},{56,24},{64... | collective-permute-start | bytes 589832 | tf_op jit(solution)/shard_map/ppermute | solution.py:439
  60.0 4.0 %collective-permute-start.19 = (bf16[192,512]{1,0:T(8,128)(2,1)S(1)}, bf16[192,512]{1,0:T(8,128)(2,1)S(1)}, u32[]{:S(2)}, u32[]{:S(2)}) collective-permute-start(bf16[192,512]{1,0:T(8,128)(2,1)S(1)} %get-tuple-element.117), channel_id=1, source_target_pairs={{0,224},{8,40},{16,240},{24,56},{32,0},{40,72},{48,16},{56,88},{64... | collective-permute-start | bytes 589832 | tf_op jit(solution)/shard_map/ppermute | solution.py:439
  64.1 2.1 %collective-permute-start.21 = (bf16[256,512]{1,0:T(8,128)(2,1)S(1)}, bf16[256,512]{1,0:T(8,128)(2,1)S(1)}, u32[]{:S(2)}, u32[]{:S(2)}) collective-permute-start(bf16[256,512]{1,0:T(8,128)(2,1)S(1)} %get-tuple-element.118.refs_1_), channel_id=1, source_target_pairs={{0,16},{8,24},{16,0},{24,8},{32,48},{40,56},{48,32},{56,40},{64,80... | collective-permute-start | bytes 786440 | tf_op jit(solution)/shard_map/ppermute | solution.py:435
  68.0 5.6 %collective-permute-done.21 = bf16[256,512]{1,0:T(8,128)(2,1)S(1)} collective-permute-done((bf16[256,512]{1,0:T(8,128)(2,1)S(1)}, bf16[256,512]{1,0:T(8,128)(2,1)S(1)}, u32[]{:S(2)}, u32[]{:S(2)}) %collective-permute-start.21) | collective-permute-done | bytes 262176 | tf_op jit(solution)/shard_map/ppermute | solution.py:435
  74.3 3.2 %collective-permute-start.27 = (bf16[192,512]{1,0:T(8,128)(2,1)S(1)}, bf16[192,512]{1,0:T(8,128)(2,1)S(1)}, u32[]{:S(2)}, u32[]{:S(2)}) collective-permute-start(bf16[192,512]{1,0:T(8,128)(2,1)S(1)} %get-tuple-element.124), channel_id=1, source_target_pairs={{0,224},{8,40},{16,240},{24,56},{32,0},{40,72},{48,16},{56,88},{64... | collective-permute-start | bytes 589832 | tf_op jit(solution)/shard_map/ppermute | solution.py:439
  77.7 3.2 %collective-permute-start.25 = (bf16[192,512]{1,0:T(8,128)(2,1)S(1)}, bf16[192,512]{1,0:T(8,128)(2,1)S(1)}, u32[]{:S(2)}, u32[]{:S(2)}) collective-permute-start(bf16[192,512]{1,0:T(8,128)(2,1)S(1)} %get-tuple-element.123), channel_id=1, source_target_pairs={{0,224},{8,40},{16,240},{24,56},{32,0},{40,72},{48,16},{56,88},{64... | collective-permute-start | bytes 589832 | tf_op jit(solution)/shard_map/ppermute | solution.py:439
  81.0 2.0 %collective-permute-start.23 = (bf16[2,400,256]{2,1,0:T(8,128)(2,1)S(1)}, bf16[2,400,256]{2,1,0:T(8,128)(2,1)S(1)}, u32[]{:S(2)}, u32[]{:S(2)}) collective-permute-start(bf16[2,400,256]{2,1,0:T(8,128)(2,1)S(1)} %shard_map.104), channel_id=1, source_target_pairs={{0,3},{1,2},{2,1},{3,0},{4,7},{5,6},{6,5},{7,4},{8,11},{9,10},{10,... | collective-permute-start | bytes 1228808 | tf_op jit(solution)/shard_map/ppermute | solution.py:432
  83.1 3.7 %collective-permute-done.24.a_2_ = bf16[192,512]{1,0:T(8,128)(2,1)S(1)} collective-permute-done((bf16[192,512]{1,0:T(8,128)(2,1)S(1)}, bf16[192,512]{1,0:T(8,128)(2,1)S(1)}, u32[]{:S(2)}, u32[]{:S(2)}) %collective-permute-start.24) | collective-permute-done | bytes 196640 | tf_op jit(solution)/shard_map/ppermute | solution.py:439
  86.8 0.7 shard_map.106
  87.5 0.8 shard_map.107
  88.3 2.8 %collective-permute-start.28 = (bf16[2,400,256]{2,1,0:T(8,128)(2,1)}, bf16[2,400,256]{2,1,0:T(8,128)(2,1)}, u32[]{:S(2)}, u32[]{:S(2)}) collective-permute-start(bf16[2,400,256]{2,1,0:T(8,128)(2,1)} %shard_map.107), channel_id=1, source_target_pairs={{0,2},{1,3},{2,0},{3,1},{4,6},{5,7},{6,4},{7,5},{8,10},{9,11},{10,... | collective-permute-start | bytes 1228808 | tf_op jit(solution)/shard_map/ppermute | solution.py:432
  91.0 3.2 %collective-permute-start.32 = (bf16[192,512]{1,0:T(8,128)(2,1)S(1)}, bf16[192,512]{1,0:T(8,128)(2,1)S(1)}, u32[]{:S(2)}, u32[]{:S(2)}) collective-permute-start(bf16[192,512]{1,0:T(8,128)(2,1)S(1)} %get-tuple-element.129), channel_id=1, source_target_pairs={{0,224},{8,40},{16,240},{24,56},{32,0},{40,72},{48,16},{56,88},{64... | collective-permute-start | bytes 589832 | tf_op jit(solution)/shard_map/ppermute | solution.py:439
  94.3 5.3 %collective-permute-done.31.a_2_ = bf16[192,512]{1,0:T(8,128)(2,1)S(1)} collective-permute-done((bf16[192,512]{1,0:T(8,128)(2,1)S(1)}, bf16[192,512]{1,0:T(8,128)(2,1)S(1)}, u32[]{:S(2)}, u32[]{:S(2)}) %collective-permute-start.31) | collective-permute-done | bytes 196640 | tf_op jit(solution)/shard_map/ppermute | solution.py:439
  99.6 0.9 shard_map.109
  100.4 4.2 %collective-permute-start.36 = (bf16[192,512]{1,0:T(8,128)(2,1)}, bf16[192,512]{1,0:T(8,128)(2,1)}, u32[]{:S(2)}, u32[]{:S(2)}) collective-permute-start(bf16[192,512]{1,0:T(8,128)(2,1)} %get-tuple-element.132), channel_id=1, source_target_pairs={{0,224},{8,40},{16,240},{24,56},{32,0},{40,72},{48,16},{56,88},{64... | collective-permute-start | bytes 589832 | tf_op jit(solution)/shard_map/ppermute | solution.py:439
  104.9 1.8 %shard_map.108 = (f32[384,256]{1,0:T(8,128)S(1)}, f32[1,256]{1,0:T(1,128)S(1)}, bf16[400,256]{1,0:T(8,128)(2,1)S(1)}) custom-call(f32[2,384,256]{2,1,0:T(8,128)} %copy-done.3, f32[1,256]{1,0:T(1,128)} %copy-done.6, bf16[2,400,256]{2,1,0:T(8,128)(2,1)} %copy-done.1, bf16[2,400,256]{2,1,0:T(8,128)(2,1)} %copy-done.2, ...), custom_call_target="tpu_custom_call" | custom-call | flops 786432 | bytes 2949120 | tf_op jit(solution)/shard_map/pallas_call | solution.py:347
  106.7 1.1 collective-permute-start.29
  107.8 4.0 %collective-permute-done.36.a_1_ = bf16[192,512]{1,0:T(8,128)(2,1)} collective-permute-done((bf16[192,512]{1,0:T(8,128)(2,1)}, bf16[192,512]{1,0:T(8,128)(2,1)}, u32[]{:S(2)}, u32[]{:S(2)}) %collective-permute-start.36) | collective-permute-done | bytes 196640 | tf_op jit(solution)/shard_map/ppermute | solution.py:439
  111.8 1.0 shard_map.111
  112.8 2.2 %collective-permute-start.37 = (bf16[192,512]{1,0:T(8,128)(2,1)S(1)}, bf16[192,512]{1,0:T(8,128)(2,1)S(1)}, u32[]{:S(2)}, u32[]{:S(2)}) collective-permute-start(bf16[192,512]{1,0:T(8,128)(2,1)S(1)} %shard_map.111), channel_id=1, source_target_pairs={{0,224},{8,40},{16,240},{24,56},{32,0},{40,72},{48,16},{56,88},{64... | collective-permute-start | bytes 589832 | tf_op jit(solution)/shard_map/ppermute | solution.py:439
  115.0 1.2 %fusion.7 = bf16[192,512]{1,0:T(8,128)(2,1)S(1)} fusion(f32[1536,512]{1,0:T(8,128)} %copy-done, bf16[192,512]{1,0:T(8,128)(2,1)} %collective-permute-done.34, bf16[192,512]{1,0:T(8,128)(2,1)} %collective-permute-done.33), kind=kLoop, calls=%fused_computation.21 | loop fusion | flops 491520 | bytes 983040 | tf_op jit(solution)/shard_map/convert_element_type | solution.py:537
  116.2 2.3 %collective-permute-done.37 = bf16[192,512]{1,0:T(8,128)(2,1)S(1)} collective-permute-done((bf16[192,512]{1,0:T(8,128)(2,1)S(1)}, bf16[192,512]{1,0:T(8,128)(2,1)S(1)}, u32[]{:S(2)}, u32[]{:S(2)}) %collective-permute-start.37) | collective-permute-done | bytes 196640 | tf_op jit(solution)/shard_map/ppermute | solution.py:439
  118.8 0.7 select_reduce_fusion
  119.5 1.1 convolution_convert_fusion
  120.6 0.8 broadcast_select_fusion
  (88 shorter events, 9.3 us)
Async XLA Ops:
  1.6 25.8 %copy-start.4 = (s32[512]{0:T(512)}, s32[512]{0:T(512)S(1)}, u32[]{:S(2)}) copy-start(s32[512]{0:T(512)S(1)} %convert_select_fusion) | copy-start | bytes 6148
  3.6 9.1 %collective-permute-start = (bf16[256,384]{1,0:T(8,128)(2,1)S(1)}, bf16[256,384]{1,0:T(8,128)(2,1)S(1)}, u32[]{:S(2)}, u32[]{:S(2)}) collective-permute-start(bf16[256,384]{1,0:T(8,128)(2,1)S(1)} %get-tuple-element.75.a_1_), channel_id=1, source_target_pairs={{0,1},{1,0},{2,3},{3,2},{4,5},{5,4},{6,7},{7,6},{8,9},{9,8},{10,11... | collective-permute-start | bytes 589832 | tf_op jit(solution)/shard_map/ppermute | solution.py:432
  5.3 7.6 %collective-permute-start.1 = (bf16[256,384]{1,0:T(8,128)(2,1)S(1)}, bf16[256,384]{1,0:T(8,128)(2,1)S(1)}, u32[]{:S(2)}, u32[]{:S(2)}) collective-permute-start(bf16[256,384]{1,0:T(8,128)(2,1)S(1)} %get-tuple-element.75.a_1_), channel_id=1, source_target_pairs={{0,3},{1,2},{2,1},{3,0},{4,7},{5,6},{6,5},{7,4},{8,11},{9,10},{10,... | collective-permute-start | bytes 589832 | tf_op jit(solution)/shard_map/ppermute | solution.py:432
  7.4 6.1 %collective-permute-start.2 = (bf16[256,384]{1,0:T(8,128)(2,1)S(1)}, bf16[256,384]{1,0:T(8,128)(2,1)S(1)}, u32[]{:S(2)}, u32[]{:S(2)}) collective-permute-start(bf16[256,384]{1,0:T(8,128)(2,1)S(1)} %get-tuple-element.75.a_1_), channel_id=1, source_target_pairs={{0,4},{1,5},{2,6},{3,7},{4,0},{5,1},{6,2},{7,3},{8,12},{9,13},{10,... | collective-permute-start | bytes 589832 | tf_op jit(solution)/shard_map/ppermute | solution.py:432
  8.0 4.7 %collective-permute-start.3 = (bf16[192,256]{1,0:T(8,128)(2,1)S(1)}, bf16[192,256]{1,0:T(8,128)(2,1)S(1)}, u32[]{:S(2)}, u32[]{:S(2)}) collective-permute-start(bf16[192,256]{1,0:T(8,128)(2,1)S(1)} %get-tuple-element.79), channel_id=1, source_target_pairs={{0,20},{1,21},{2,22},{3,23},{4,16},{5,17},{6,18},{7,19},{8,28},{9,... | collective-permute-start | bytes 294920 | tf_op jit(solution)/shard_map/ppermute | solution.py:444
  13.5 13.9 %collective-permute-start.4 = (bf16[256,384]{1,0:T(8,128)(2,1)S(1)}, bf16[256,384]{1,0:T(8,128)(2,1)S(1)}, u32[]{:S(2)}, u32[]{:S(2)}) collective-permute-start(bf16[256,384]{1,0:T(8,128)(2,1)S(1)} %collective-permute-done.a_3_), channel_id=1, source_target_pairs={{0,4},{1,5},{2,6},{3,7},{4,0},{5,1},{6,2},{7,3},{8,12},{9,13},{10,... | collective-permute-start | bytes 589832 | tf_op jit(solution)/shard_map/ppermute | solution.py:432
  15.4 12.0 %collective-permute-start.5 = (bf16[256,384]{1,0:T(8,128)(2,1)S(1)}, bf16[256,384]{1,0:T(8,128)(2,1)S(1)}, u32[]{:S(2)}, u32[]{:S(2)}) collective-permute-start(bf16[256,384]{1,0:T(8,128)(2,1)S(1)} %collective-permute-done.1.a_4_), channel_id=1, source_target_pairs={{0,4},{1,5},{2,6},{3,7},{4,0},{5,1},{6,2},{7,3},{8,12},{9,13},{10,... | collective-permute-start | bytes 589832 | tf_op jit(solution)/shard_map/ppermute | solution.py:432
  15.5 11.9 %collective-permute-start.6 = (bf16[256,384]{1,0:T(8,128)(2,1)S(1)}, bf16[256,384]{1,0:T(8,128)(2,1)S(1)}, u32[]{:S(2)}, u32[]{:S(2)}) collective-permute-start(bf16[256,384]{1,0:T(8,128)(2,1)S(1)} %get-tuple-element.75.a_1_), channel_id=1, source_target_pairs={{0,2},{1,3},{2,0},{3,1},{4,6},{5,7},{6,4},{7,5},{8,10},{9,11},{10,... | collective-permute-start | bytes 589832 | tf_op jit(solution)/shard_map/ppermute | solution.py:432
  16.8 10.6 %collective-permute-start.7 = (bf16[256,384]{1,0:T(8,128)(2,1)S(1)}, bf16[256,384]{1,0:T(8,128)(2,1)S(1)}, u32[]{:S(2)}, u32[]{:S(2)}) collective-permute-start(bf16[256,384]{1,0:T(8,128)(2,1)S(1)} %collective-permute-done.2.a_2_), channel_id=1, source_target_pairs={{0,2},{1,3},{2,0},{3,1},{4,6},{5,7},{6,4},{7,5},{8,10},{9,11},{10,... | collective-permute-start | bytes 589832 | tf_op jit(solution)/shard_map/ppermute | solution.py:432
  19.1 8.3 %collective-permute-start.8 = (bf16[192,256]{1,0:T(8,128)(2,1)S(1)}, bf16[192,256]{1,0:T(8,128)(2,1)S(1)}, u32[]{:S(2)}, u32[]{:S(2)}) collective-permute-start(bf16[192,256]{1,0:T(8,128)(2,1)S(1)} %get-tuple-element.79), channel_id=1, source_target_pairs={{0,16},{8,24},{16,0},{24,8},{32,48},{40,56},{48,32},{56,40},{64,80... | collective-permute-start | bytes 294920 | tf_op jit(solution)/shard_map/ppermute | solution.py:435
  27.4 8.8 %collective-permute-start.9 = (bf16[2,192,256]{2,1,0:T(8,128)(2,1)S(1)}, bf16[2,192,256]{2,1,0:T(8,128)(2,1)S(1)}, u32[]{:S(2)}, u32[]{:S(2)}) collective-permute-start(bf16[2,192,256]{2,1,0:T(8,128)(2,1)S(1)} %pad_maximum_fusion.a_1_), channel_id=1, source_target_pairs={{0,1},{1,0},{2,3},{3,2},{4,5},{5,4},{6,7},{7,6},{8,9},{9,8},{10,11... | collective-permute-start | bytes 589832 | tf_op jit(solution)/shard_map/ppermute | solution.py:432
  28.2 8.0 %collective-permute-start.10 = (bf16[2,192,256]{2,1,0:T(8,128)(2,1)S(1)}, bf16[2,192,256]{2,1,0:T(8,128)(2,1)S(1)}, u32[]{:S(2)}, u32[]{:S(2)}) collective-permute-start(bf16[2,192,256]{2,1,0:T(8,128)(2,1)S(1)} %pad_maximum_fusion.a_1_), channel_id=1, source_target_pairs={{0,2},{1,3},{2,0},{3,1},{4,6},{5,7},{6,4},{7,5},{8,10},{9,11},{10,... | collective-permute-start | bytes 589832 | tf_op jit(solution)/shard_map/ppermute | solution.py:432
  30.0 8.1 %collective-permute-start.11 = (bf16[2,192,256]{2,1,0:T(8,128)(2,1)S(1)}, bf16[2,192,256]{2,1,0:T(8,128)(2,1)S(1)}, u32[]{:S(2)}, u32[]{:S(2)}) collective-permute-start(bf16[2,192,256]{2,1,0:T(8,128)(2,1)S(1)} %pad_maximum_fusion.a_1_), channel_id=1, source_target_pairs={{0,3},{1,2},{2,1},{3,0},{4,7},{5,6},{6,5},{7,4},{8,11},{9,10},{10,... | collective-permute-start | bytes 589832 | tf_op jit(solution)/shard_map/ppermute | solution.py:432
  36.2 13.1 %copy-start.6 = (f32[1,256]{1,0:T(1,128)}, f32[1,256]{1,0:T(1,128)S(1)}, u32[]{:S(2)}) copy-start(f32[1,256]{1,0:T(1,128)S(1)} %get-tuple-element.96.refs_4_.route) | copy-start | bytes 3076
  38.8 10.5 %collective-permute-start.12 = (bf16[8,192,256]{2,1,0:T(8,128)(2,1)S(1)}, bf16[8,192,256]{2,1,0:T(8,128)(2,1)S(1)}, u32[]{:S(2)}, u32[]{:S(2)}) collective-permute-start(bf16[8,192,256]{2,1,0:T(8,128)(2,1)S(1)} %get-tuple-element.106), channel_id=1, source_target_pairs={{0,8},{8,0},{16,24},{24,16},{32,40},{40,32},{48,56},{56,48},{64,72... | collective-permute-start | bytes 2359304 | tf_op jit(solution)/shard_map/ppermute | solution.py:435
  38.9 10.4 %collective-permute-start.13 = (bf16[256,512]{1,0:T(8,128)(2,1)S(1)}, bf16[256,512]{1,0:T(8,128)(2,1)S(1)}, u32[]{:S(2)}, u32[]{:S(2)}) collective-permute-start(bf16[256,512]{1,0:T(8,128)(2,1)S(1)} %get-tuple-element.94.refs_2_), channel_id=1, source_target_pairs={{0,8},{8,0},{16,24},{24,16},{32,40},{40,32},{48,56},{56,48},{64,72... | collective-permute-start | bytes 786440 | tf_op jit(solution)/shard_map/ppermute | solution.py:435
  39.4 15.7 %collective-permute-start.15 = (bf16[256,512]{1,0:T(8,128)(2,1)S(1)}, bf16[256,512]{1,0:T(8,128)(2,1)S(1)}, u32[]{:S(2)}, u32[]{:S(2)}) collective-permute-start(bf16[256,512]{1,0:T(8,128)(2,1)S(1)} %get-tuple-element.94.refs_2_), channel_id=1, source_target_pairs={{0,24},{8,16},{16,8},{24,0},{32,56},{40,48},{48,40},{56,32},{64,88... | collective-permute-start | bytes 786440 | tf_op jit(solution)/shard_map/ppermute | solution.py:435
  40.5 14.6 %collective-permute-start.14 = (bf16[256,512]{1,0:T(8,128)(2,1)S(1)}, bf16[256,512]{1,0:T(8,128)(2,1)S(1)}, u32[]{:S(2)}, u32[]{:S(2)}) collective-permute-start(bf16[256,512]{1,0:T(8,128)(2,1)S(1)} %get-tuple-element.92.refs_0_), channel_id=1, source_target_pairs={{0,16},{8,24},{16,0},{24,8},{32,48},{40,56},{48,32},{56,40},{64,80... | collective-permute-start | bytes 786440 | tf_op jit(solution)/shard_map/ppermute | solution.py:435
  42.6 14.0 %collective-permute-start.16 = (bf16[8,192,256]{2,1,0:T(8,128)(2,1)S(1)}, bf16[8,192,256]{2,1,0:T(8,128)(2,1)S(1)}, u32[]{:S(2)}, u32[]{:S(2)}) collective-permute-start(bf16[8,192,256]{2,1,0:T(8,128)(2,1)S(1)} %get-tuple-element.113), channel_id=1, source_target_pairs={{0,8},{8,0},{16,24},{24,16},{32,40},{40,32},{48,56},{56,48},{64,72... | collective-permute-start | bytes 2359304 | tf_op jit(solution)/shard_map/ppermute | solution.py:435
  49.3 0.9 copy-start.3
  55.1 12.3 %collective-permute-start.22 = (bf16[256,512]{1,0:T(8,128)(2,1)S(1)}, bf16[256,512]{1,0:T(8,128)(2,1)S(1)}, u32[]{:S(2)}, u32[]{:S(2)}) collective-permute-start(bf16[256,512]{1,0:T(8,128)(2,1)S(1)} %get-tuple-element.119.refs_3_), channel_id=1, source_target_pairs={{0,24},{8,16},{16,8},{24,0},{32,56},{40,48},{48,40},{56,32},{64,88... | collective-permute-start | bytes 786440 | tf_op jit(solution)/shard_map/ppermute | solution.py:435
  56.0 8.1 %collective-permute-start.20 = (bf16[256,512]{1,0:T(8,128)(2,1)S(1)}, bf16[256,512]{1,0:T(8,128)(2,1)S(1)}, u32[]{:S(2)}, u32[]{:S(2)}) collective-permute-start(bf16[256,512]{1,0:T(8,128)(2,1)S(1)} %get-tuple-element.119.refs_3_), channel_id=1, source_target_pairs={{0,8},{8,0},{16,24},{24,16},{32,40},{40,32},{48,56},{56,48},{64,72... | collective-permute-start | bytes 786440 | tf_op jit(solution)/shard_map/ppermute | solution.py:435
  57.8 46.8 %copy-start = (f32[1536,512]{1,0:T(8,128)}, f32[1536,512]{1,0:T(8,128)S(1)}, u32[]{:S(2)}) copy-start(f32[1536,512]{1,0:T(8,128)S(1)} %fusion.1) | copy-start | bytes 9437188
  57.9 19.7 %collective-permute-start.18 = (bf16[192,512]{1,0:T(8,128)(2,1)S(1)}, bf16[192,512]{1,0:T(8,128)(2,1)S(1)}, u32[]{:S(2)}, u32[]{:S(2)}) collective-permute-start(bf16[192,512]{1,0:T(8,128)(2,1)S(1)} %get-tuple-element.115._.a_2_), channel_id=1, source_target_pairs={{0,32},{8,232},{16,48},{24,248},{32,64},{40,8},{48,80},{56,24},{64... | collective-permute-start | bytes 589832 | tf_op jit(solution)/shard_map/ppermute | solution.py:439
  59.9 21.0 %collective-permute-start.17 = (bf16[2,400,256]{2,1,0:T(8,128)(2,1)S(1)}, bf16[2,400,256]{2,1,0:T(8,128)(2,1)S(1)}, u32[]{:S(2)}, u32[]{:S(2)}) collective-permute-start(bf16[2,400,256]{2,1,0:T(8,128)(2,1)S(1)} %shard_map.100), channel_id=1, source_target_pairs={{0,1},{1,0},{2,3},{3,2},{4,5},{5,4},{6,7},{7,6},{8,9},{9,8},{10,11... | collective-permute-start | bytes 1228808 | tf_op jit(solution)/shard_map/ppermute | solution.py:432
  60.0 17.5 %collective-permute-start.19 = (bf16[192,512]{1,0:T(8,128)(2,1)S(1)}, bf16[192,512]{1,0:T(8,128)(2,1)S(1)}, u32[]{:S(2)}, u32[]{:S(2)}) collective-permute-start(bf16[192,512]{1,0:T(8,128)(2,1)S(1)} %get-tuple-element.117), channel_id=1, source_target_pairs={{0,224},{8,40},{16,240},{24,56},{32,0},{40,72},{48,16},{56,88},{64... | collective-permute-start | bytes 589832 | tf_op jit(solution)/shard_map/ppermute | solution.py:439
  64.1 9.5 %collective-permute-start.21 = (bf16[256,512]{1,0:T(8,128)(2,1)S(1)}, bf16[256,512]{1,0:T(8,128)(2,1)S(1)}, u32[]{:S(2)}, u32[]{:S(2)}) collective-permute-start(bf16[256,512]{1,0:T(8,128)(2,1)S(1)} %get-tuple-element.118.refs_1_), channel_id=1, source_target_pairs={{0,16},{8,24},{16,0},{24,8},{32,48},{40,56},{48,32},{56,40},{64,80... | collective-permute-start | bytes 786440 | tf_op jit(solution)/shard_map/ppermute | solution.py:435
  74.2 8.7 %collective-permute-start.26 = (bf16[192,512]{1,0:T(8,128)(2,1)S(1)}, bf16[192,512]{1,0:T(8,128)(2,1)S(1)}, u32[]{:S(2)}, u32[]{:S(2)}) collective-permute-start(bf16[192,512]{1,0:T(8,128)(2,1)S(1)} %get-tuple-element.120.a_4_), channel_id=1, source_target_pairs={{0,32},{8,232},{16,48},{24,248},{32,64},{40,8},{48,80},{56,24},{64... | collective-permute-start | bytes 589832 | tf_op jit(solution)/shard_map/ppermute | solution.py:439
  74.3 8.7 %collective-permute-start.27 = (bf16[192,512]{1,0:T(8,128)(2,1)S(1)}, bf16[192,512]{1,0:T(8,128)(2,1)S(1)}, u32[]{:S(2)}, u32[]{:S(2)}) collective-permute-start(bf16[192,512]{1,0:T(8,128)(2,1)S(1)} %get-tuple-element.124), channel_id=1, source_target_pairs={{0,224},{8,40},{16,240},{24,56},{32,0},{40,72},{48,16},{56,88},{64... | collective-permute-start | bytes 589832 | tf_op jit(solution)/shard_map/ppermute | solution.py:439
  77.6 9.1 %collective-permute-start.24 = (bf16[192,512]{1,0:T(8,128)(2,1)S(1)}, bf16[192,512]{1,0:T(8,128)(2,1)S(1)}, u32[]{:S(2)}, u32[]{:S(2)}) collective-permute-start(bf16[192,512]{1,0:T(8,128)(2,1)S(1)} %get-tuple-element.121._.a_4_), channel_id=1, source_target_pairs={{0,32},{8,232},{16,48},{24,248},{32,64},{40,8},{48,80},{56,24},{64... | collective-permute-start | bytes 589832 | tf_op jit(solution)/shard_map/ppermute | solution.py:439
  77.7 9.0 %collective-permute-start.25 = (bf16[192,512]{1,0:T(8,128)(2,1)S(1)}, bf16[192,512]{1,0:T(8,128)(2,1)S(1)}, u32[]{:S(2)}, u32[]{:S(2)}) collective-permute-start(bf16[192,512]{1,0:T(8,128)(2,1)S(1)} %get-tuple-element.123), channel_id=1, source_target_pairs={{0,224},{8,40},{16,240},{24,56},{32,0},{40,72},{48,16},{56,88},{64... | collective-permute-start | bytes 589832 | tf_op jit(solution)/shard_map/ppermute | solution.py:439
  81.0 2.1 %copy-start.1 = (bf16[2,400,256]{2,1,0:T(8,128)(2,1)}, bf16[2,400,256]{2,1,0:T(8,128)(2,1)S(1)}, u32[]{:S(2)}) copy-start(bf16[2,400,256]{2,1,0:T(8,128)(2,1)S(1)} %collective-permute-done.17.a_5_.first) | copy-start | bytes 1228804
  81.0 18.5 %collective-permute-start.23 = (bf16[2,400,256]{2,1,0:T(8,128)(2,1)S(1)}, bf16[2,400,256]{2,1,0:T(8,128)(2,1)S(1)}, u32[]{:S(2)}, u32[]{:S(2)}) collective-permute-start(bf16[2,400,256]{2,1,0:T(8,128)(2,1)S(1)} %shard_map.104), channel_id=1, source_target_pairs={{0,3},{1,2},{2,1},{3,0},{4,7},{5,6},{6,5},{7,4},{8,11},{9,10},{10,... | collective-permute-start | bytes 1228808 | tf_op jit(solution)/shard_map/ppermute | solution.py:432
  88.3 16.6 %collective-permute-start.28 = (bf16[2,400,256]{2,1,0:T(8,128)(2,1)}, bf16[2,400,256]{2,1,0:T(8,128)(2,1)}, u32[]{:S(2)}, u32[]{:S(2)}) collective-permute-start(bf16[2,400,256]{2,1,0:T(8,128)(2,1)} %shard_map.107), channel_id=1, source_target_pairs={{0,2},{1,3},{2,0},{3,1},{4,6},{5,7},{6,4},{7,5},{8,10},{9,11},{10,... | collective-permute-start | bytes 1228808 | tf_op jit(solution)/shard_map/ppermute | solution.py:432
  91.0 8.5 %collective-permute-start.31 = (bf16[192,512]{1,0:T(8,128)(2,1)S(1)}, bf16[192,512]{1,0:T(8,128)(2,1)S(1)}, u32[]{:S(2)}, u32[]{:S(2)}) collective-permute-start(bf16[192,512]{1,0:T(8,128)(2,1)S(1)} %get-tuple-element.125.a_4_), channel_id=1, source_target_pairs={{0,32},{8,232},{16,48},{24,248},{32,64},{40,8},{48,80},{56,24},{64... | collective-permute-start | bytes 589832 | tf_op jit(solution)/shard_map/ppermute | solution.py:439
  91.0 8.5 %collective-permute-start.32 = (bf16[192,512]{1,0:T(8,128)(2,1)S(1)}, bf16[192,512]{1,0:T(8,128)(2,1)S(1)}, u32[]{:S(2)}, u32[]{:S(2)}) collective-permute-start(bf16[192,512]{1,0:T(8,128)(2,1)S(1)} %get-tuple-element.129), channel_id=1, source_target_pairs={{0,224},{8,40},{16,240},{24,56},{32,0},{40,72},{48,16},{56,88},{64... | collective-permute-start | bytes 589832 | tf_op jit(solution)/shard_map/ppermute | solution.py:439
  94.3 10.4 %collective-permute-start.30 = (bf16[192,512]{1,0:T(8,128)(2,1)S(1)}, bf16[192,512]{1,0:T(8,128)(2,1)S(1)}, u32[]{:S(2)}, u32[]{:S(2)}) collective-permute-start(bf16[192,512]{1,0:T(8,128)(2,1)S(1)} %get-tuple-element.126._.a_4_), channel_id=1, source_target_pairs={{0,32},{8,232},{16,48},{24,248},{32,64},{40,8},{48,80},{56,24},{64... | collective-permute-start | bytes 589832 | tf_op jit(solution)/shard_map/ppermute | solution.py:439
  99.5 15.4 %collective-permute-start.34 = (bf16[192,512]{1,0:T(8,128)(2,1)}, bf16[192,512]{1,0:T(8,128)(2,1)}, u32[]{:S(2)}, u32[]{:S(2)}) collective-permute-start(bf16[192,512]{1,0:T(8,128)(2,1)} %get-tuple-element.131), channel_id=1, source_target_pairs={{0,224},{8,40},{16,240},{24,56},{32,0},{40,72},{48,16},{56,88},{64... | collective-permute-start | bytes 589832 | tf_op jit(solution)/shard_map/ppermute | solution.py:439
  99.5 0.9 copy-start.2
  100.4 11.4 %collective-permute-start.36 = (bf16[192,512]{1,0:T(8,128)(2,1)}, bf16[192,512]{1,0:T(8,128)(2,1)}, u32[]{:S(2)}, u32[]{:S(2)}) collective-permute-start(bf16[192,512]{1,0:T(8,128)(2,1)} %get-tuple-element.132), channel_id=1, source_target_pairs={{0,224},{8,40},{16,240},{24,56},{32,0},{40,72},{48,16},{56,88},{64... | collective-permute-start | bytes 589832 | tf_op jit(solution)/shard_map/ppermute | solution.py:439
  104.7 10.3 %collective-permute-start.33 = (bf16[192,512]{1,0:T(8,128)(2,1)S(1)}, bf16[192,512]{1,0:T(8,128)(2,1)}, u32[]{:S(2)}, u32[]{:S(2)}) collective-permute-start(bf16[192,512]{1,0:T(8,128)(2,1)S(1)} %shard_map.110.a_2_), channel_id=1, source_target_pairs={{0,32},{8,232},{16,48},{24,248},{32,64},{40,8},{48,80},{56,24},{64... | collective-permute-start | bytes 589832 | tf_op jit(solution)/shard_map/ppermute | solution.py:439
  104.8 11.4 %collective-permute-start.35 = (bf16[192,512]{1,0:T(8,128)(2,1)S(1)}, bf16[192,512]{1,0:T(8,128)(2,1)S(1)}, u32[]{:S(2)}, u32[]{:S(2)}) collective-permute-start(bf16[192,512]{1,0:T(8,128)(2,1)S(1)} %get-tuple-element.130.a_2_), channel_id=1, source_target_pairs={{0,32},{8,232},{16,48},{24,248},{32,64},{40,8},{48,80},{56,24},{64... | collective-permute-start | bytes 589832 | tf_op jit(solution)/shard_map/ppermute | solution.py:439
  106.7 12.1 %copy-start.5 = (s32[512]{0:T(512)S(1)}, s32[512]{0:T(512)}, u32[]{:S(2)}) copy-start(s32[512]{0:T(512)} %copy-done.4) | copy-start | bytes 6148
  106.7 12.0 %collective-permute-start.29 = (bf16[400,256]{1,0:T(8,128)(2,1)S(1)}, bf16[400,256]{1,0:T(8,128)(2,1)S(1)}, u32[]{:S(2)}, u32[]{:S(2)}) collective-permute-start(bf16[400,256]{1,0:T(8,128)(2,1)S(1)} %get-tuple-element.128.a_3_), channel_id=1, source_target_pairs={{0,4},{1,5},{2,6},{3,7},{4,0},{5,1},{6,2},{7,3},{8,12},{9,13},{10,... | collective-permute-start | bytes 614408 | tf_op jit(solution)/shard_map/ppermute | solution.py:432
  112.8 5.7 %collective-permute-start.37 = (bf16[192,512]{1,0:T(8,128)(2,1)S(1)}, bf16[192,512]{1,0:T(8,128)(2,1)S(1)}, u32[]{:S(2)}, u32[]{:S(2)}) collective-permute-start(bf16[192,512]{1,0:T(8,128)(2,1)S(1)} %shard_map.111), channel_id=1, source_target_pairs={{0,224},{8,40},{16,240},{24,56},{32,0},{40,72},{48,16},{56,88},{64... | collective-permute-start | bytes 589832 | tf_op jit(solution)/shard_map/ppermute | solution.py:439
  118.6 2.0 %collective-permute-start.38 = (bf16[96,1024]{1,0:T(8,128)(2,1)S(1)}, bf16[96,1024]{1,0:T(8,128)(2,1)S(1)}, u32[]{:S(2)}, u32[]{:S(2)}) collective-permute-start(bf16[96,1024]{1,0:T(8,128)(2,1)S(1)} %fusion.11), channel_id=1, source_target_pairs={{0,8},{8,0},{16,24},{24,16},{32,40},{40,32},{48,56},{56,48},{64,72... | collective-permute-start | bytes 589832 | tf_op jit(solution)/shard_map/ppermute | solution.py:435

commit v4 on v2

--- a/solution.py
+++ b/solution.py
@@ -546,13 +546,18 @@
         waited = rings[c].hop(0, [waited])
     for i in range(1, n_z // 2):
         waited = rings[0].hop(i, [waited])
-        if i < 3:
-            sums[4 - i] = over_tensor(after(sent[i], waited), 4 - i)
-        else:
+        if i == 1:
+            sums[3] = over_tensor(after(sent[1], waited), 3)
+            sums[2] = over_tensor(after(sent[2], waited), 2)
+        if i == 3:
             parts = [sums[1], sums[3], sums[2]]
-            total, route_total, message = combine(own_part, route_part, parts)
+            in_hbm = lambda a: pltpu.with_memory_space_constraint(a, pltpu.HBM)
+            total, route_total, message = combine(
+                in_hbm(own_part), in_hbm(route_part), [in_hbm(a) for a in parts]
+            )
         for ring in rings[1:]:
-            waited = ring.hop(i, [waited, message if i == 3 else sums[(1, 3)[i - 1]]])
+            needed = ([sums[1]], [sums[3], sums[2]], [message] if i == 3 else [])[i - 1]
+            waited = ring.hop(i, [waited, *needed])
     whole_rows = jnp.concatenate([ring.finish() for ring in rings], axis=2)
     kept = lax.dynamic_index_in_dim(whole_rows, core, 0, keepdims=False)
     swapped = over_dp(lax.dynamic_index_in_dim(whole_rows, 1 - core, 0, keepdims=False), 1)

time: 123 us -> 122 us (level); the launches traced: 123 us -> 120 us
  starting transfers between devices: 62.7 us -> 57.6 us
  waiting for transfers between devices: 20.5 us -> 22.9 us
    ppermute x14, starting transfers between devices: 31.2 us -> 26.4 us  [along_z(): return lax.ppermute(x, 'dp', pairs)]
    ppermute x14, waiting for transfers between devices: 8.06 us -> 9.64 us  [over_tensor(): return lax.ppermute(x, 'tensor', [(i, i ^ k) for i in range(n_tensor)])]
    unnamed x20 -> x18, local copies, waits for them, and re-layouts: 2.83 us -> 2.59 us
  transfers between devices with their start and end apart: 39 -> 39, of which waited for: 12 -> 12; matrix products, arithmetic and copies ran while one was open for 7% -> 7% of each run, Pallas kernels for 16% -> 15%
where the time goes in v4:
time: 122 us; the launch traced here: 120 us
  starting transfers between devices  57.6 us (47%)
  Pallas kernels  24.2 us (20%)
  waiting for transfers between devices  22.9 us (19%)
  matrix products  5.84 us (5%)
  other arithmetic  5.31 us (4%)
  local copies, waits for them, and re-layouts  2.69 us (2%)
    ppermute x14, starting transfers between devices, along_z(): return lax.ppermute(x, 'dp', pairs)  26.4 us
    ppermute x14, starting transfers between devices, over_tensor(): return lax.ppermute(x, 'tensor', [(i, i ^ k) for i in range(n_tensor)])  18.5 us
    ppermute x10, starting transfers between devices, over_dp(): return lax.ppermute(x, 'dp', [(i, i ^ k) for i in range(n_dp)])  10.5 us
    ppermute x14, waiting for transfers between devices, along_z(): return lax.ppermute(x, 'dp', pairs)  9.92 us
    ppermute x14, waiting for transfers between devices, over_tensor(): return lax.ppermute(x, 'tensor', [(i, i ^ k) for i in range(n_tensor)])  9.64 us
    pallas_call x1, Pallas kernels, token_parts(): pl.pallas_call(back_kernel, grid_spec=pltpu.PrefetchScalarGridSpec(num_sc...  5.93 us
    pallas_call x1, Pallas kernels, early(): pl.pallas_call(lambda *a: early_kernel(n, *a), grid_spec=pltpu.PrefetchSc...  5.45 us
    dot_general x8, matrix products, product(): return jnp.dot(a.reshape(n_z * half, CAP), b, preferred_element_type=F32)  4.56 us
  transfers between devices with their start and end apart: 39, of which 12 were waited for; matrix products, arithmetic and copies ran while one was open for 7% of the time, Pallas kernels for 15%

profile of v4, /device:TPU:2, one launch (start us, length us, event | category | flops | bytes accessed | tf_op | source)
XLA Modules:
  0.0 119.7 jit_solution(3625165278360754950)
XLA Ops:
  1.7 1.9 %shard_map.93 = (bf16[256,384]{1,0:T(8,128)(2,1)S(1)}, bf16[192,256]{1,0:T(8,128)(2,1)S(1)}) custom-call(s32[4]{0:T(128)S(1)} %pad_add_fusion.info.a_0_, s32[1,512]{1,0:T(1,128)S(1)} %bitcast.70, bf16[512,384]{1,0:T(8,128)(2,1)} %tokens.1), custom_call_target="tpu_custom_call" | custom-call | flops 100663296 | bytes 786432 | tf_op jit(solution)/shard_map/pallas_call | solution.py:41
  3.6 1.7 %collective-permute-start = (bf16[256,384]{1,0:T(8,128)(2,1)S(1)}, bf16[256,384]{1,0:T(8,128)(2,1)S(1)}, u32[]{:S(2)}, u32[]{:S(2)}) collective-permute-start(bf16[256,384]{1,0:T(8,128)(2,1)S(1)} %get-tuple-element.79.a_1_), channel_id=1, source_target_pairs={{0,1},{1,0},{2,3},{3,2},{4,5},{5,4},{6,7},{7,6},{8,9},{9,8},{10,11... | collective-permute-start | bytes 589832 | tf_op jit(solution)/shard_map/ppermute | solution.py:432
  5.3 2.2 %collective-permute-start.1 = (bf16[256,384]{1,0:T(8,128)(2,1)S(1)}, bf16[256,384]{1,0:T(8,128)(2,1)S(1)}, u32[]{:S(2)}, u32[]{:S(2)}) collective-permute-start(bf16[256,384]{1,0:T(8,128)(2,1)S(1)} %get-tuple-element.79.a_1_), channel_id=1, source_target_pairs={{0,3},{1,2},{2,1},{3,0},{4,7},{5,6},{6,5},{7,4},{8,11},{9,10},{10,... | collective-permute-start | bytes 589832 | tf_op jit(solution)/shard_map/ppermute | solution.py:432
  8.0 2.2 %collective-permute-start.3 = (bf16[192,256]{1,0:T(8,128)(2,1)S(1)}, bf16[192,256]{1,0:T(8,128)(2,1)S(1)}, u32[]{:S(2)}, u32[]{:S(2)}) collective-permute-start(bf16[192,256]{1,0:T(8,128)(2,1)S(1)} %get-tuple-element.83), channel_id=1, source_target_pairs={{0,20},{1,21},{2,22},{3,23},{4,16},{5,17},{6,18},{7,19},{8,28},{9,... | collective-permute-start | bytes 294920 | tf_op jit(solution)/shard_map/ppermute | solution.py:444
  10.1 0.7 select_reduce_fusion.1
  10.9 1.7 %shard_map.94 = (bf16[256,1024]{1,0:T(8,128)(2,1)S(1)}, f32[256,1]{1,0:T(8,128)S(1)}) custom-call(s32[1,512]{1,0:T(1,128)S(1)} %bitcast.71, f32[1,512]{1,0:T(1,128)S(1)} %bitcast.72, bf16[512,1024]{1,0:T(8,128)(2,1)} %cot.1), custom_call_target="tpu_custom_call" | custom-call | flops 268435456 | bytes 2097152 | tf_op jit(solution)/shard_map/pallas_call | solution.py:71
  13.5 1.9 %collective-permute-start.4 = (bf16[256,384]{1,0:T(8,128)(2,1)S(1)}, bf16[256,384]{1,0:T(8,128)(2,1)S(1)}, u32[]{:S(2)}, u32[]{:S(2)}) collective-permute-start(bf16[256,384]{1,0:T(8,128)(2,1)S(1)} %collective-permute-done.a_3_), channel_id=1, source_target_pairs={{0,4},{1,5},{2,6},{3,7},{4,0},{5,1},{6,2},{7,3},{8,12},{9,13},{10,... | collective-permute-start | bytes 589832 | tf_op jit(solution)/shard_map/ppermute | solution.py:432
  15.5 1.2 %collective-permute-start.6 = (bf16[256,384]{1,0:T(8,128)(2,1)S(1)}, bf16[256,384]{1,0:T(8,128)(2,1)S(1)}, u32[]{:S(2)}, u32[]{:S(2)}) collective-permute-start(bf16[256,384]{1,0:T(8,128)(2,1)S(1)} %get-tuple-element.79.a_1_), channel_id=1, source_target_pairs={{0,2},{1,3},{2,0},{3,1},{4,6},{5,7},{6,4},{7,5},{8,10},{9,11},{10,... | collective-permute-start | bytes 589832 | tf_op jit(solution)/shard_map/ppermute | solution.py:432
  16.8 2.3 %collective-permute-start.7 = (bf16[256,384]{1,0:T(8,128)(2,1)S(1)}, bf16[256,384]{1,0:T(8,128)(2,1)S(1)}, u32[]{:S(2)}, u32[]{:S(2)}) collective-permute-start(bf16[256,384]{1,0:T(8,128)(2,1)S(1)} %collective-permute-done.2.a_2_), channel_id=1, source_target_pairs={{0,2},{1,3},{2,0},{3,1},{4,6},{5,7},{6,4},{7,5},{8,10},{9,11},{10,... | collective-permute-start | bytes 589832 | tf_op jit(solution)/shard_map/ppermute | solution.py:432
  19.1 2.8 %collective-permute-start.8 = (bf16[192,256]{1,0:T(8,128)(2,1)S(1)}, bf16[192,256]{1,0:T(8,128)(2,1)S(1)}, u32[]{:S(2)}, u32[]{:S(2)}) collective-permute-start(bf16[192,256]{1,0:T(8,128)(2,1)S(1)} %get-tuple-element.83), channel_id=1, source_target_pairs={{0,16},{8,24},{16,0},{24,8},{32,48},{40,56},{48,32},{56,40},{64,80... | collective-permute-start | bytes 294920 | tf_op jit(solution)/shard_map/ppermute | solution.py:435
  21.9 5.5 %shard_map.95 = (f32[256,1024]{1,0:T(8,128)S(1)}, f32[256,1024]{1,0:T(8,128)S(1)}, bf16[4,192,256]{2,1,0:T(8,128)(2,1)S(1)}, bf16[3072,1024]{1,0:T(8,128)(2,1)S(1)}, bf16[3072,1024]{1,0:T(8,128)(2,1)S(1)}) custom-call(s32[9]{0:T(128)S(1)} %stack.62.a_0_, bf16[256,384]{1,0:T(8,128)(2,1)S(1)} %get-tuple-element.79.a_1_, ...), custom_call_target="tpu_custom_call" | custom-call | flops 1610612736 | bytes 12582912 | tf_op jit(solution)/shard_map/pallas_call | solution.py:135
  27.4 4.0 %shard_map.96 = (bf16[256,512]{1,0:T(8,128)(2,1)S(1)}, bf16[256,512]{1,0:T(8,128)(2,1)S(1)}, bf16[256,512]{1,0:T(8,128)(2,1)S(1)}, bf16[256,512]{1,0:T(8,128)(2,...) custom-call(s32[4]{0:T(128)S(1)} %pad_add_fusion.info.a_0_, ...), custom_call_target="tpu_custom_call" | custom-call | flops 1610612736 | bytes 4194304 | tf_op jit(solution)/shard_map/pallas_call | solution.py:222
  32.7 2.5 %collective-permute-start.14 = (bf16[256,512]{1,0:T(8,128)(2,1)S(1)}, bf16[256,512]{1,0:T(8,128)(2,1)S(1)}, u32[]{:S(2)}, u32[]{:S(2)}) collective-permute-start(bf16[256,512]{1,0:T(8,128)(2,1)S(1)} %get-tuple-element.99.refs_0_), channel_id=1, source_target_pairs={{0,16},{8,24},{16,0},{24,8},{32,48},{40,56},{48,32},{56,40},{64,80... | collective-permute-start | bytes 786440 | tf_op jit(solution)/shard_map/ppermute | solution.py:435
  35.8 0.8 collective-permute-start.10
  36.6 1.8 %collective-permute-start.11 = (bf16[2,192,256]{2,1,0:T(8,128)(2,1)S(1)}, bf16[2,192,256]{2,1,0:T(8,128)(2,1)S(1)}, u32[]{:S(2)}, u32[]{:S(2)}) collective-permute-start(bf16[2,192,256]{2,1,0:T(8,128)(2,1)S(1)} %pad_maximum_fusion.refs_5_.a_1_), channel_id=1, source_target_pairs={{0,2},{1,3},{2,0},{3,1},{4,6},{5,7},{6,4},{7,5},{8,10},{9,11},{10,... | collective-permute-start | bytes 589832 | tf_op jit(solution)/shard_map/ppermute | solution.py:432
  38.4 2.2 %collective-permute-start.12 = (bf16[2,192,256]{2,1,0:T(8,128)(2,1)S(1)}, bf16[2,192,256]{2,1,0:T(8,128)(2,1)S(1)}, u32[]{:S(2)}, u32[]{:S(2)}) collective-permute-start(bf16[2,192,256]{2,1,0:T(8,128)(2,1)S(1)} %pad_maximum_fusion.refs_5_.a_1_), channel_id=1, source_target_pairs={{0,3},{1,2},{2,1},{3,0},{4,7},{5,6},{6,5},{7,4},{8,11},{9,10},{10,... | collective-permute-start | bytes 589832 | tf_op jit(solution)/shard_map/ppermute | solution.py:432
  41.2 5.9 %shard_map.97 = (f32[2,384,256]{2,1,0:T(8,128)S(1)}, bf16[2,400,256]{2,1,0:T(8,128)(2,1)S(1)}, bf16[2,400,256]{2,1,0:T(8,128)(2,1)S(1)}, bf16[2,400,256]{2,1,0:T(8,128)(2,1)S(1)}) custom-call(s32[4]{0:T(128)S(1)} %pad_add_fusion.info.a_0_, bf16[256,512]{1,0:T(8,128)(2,1)S(1)} %get-tuple-element.99.refs_0_, bf16[256,512]{1,0:T(8,128)(2,1)S(1)} %get-tuple-element.126.refs_1_, ...), custom_call_target="tpu_custom_call" | custom-call | flops 3221225472 | bytes 12582912 | tf_op jit(solution)/shard_map/pallas_call | solution.py:296
  47.7 2.6 %collective-permute-done.12.a_4_ = bf16[2,192,256]{2,1,0:T(8,128)(2,1)S(1)} collective-permute-done((bf16[2,192,256]{2,1,0:T(8,128)(2,1)S(1)}, bf16[2,192,256]{2,1,0:T(8,128)(2,1)S(1)}, u32[]{:S(2)}, u32[]{:S(2)}) %collective-permute-start.12) | collective-permute-done | bytes 196640 | tf_op jit(solution)/shard_map/ppermute | solution.py:432
  51.0 1.4 %collective-permute-start.22 = (bf16[256,512]{1,0:T(8,128)(2,1)S(1)}, bf16[256,512]{1,0:T(8,128)(2,1)S(1)}, u32[]{:S(2)}, u32[]{:S(2)}) collective-permute-start(bf16[256,512]{1,0:T(8,128)(2,1)S(1)} %get-tuple-element.127.refs_3_), channel_id=1, source_target_pairs={{0,24},{8,16},{16,8},{24,0},{32,56},{40,48},{48,40},{56,32},{64,88... | collective-permute-start | bytes 786440 | tf_op jit(solution)/shard_map/ppermute | solution.py:435
  52.5 2.3 %collective-permute-start.21 = (bf16[256,512]{1,0:T(8,128)(2,1)S(1)}, bf16[256,512]{1,0:T(8,128)(2,1)S(1)}, u32[]{:S(2)}, u32[]{:S(2)}) collective-permute-start(bf16[256,512]{1,0:T(8,128)(2,1)S(1)} %get-tuple-element.126.refs_1_), channel_id=1, source_target_pairs={{0,16},{8,24},{16,0},{24,8},{32,48},{40,56},{48,32},{56,40},{64,80... | collective-permute-start | bytes 786440 | tf_op jit(solution)/shard_map/ppermute | solution.py:435
  56.6 2.0 %collective-permute-start.18 = (bf16[192,512]{1,0:T(8,128)(2,1)S(1)}, bf16[192,512]{1,0:T(8,128)(2,1)S(1)}, u32[]{:S(2)}, u32[]{:S(2)}) collective-permute-start(bf16[192,512]{1,0:T(8,128)(2,1)S(1)} %get-tuple-element.123._.a_2_), channel_id=1, source_target_pairs={{0,32},{8,232},{16,48},{24,248},{32,64},{40,8},{48,80},{56,24},{64... | collective-permute-start | bytes 589832 | tf_op jit(solution)/shard_map/ppermute | solution.py:439
  58.7 4.0 %collective-permute-start.19 = (bf16[192,512]{1,0:T(8,128)(2,1)S(1)}, bf16[192,512]{1,0:T(8,128)(2,1)S(1)}, u32[]{:S(2)}, u32[]{:S(2)}) collective-permute-start(bf16[192,512]{1,0:T(8,128)(2,1)S(1)} %get-tuple-element.125), channel_id=1, source_target_pairs={{0,224},{8,40},{16,240},{24,56},{32,0},{40,72},{48,16},{56,88},{64... | collective-permute-start | bytes 589832 | tf_op jit(solution)/shard_map/ppermute | solution.py:439
  63.9 2.9 %collective-permute-done.21 = bf16[256,512]{1,0:T(8,128)(2,1)S(1)} collective-permute-done((bf16[256,512]{1,0:T(8,128)(2,1)S(1)}, bf16[256,512]{1,0:T(8,128)(2,1)S(1)}, u32[]{:S(2)}, u32[]{:S(2)}) %collective-permute-start.21) | collective-permute-done | bytes 262176 | tf_op jit(solution)/shard_map/ppermute | solution.py:435
  67.5 2.0 %collective-permute-start.28 = (bf16[192,512]{1,0:T(8,128)(2,1)S(1)}, bf16[192,512]{1,0:T(8,128)(2,1)S(1)}, u32[]{:S(2)}, u32[]{:S(2)}) collective-permute-start(bf16[192,512]{1,0:T(8,128)(2,1)S(1)} %get-tuple-element.128.a_4_), channel_id=1, source_target_pairs={{0,32},{8,232},{16,48},{24,248},{32,64},{40,8},{48,80},{56,24},{64... | collective-permute-start | bytes 589832 | tf_op jit(solution)/shard_map/ppermute | solution.py:439
  69.5 4.0 %collective-permute-start.29 = (bf16[192,512]{1,0:T(8,128)(2,1)S(1)}, bf16[192,512]{1,0:T(8,128)(2,1)S(1)}, u32[]{:S(2)}, u32[]{:S(2)}) collective-permute-start(bf16[192,512]{1,0:T(8,128)(2,1)S(1)} %get-tuple-element.134), channel_id=1, source_target_pairs={{0,224},{8,40},{16,240},{24,56},{32,0},{40,72},{48,16},{56,88},{64... | collective-permute-start | bytes 589832 | tf_op jit(solution)/shard_map/ppermute | solution.py:439
  73.6 2.3 %collective-permute-start.23 = (bf16[2,400,256]{2,1,0:T(8,128)(2,1)S(1)}, bf16[2,400,256]{2,1,0:T(8,128)(2,1)S(1)}, u32[]{:S(2)}, u32[]{:S(2)}) collective-permute-start(bf16[2,400,256]{2,1,0:T(8,128)(2,1)S(1)} %shard_map.104), channel_id=1, source_target_pairs={{0,3},{1,2},{2,1},{3,0},{4,7},{5,6},{6,5},{7,4},{8,11},{9,10},{10,... | collective-permute-start | bytes 1228808 | tf_op jit(solution)/shard_map/ppermute | solution.py:432
  76.0 1.5 %collective-permute-done.28.a_2_ = bf16[192,512]{1,0:T(8,128)(2,1)S(1)} collective-permute-done((bf16[192,512]{1,0:T(8,128)(2,1)S(1)}, bf16[192,512]{1,0:T(8,128)(2,1)S(1)}, u32[]{:S(2)}, u32[]{:S(2)}) %collective-permute-start.28) | collective-permute-done | bytes 196640 | tf_op jit(solution)/shard_map/ppermute | solution.py:439
  77.5 3.4 %collective-permute-start.27 = (bf16[192,512]{1,0:T(8,128)(2,1)S(1)}, bf16[192,512]{1,0:T(8,128)(2,1)S(1)}, u32[]{:S(2)}, u32[]{:S(2)}) collective-permute-start(bf16[192,512]{1,0:T(8,128)(2,1)S(1)} %get-tuple-element.133), channel_id=1, source_target_pairs={{0,224},{8,40},{16,240},{24,56},{32,0},{40,72},{48,16},{56,88},{64... | collective-permute-start | bytes 589832 | tf_op jit(solution)/shard_map/ppermute | solution.py:439
  81.8 4.0 %collective-permute-done.26.a_2_ = bf16[192,512]{1,0:T(8,128)(2,1)S(1)} collective-permute-done((bf16[192,512]{1,0:T(8,128)(2,1)S(1)}, bf16[192,512]{1,0:T(8,128)(2,1)S(1)}, u32[]{:S(2)}, u32[]{:S(2)}) %collective-permute-start.26) | collective-permute-done | bytes 196640 | tf_op jit(solution)/shard_map/ppermute | solution.py:439
  85.8 1.0 collective-permute-start.32
  86.8 0.7 shard_map.108
  87.6 1.0 collective-permute-start.30
  88.6 5.7 %collective-permute-done.23.third.a_5_ = bf16[2,400,256]{2,1,0:T(8,128)(2,1)S(1)} collective-permute-done((bf16[2,400,256]{2,1,0:T(8,128)(2,1)S(1)}, bf16[2,400,256]{2,1,0:T(8,128)(2,1)S(1)}, u32[]{:S(2)}, u32[]{:S(2)}) %collective-permute-start.23) | collective-permute-done | bytes 409632 | tf_op jit(solution)/shard_map/ppermute | solution.py:432
  94.3 2.9 %collective-permute-start.34 = (bf16[192,512]{1,0:T(8,128)(2,1)}, bf16[192,512]{1,0:T(8,128)(2,1)}, u32[]{:S(2)}, u32[]{:S(2)}) collective-permute-start(bf16[192,512]{1,0:T(8,128)(2,1)} %get-tuple-element.139), channel_id=1, source_target_pairs={{0,224},{8,40},{16,240},{24,56},{32,0},{40,72},{48,16},{56,88},{64... | collective-permute-start | bytes 589832 | tf_op jit(solution)/shard_map/ppermute | solution.py:439
  97.3 0.8 shard_map.109
  98.3 1.9 %collective-permute-start.33 = (bf16[192,512]{1,0:T(8,128)(2,1)S(1)}, bf16[192,512]{1,0:T(8,128)(2,1)}, u32[]{:S(2)}, u32[]{:S(2)}) collective-permute-start(bf16[192,512]{1,0:T(8,128)(2,1)S(1)} %shard_map.110.a_2_), channel_id=1, source_target_pairs={{0,32},{8,232},{16,48},{24,248},{32,64},{40,8},{48,80},{56,24},{64... | collective-permute-start | bytes 589832 | tf_op jit(solution)/shard_map/ppermute | solution.py:439
  100.3 1.8 %shard_map.106 = (f32[384,256]{1,0:T(8,128)S(1)}, f32[1,256]{1,0:T(1,128)S(1)}, bf16[400,256]{1,0:T(8,128)(2,1)S(1)}) custom-call(f32[2,384,256]{2,1,0:T(8,128)} %copy-done.5, f32[1,256]{1,0:T(1,128)} %copy-done.8, bf16[2,400,256]{2,1,0:T(8,128)(2,1)} %copy-done.2, bf16[2,400,256]{2,1,0:T(8,128)(2,1)} %copy-done.3, bf16[2,400,256]{2,1,0:T(8,128)(2,1)} %copy-done.4), custom_call_target="tpu_custom_call" | custom-call | flops 786432 | bytes 2949120 | tf_op jit(solution)/shard_map/pallas_call | solution.py:347
  102.1 1.3 %collective-permute-start.25 = (bf16[400,256]{1,0:T(8,128)(2,1)S(1)}, bf16[400,256]{1,0:T(8,128)(2,1)S(1)}, u32[]{:S(2)}, u32[]{:S(2)}) collective-permute-start(bf16[400,256]{1,0:T(8,128)(2,1)S(1)} %get-tuple-element.132.a_3_), channel_id=1, source_target_pairs={{0,4},{1,5},{2,6},{3,7},{4,0},{5,1},{6,2},{7,3},{8,12},{9,13},{10,... | collective-permute-start | bytes 614408 | tf_op jit(solution)/shard_map/ppermute | solution.py:432
  103.4 3.1 %collective-permute-done.36.a_1_ = bf16[192,512]{1,0:T(8,128)(2,1)} collective-permute-done((bf16[192,512]{1,0:T(8,128)(2,1)}, bf16[192,512]{1,0:T(8,128)(2,1)}, u32[]{:S(2)}, u32[]{:S(2)}) %collective-permute-start.36) | collective-permute-done | bytes 196640 | tf_op jit(solution)/shard_map/ppermute | solution.py:439
  106.4 1.9 %copy-done.1 = f32[1536,512]{1,0:T(8,128)S(1)} copy-done((f32[1536,512]{1,0:T(8,128)S(1)}, f32[1536,512]{1,0:T(8,128)}, u32[]{:S(2)}) %copy-start.1) | copy-done | bytes 3145752
  108.3 1.0 shard_map.111
  109.3 3.8 %collective-permute-start.37 = (bf16[192,512]{1,0:T(8,128)(2,1)S(1)}, bf16[192,512]{1,0:T(8,128)(2,1)S(1)}, u32[]{:S(2)}, u32[]{:S(2)}) collective-permute-start(bf16[192,512]{1,0:T(8,128)(2,1)S(1)} %shard_map.111), channel_id=1, source_target_pairs={{0,224},{8,40},{16,240},{24,56},{32,0},{40,72},{48,16},{56,88},{64... | collective-permute-start | bytes 589832 | tf_op jit(solution)/shard_map/ppermute | solution.py:439
  113.0 1.1 fusion.6
  114.2 0.7 select_reduce_fusion
  114.9 1.3 %collective-permute-done.37 = bf16[192,512]{1,0:T(8,128)(2,1)S(1)} collective-permute-done((bf16[192,512]{1,0:T(8,128)(2,1)S(1)}, bf16[192,512]{1,0:T(8,128)(2,1)S(1)}, u32[]{:S(2)}, u32[]{:S(2)}) %collective-permute-start.37) | collective-permute-done | bytes 196640 | tf_op jit(solution)/shard_map/ppermute | solution.py:439
  116.2 1.1 fusion.4
  117.4 1.1 convolution_convert_fusion
  118.9 0.8 broadcast_select_fusion
  (92 shorter events, 12.0 us)
Async XLA Ops:
  1.6 25.8 %copy-start.6 = (s32[512]{0:T(512)}, s32[512]{0:T(512)S(1)}, u32[]{:S(2)}) copy-start(s32[512]{0:T(512)S(1)} %convert_select_fusion) | copy-start | bytes 6148
  3.6 9.1 %collective-permute-start = (bf16[256,384]{1,0:T(8,128)(2,1)S(1)}, bf16[256,384]{1,0:T(8,128)(2,1)S(1)}, u32[]{:S(2)}, u32[]{:S(2)}) collective-permute-start(bf16[256,384]{1,0:T(8,128)(2,1)S(1)} %get-tuple-element.79.a_1_), channel_id=1, source_target_pairs={{0,1},{1,0},{2,3},{3,2},{4,5},{5,4},{6,7},{7,6},{8,9},{9,8},{10,11... | collective-permute-start | bytes 589832 | tf_op jit(solution)/shard_map/ppermute | solution.py:432
  5.3 7.6 %collective-permute-start.1 = (bf16[256,384]{1,0:T(8,128)(2,1)S(1)}, bf16[256,384]{1,0:T(8,128)(2,1)S(1)}, u32[]{:S(2)}, u32[]{:S(2)}) collective-permute-start(bf16[256,384]{1,0:T(8,128)(2,1)S(1)} %get-tuple-element.79.a_1_), channel_id=1, source_target_pairs={{0,3},{1,2},{2,1},{3,0},{4,7},{5,6},{6,5},{7,4},{8,11},{9,10},{10,... | collective-permute-start | bytes 589832 | tf_op jit(solution)/shard_map/ppermute | solution.py:432
  7.4 6.1 %collective-permute-start.2 = (bf16[256,384]{1,0:T(8,128)(2,1)S(1)}, bf16[256,384]{1,0:T(8,128)(2,1)S(1)}, u32[]{:S(2)}, u32[]{:S(2)}) collective-permute-start(bf16[256,384]{1,0:T(8,128)(2,1)S(1)} %get-tuple-element.79.a_1_), channel_id=1, source_target_pairs={{0,4},{1,5},{2,6},{3,7},{4,0},{5,1},{6,2},{7,3},{8,12},{9,13},{10,... | collective-permute-start | bytes 589832 | tf_op jit(solution)/shard_map/ppermute | solution.py:432
  8.0 4.7 %collective-permute-start.3 = (bf16[192,256]{1,0:T(8,128)(2,1)S(1)}, bf16[192,256]{1,0:T(8,128)(2,1)S(1)}, u32[]{:S(2)}, u32[]{:S(2)}) collective-permute-start(bf16[192,256]{1,0:T(8,128)(2,1)S(1)} %get-tuple-element.83), channel_id=1, source_target_pairs={{0,20},{1,21},{2,22},{3,23},{4,16},{5,17},{6,18},{7,19},{8,28},{9,... | collective-permute-start | bytes 294920 | tf_op jit(solution)/shard_map/ppermute | solution.py:444
  13.5 13.9 %collective-permute-start.4 = (bf16[256,384]{1,0:T(8,128)(2,1)S(1)}, bf16[256,384]{1,0:T(8,128)(2,1)S(1)}, u32[]{:S(2)}, u32[]{:S(2)}) collective-permute-start(bf16[256,384]{1,0:T(8,128)(2,1)S(1)} %collective-permute-done.a_3_), channel_id=1, source_target_pairs={{0,4},{1,5},{2,6},{3,7},{4,0},{5,1},{6,2},{7,3},{8,12},{9,13},{10,... | collective-permute-start | bytes 589832 | tf_op jit(solution)/shard_map/ppermute | solution.py:432
  15.4 12.0 %collective-permute-start.5 = (bf16[256,384]{1,0:T(8,128)(2,1)S(1)}, bf16[256,384]{1,0:T(8,128)(2,1)S(1)}, u32[]{:S(2)}, u32[]{:S(2)}) collective-permute-start(bf16[256,384]{1,0:T(8,128)(2,1)S(1)} %collective-permute-done.1.a_4_), channel_id=1, source_target_pairs={{0,4},{1,5},{2,6},{3,7},{4,0},{5,1},{6,2},{7,3},{8,12},{9,13},{10,... | collective-permute-start | bytes 589832 | tf_op jit(solution)/shard_map/ppermute | solution.py:432
  15.5 11.9 %collective-permute-start.6 = (bf16[256,384]{1,0:T(8,128)(2,1)S(1)}, bf16[256,384]{1,0:T(8,128)(2,1)S(1)}, u32[]{:S(2)}, u32[]{:S(2)}) collective-permute-start(bf16[256,384]{1,0:T(8,128)(2,1)S(1)} %get-tuple-element.79.a_1_), channel_id=1, source_target_pairs={{0,2},{1,3},{2,0},{3,1},{4,6},{5,7},{6,4},{7,5},{8,10},{9,11},{10,... | collective-permute-start | bytes 589832 | tf_op jit(solution)/shard_map/ppermute | solution.py:432
  16.8 10.6 %collective-permute-start.7 = (bf16[256,384]{1,0:T(8,128)(2,1)S(1)}, bf16[256,384]{1,0:T(8,128)(2,1)S(1)}, u32[]{:S(2)}, u32[]{:S(2)}) collective-permute-start(bf16[256,384]{1,0:T(8,128)(2,1)S(1)} %collective-permute-done.2.a_2_), channel_id=1, source_target_pairs={{0,2},{1,3},{2,0},{3,1},{4,6},{5,7},{6,4},{7,5},{8,10},{9,11},{10,... | collective-permute-start | bytes 589832 | tf_op jit(solution)/shard_map/ppermute | solution.py:432
  19.1 8.3 %collective-permute-start.8 = (bf16[192,256]{1,0:T(8,128)(2,1)S(1)}, bf16[192,256]{1,0:T(8,128)(2,1)S(1)}, u32[]{:S(2)}, u32[]{:S(2)}) collective-permute-start(bf16[192,256]{1,0:T(8,128)(2,1)S(1)} %get-tuple-element.83), channel_id=1, source_target_pairs={{0,16},{8,24},{16,0},{24,8},{32,48},{40,56},{48,32},{56,40},{64,80... | collective-permute-start | bytes 294920 | tf_op jit(solution)/shard_map/ppermute | solution.py:435
  31.4 9.8 %copy-start.8 = (f32[1,256]{1,0:T(1,128)}, f32[1,256]{1,0:T(1,128)S(1)}, u32[]{:S(2)}) copy-start(f32[1,256]{1,0:T(1,128)S(1)} %get-tuple-element.103.refs_4_.route) | copy-start | bytes 3076
  31.4 4.4 %collective-permute-start.9 = (bf16[8,192,256]{2,1,0:T(8,128)(2,1)S(1)}, bf16[8,192,256]{2,1,0:T(8,128)(2,1)S(1)}, u32[]{:S(2)}, u32[]{:S(2)}) collective-permute-start(bf16[8,192,256]{2,1,0:T(8,128)(2,1)S(1)} %get-tuple-element.97), channel_id=1, source_target_pairs={{0,8},{8,0},{16,24},{24,16},{32,40},{40,32},{48,56},{56,48},{64,72... | collective-permute-start | bytes 2359304 | tf_op jit(solution)/shard_map/ppermute | solution.py:435
  31.5 6.9 %collective-permute-start.13 = (bf16[256,512]{1,0:T(8,128)(2,1)S(1)}, bf16[256,512]{1,0:T(8,128)(2,1)S(1)}, u32[]{:S(2)}, u32[]{:S(2)}) collective-permute-start(bf16[256,512]{1,0:T(8,128)(2,1)S(1)} %get-tuple-element.101.refs_2_), channel_id=1, source_target_pairs={{0,8},{8,0},{16,24},{24,16},{32,40},{40,32},{48,56},{56,48},{64,72... | collective-permute-start | bytes 786440 | tf_op jit(solution)/shard_map/ppermute | solution.py:435
  32.0 19.0 %collective-permute-start.15 = (bf16[256,512]{1,0:T(8,128)(2,1)S(1)}, bf16[256,512]{1,0:T(8,128)(2,1)S(1)}, u32[]{:S(2)}, u32[]{:S(2)}) collective-permute-start(bf16[256,512]{1,0:T(8,128)(2,1)S(1)} %get-tuple-element.101.refs_2_), channel_id=1, source_target_pairs={{0,24},{8,16},{16,8},{24,0},{32,56},{40,48},{48,40},{56,32},{64,88... | collective-permute-start | bytes 786440 | tf_op jit(solution)/shard_map/ppermute | solution.py:435
  32.7 18.3 %collective-permute-start.14 = (bf16[256,512]{1,0:T(8,128)(2,1)S(1)}, bf16[256,512]{1,0:T(8,128)(2,1)S(1)}, u32[]{:S(2)}, u32[]{:S(2)}) collective-permute-start(bf16[256,512]{1,0:T(8,128)(2,1)S(1)} %get-tuple-element.99.refs_0_), channel_id=1, source_target_pairs={{0,16},{8,24},{16,0},{24,8},{32,48},{40,56},{48,32},{56,40},{64,80... | collective-permute-start | bytes 786440 | tf_op jit(solution)/shard_map/ppermute | solution.py:435
  35.8 11.3 %collective-permute-start.10 = (bf16[2,192,256]{2,1,0:T(8,128)(2,1)S(1)}, bf16[2,192,256]{2,1,0:T(8,128)(2,1)S(1)}, u32[]{:S(2)}, u32[]{:S(2)}) collective-permute-start(bf16[2,192,256]{2,1,0:T(8,128)(2,1)S(1)} %pad_maximum_fusion.refs_5_.a_1_), channel_id=1, source_target_pairs={{0,1},{1,0},{2,3},{3,2},{4,5},{5,4},{6,7},{7,6},{8,9},{9,8},{10,11... | collective-permute-start | bytes 589832 | tf_op jit(solution)/shard_map/ppermute | solution.py:432
  36.6 11.1 %collective-permute-start.11 = (bf16[2,192,256]{2,1,0:T(8,128)(2,1)S(1)}, bf16[2,192,256]{2,1,0:T(8,128)(2,1)S(1)}, u32[]{:S(2)}, u32[]{:S(2)}) collective-permute-start(bf16[2,192,256]{2,1,0:T(8,128)(2,1)S(1)} %pad_maximum_fusion.refs_5_.a_1_), channel_id=1, source_target_pairs={{0,2},{1,3},{2,0},{3,1},{4,6},{5,7},{6,4},{7,5},{8,10},{9,11},{10,... | collective-permute-start | bytes 589832 | tf_op jit(solution)/shard_map/ppermute | solution.py:432
  38.4 11.8 %collective-permute-start.12 = (bf16[2,192,256]{2,1,0:T(8,128)(2,1)S(1)}, bf16[2,192,256]{2,1,0:T(8,128)(2,1)S(1)}, u32[]{:S(2)}, u32[]{:S(2)}) collective-permute-start(bf16[2,192,256]{2,1,0:T(8,128)(2,1)S(1)} %pad_maximum_fusion.refs_5_.a_1_), channel_id=1, source_target_pairs={{0,3},{1,2},{2,1},{3,0},{4,7},{5,6},{6,5},{7,4},{8,11},{9,10},{10,... | collective-permute-start | bytes 589832 | tf_op jit(solution)/shard_map/ppermute | solution.py:432
  47.1 8.8 %copy-start.5 = (f32[2,384,256]{2,1,0:T(8,128)}, f32[2,384,256]{2,1,0:T(8,128)S(1)}, u32[]{:S(2)}) copy-start(f32[2,384,256]{2,1,0:T(8,128)S(1)} %get-tuple-element.110.own) | copy-start | bytes 2359300
  50.9 5.0 %collective-permute-start.16 = (bf16[8,192,256]{2,1,0:T(8,128)(2,1)S(1)}, bf16[8,192,256]{2,1,0:T(8,128)(2,1)S(1)}, u32[]{:S(2)}, u32[]{:S(2)}) collective-permute-start(bf16[8,192,256]{2,1,0:T(8,128)(2,1)S(1)} %get-tuple-element.121), channel_id=1, source_target_pairs={{0,8},{8,0},{16,24},{24,16},{32,40},{40,32},{48,56},{56,48},{64,72... | collective-permute-start | bytes 2359304 | tf_op jit(solution)/shard_map/ppermute | solution.py:435
  51.0 12.3 %collective-permute-start.22 = (bf16[256,512]{1,0:T(8,128)(2,1)S(1)}, bf16[256,512]{1,0:T(8,128)(2,1)S(1)}, u32[]{:S(2)}, u32[]{:S(2)}) collective-permute-start(bf16[256,512]{1,0:T(8,128)(2,1)S(1)} %get-tuple-element.127.refs_3_), channel_id=1, source_target_pairs={{0,24},{8,16},{16,8},{24,0},{32,56},{40,48},{48,40},{56,32},{64,88... | collective-permute-start | bytes 786440 | tf_op jit(solution)/shard_map/ppermute | solution.py:435
  52.4 2.9 %collective-permute-start.20 = (bf16[256,512]{1,0:T(8,128)(2,1)S(1)}, bf16[256,512]{1,0:T(8,128)(2,1)S(1)}, u32[]{:S(2)}, u32[]{:S(2)}) collective-permute-start(bf16[256,512]{1,0:T(8,128)(2,1)S(1)} %get-tuple-element.127.refs_3_), channel_id=1, source_target_pairs={{0,8},{8,0},{16,24},{24,16},{32,40},{40,32},{48,56},{56,48},{64,72... | collective-permute-start | bytes 786440 | tf_op jit(solution)/shard_map/ppermute | solution.py:435
  52.5 14.3 %collective-permute-start.21 = (bf16[256,512]{1,0:T(8,128)(2,1)S(1)}, bf16[256,512]{1,0:T(8,128)(2,1)S(1)}, u32[]{:S(2)}, u32[]{:S(2)}) collective-permute-start(bf16[256,512]{1,0:T(8,128)(2,1)S(1)} %get-tuple-element.126.refs_1_), channel_id=1, source_target_pairs={{0,16},{8,24},{16,0},{24,8},{32,48},{40,56},{48,32},{56,40},{64,80... | collective-permute-start | bytes 786440 | tf_op jit(solution)/shard_map/ppermute | solution.py:435
  56.6 16.9 %collective-permute-start.18 = (bf16[192,512]{1,0:T(8,128)(2,1)S(1)}, bf16[192,512]{1,0:T(8,128)(2,1)S(1)}, u32[]{:S(2)}, u32[]{:S(2)}) collective-permute-start(bf16[192,512]{1,0:T(8,128)(2,1)S(1)} %get-tuple-element.123._.a_2_), channel_id=1, source_target_pairs={{0,32},{8,232},{16,48},{24,248},{32,64},{40,8},{48,80},{56,24},{64... | collective-permute-start | bytes 589832 | tf_op jit(solution)/shard_map/ppermute | solution.py:439
  58.6 22.4 %collective-permute-start.17 = (bf16[2,400,256]{2,1,0:T(8,128)(2,1)S(1)}, bf16[2,400,256]{2,1,0:T(8,128)(2,1)S(1)}, u32[]{:S(2)}, u32[]{:S(2)}) collective-permute-start(bf16[2,400,256]{2,1,0:T(8,128)(2,1)S(1)} %shard_map.100), channel_id=1, source_target_pairs={{0,1},{1,0},{2,3},{3,2},{4,5},{5,4},{6,7},{7,6},{8,9},{9,8},{10,11... | collective-permute-start | bytes 1228808 | tf_op jit(solution)/shard_map/ppermute | solution.py:432
  58.7 14.8 %collective-permute-start.19 = (bf16[192,512]{1,0:T(8,128)(2,1)S(1)}, bf16[192,512]{1,0:T(8,128)(2,1)S(1)}, u32[]{:S(2)}, u32[]{:S(2)}) collective-permute-start(bf16[192,512]{1,0:T(8,128)(2,1)S(1)} %get-tuple-element.125), channel_id=1, source_target_pairs={{0,224},{8,40},{16,240},{24,56},{32,0},{40,72},{48,16},{56,88},{64... | collective-permute-start | bytes 589832 | tf_op jit(solution)/shard_map/ppermute | solution.py:439
  67.4 29.8 %copy-start = (f32[1536,512]{1,0:T(8,128)}, f32[1536,512]{1,0:T(8,128)S(1)}, u32[]{:S(2)}) copy-start(f32[1536,512]{1,0:T(8,128)S(1)} %fusion) | copy-start | bytes 9437188
  67.5 10.1 %collective-permute-start.28 = (bf16[192,512]{1,0:T(8,128)(2,1)S(1)}, bf16[192,512]{1,0:T(8,128)(2,1)S(1)}, u32[]{:S(2)}, u32[]{:S(2)}) collective-permute-start(bf16[192,512]{1,0:T(8,128)(2,1)S(1)} %get-tuple-element.128.a_4_), channel_id=1, source_target_pairs={{0,32},{8,232},{16,48},{24,248},{32,64},{40,8},{48,80},{56,24},{64... | collective-permute-start | bytes 589832 | tf_op jit(solution)/shard_map/ppermute | solution.py:439
  69.5 8.1 %collective-permute-start.29 = (bf16[192,512]{1,0:T(8,128)(2,1)S(1)}, bf16[192,512]{1,0:T(8,128)(2,1)S(1)}, u32[]{:S(2)}, u32[]{:S(2)}) collective-permute-start(bf16[192,512]{1,0:T(8,128)(2,1)S(1)} %get-tuple-element.134), channel_id=1, source_target_pairs={{0,224},{8,40},{16,240},{24,56},{32,0},{40,72},{48,16},{56,88},{64... | collective-permute-start | bytes 589832 | tf_op jit(solution)/shard_map/ppermute | solution.py:439
  73.6 20.7 %collective-permute-start.23 = (bf16[2,400,256]{2,1,0:T(8,128)(2,1)S(1)}, bf16[2,400,256]{2,1,0:T(8,128)(2,1)S(1)}, u32[]{:S(2)}, u32[]{:S(2)}) collective-permute-start(bf16[2,400,256]{2,1,0:T(8,128)(2,1)S(1)} %shard_map.104), channel_id=1, source_target_pairs={{0,3},{1,2},{2,1},{3,0},{4,7},{5,6},{6,5},{7,4},{8,11},{9,10},{10,... | collective-permute-start | bytes 1228808 | tf_op jit(solution)/shard_map/ppermute | solution.py:432
  75.9 21.3 %collective-permute-start.24 = (bf16[2,400,256]{2,1,0:T(8,128)(2,1)S(1)}, bf16[2,400,256]{2,1,0:T(8,128)(2,1)S(1)}, u32[]{:S(2)}, u32[]{:S(2)}) collective-permute-start(bf16[2,400,256]{2,1,0:T(8,128)(2,1)S(1)} %shard_map.105), channel_id=1, source_target_pairs={{0,2},{1,3},{2,0},{3,1},{4,6},{5,7},{6,4},{7,5},{8,10},{9,11},{10,... | collective-permute-start | bytes 1228808 | tf_op jit(solution)/shard_map/ppermute | solution.py:432
  77.5 8.3 %collective-permute-start.26 = (bf16[192,512]{1,0:T(8,128)(2,1)S(1)}, bf16[192,512]{1,0:T(8,128)(2,1)S(1)}, u32[]{:S(2)}, u32[]{:S(2)}) collective-permute-start(bf16[192,512]{1,0:T(8,128)(2,1)S(1)} %get-tuple-element.129._.a_4_), channel_id=1, source_target_pairs={{0,32},{8,232},{16,48},{24,248},{32,64},{40,8},{48,80},{56,24},{64... | collective-permute-start | bytes 589832 | tf_op jit(solution)/shard_map/ppermute | solution.py:439
  77.5 9.3 %collective-permute-start.27 = (bf16[192,512]{1,0:T(8,128)(2,1)S(1)}, bf16[192,512]{1,0:T(8,128)(2,1)S(1)}, u32[]{:S(2)}, u32[]{:S(2)}) collective-permute-start(bf16[192,512]{1,0:T(8,128)(2,1)S(1)} %get-tuple-element.133), channel_id=1, source_target_pairs={{0,224},{8,40},{16,240},{24,56},{32,0},{40,72},{48,16},{56,88},{64... | collective-permute-start | bytes 589832 | tf_op jit(solution)/shard_map/ppermute | solution.py:439
  81.0 0.8 copy-start.2
  81.8 15.5 %collective-permute-start.31 = (bf16[192,512]{1,0:T(8,128)(2,1)S(1)}, bf16[192,512]{1,0:T(8,128)(2,1)S(1)}, u32[]{:S(2)}, u32[]{:S(2)}) collective-permute-start(bf16[192,512]{1,0:T(8,128)(2,1)S(1)} %get-tuple-element.135.a_4_), channel_id=1, source_target_pairs={{0,32},{8,232},{16,48},{24,248},{32,64},{40,8},{48,80},{56,24},{64... | collective-permute-start | bytes 589832 | tf_op jit(solution)/shard_map/ppermute | solution.py:439
  85.8 11.5 %collective-permute-start.32 = (bf16[192,512]{1,0:T(8,128)(2,1)S(1)}, bf16[192,512]{1,0:T(8,128)(2,1)S(1)}, u32[]{:S(2)}, u32[]{:S(2)}) collective-permute-start(bf16[192,512]{1,0:T(8,128)(2,1)S(1)} %get-tuple-element.137), channel_id=1, source_target_pairs={{0,224},{8,40},{16,240},{24,56},{32,0},{40,72},{48,16},{56,88},{64... | collective-permute-start | bytes 589832 | tf_op jit(solution)/shard_map/ppermute | solution.py:439
  87.6 10.7 %collective-permute-start.30 = (bf16[192,512]{1,0:T(8,128)(2,1)S(1)}, bf16[192,512]{1,0:T(8,128)(2,1)S(1)}, u32[]{:S(2)}, u32[]{:S(2)}) collective-permute-start(bf16[192,512]{1,0:T(8,128)(2,1)S(1)} %get-tuple-element.136.a_4_), channel_id=1, source_target_pairs={{0,32},{8,232},{16,48},{24,248},{32,64},{40,8},{48,80},{56,24},{64... | collective-permute-start | bytes 589832 | tf_op jit(solution)/shard_map/ppermute | solution.py:439
  94.3 3.8 %copy-start.3 = (bf16[2,400,256]{2,1,0:T(8,128)(2,1)}, bf16[2,400,256]{2,1,0:T(8,128)(2,1)S(1)}, u32[]{:S(2)}) copy-start(bf16[2,400,256]{2,1,0:T(8,128)(2,1)S(1)} %collective-permute-done.23.third.a_5_) | copy-start | bytes 1228804
  94.3 18.8 %collective-permute-start.34 = (bf16[192,512]{1,0:T(8,128)(2,1)}, bf16[192,512]{1,0:T(8,128)(2,1)}, u32[]{:S(2)}, u32[]{:S(2)}) collective-permute-start(bf16[192,512]{1,0:T(8,128)(2,1)} %get-tuple-element.139), channel_id=1, source_target_pairs={{0,224},{8,40},{16,240},{24,56},{32,0},{40,72},{48,16},{56,88},{64... | collective-permute-start | bytes 589832 | tf_op jit(solution)/shard_map/ppermute | solution.py:439
  97.2 0.8 copy-start.4
  98.1 8.4 %collective-permute-start.36 = (bf16[192,512]{1,0:T(8,128)(2,1)}, bf16[192,512]{1,0:T(8,128)(2,1)}, u32[]{:S(2)}, u32[]{:S(2)}) collective-permute-start(bf16[192,512]{1,0:T(8,128)(2,1)} %get-tuple-element.140), channel_id=1, source_target_pairs={{0,224},{8,40},{16,240},{24,56},{32,0},{40,72},{48,16},{56,88},{64... | collective-permute-start | bytes 589832 | tf_op jit(solution)/shard_map/ppermute | solution.py:439
  98.3 14.8 %collective-permute-start.33 = (bf16[192,512]{1,0:T(8,128)(2,1)S(1)}, bf16[192,512]{1,0:T(8,128)(2,1)}, u32[]{:S(2)}, u32[]{:S(2)}) collective-permute-start(bf16[192,512]{1,0:T(8,128)(2,1)S(1)} %shard_map.110.a_2_), channel_id=1, source_target_pairs={{0,32},{8,232},{16,48},{24,248},{32,64},{40,8},{48,80},{56,24},{64... | collective-permute-start | bytes 589832 | tf_op jit(solution)/shard_map/ppermute | solution.py:439
  100.2 14.0 %copy-start.7 = (s32[512]{0:T(512)S(1)}, s32[512]{0:T(512)}, u32[]{:S(2)}) copy-start(s32[512]{0:T(512)} %copy-done.6) | copy-start | bytes 6148
  100.2 14.7 %collective-permute-start.35 = (bf16[192,512]{1,0:T(8,128)(2,1)S(1)}, bf16[192,512]{1,0:T(8,128)(2,1)S(1)}, u32[]{:S(2)}, u32[]{:S(2)}) collective-permute-start(bf16[192,512]{1,0:T(8,128)(2,1)S(1)} %get-tuple-element.138.a_2_), channel_id=1, source_target_pairs={{0,32},{8,232},{16,48},{24,248},{32,64},{40,8},{48,80},{56,24},{64... | collective-permute-start | bytes 589832 | tf_op jit(solution)/shard_map/ppermute | solution.py:439
  102.1 12.1 %collective-permute-start.25 = (bf16[400,256]{1,0:T(8,128)(2,1)S(1)}, bf16[400,256]{1,0:T(8,128)(2,1)S(1)}, u32[]{:S(2)}, u32[]{:S(2)}) collective-permute-start(bf16[400,256]{1,0:T(8,128)(2,1)S(1)} %get-tuple-element.132.a_3_), channel_id=1, source_target_pairs={{0,4},{1,5},{2,6},{3,7},{4,0},{5,1},{6,2},{7,3},{8,12},{9,13},{10,... | collective-permute-start | bytes 614408 | tf_op jit(solution)/shard_map/ppermute | solution.py:432
  106.4 1.9 %copy-start.1 = (f32[1536,512]{1,0:T(8,128)S(1)}, f32[1536,512]{1,0:T(8,128)}, u32[]{:S(2)}) copy-start(f32[1536,512]{1,0:T(8,128)} %copy-done) | copy-start | bytes 9437188
  109.3 7.0 %collective-permute-start.37 = (bf16[192,512]{1,0:T(8,128)(2,1)S(1)}, bf16[192,512]{1,0:T(8,128)(2,1)S(1)}, u32[]{:S(2)}, u32[]{:S(2)}) collective-permute-start(bf16[192,512]{1,0:T(8,128)(2,1)S(1)} %shard_map.111), channel_id=1, source_target_pairs={{0,224},{8,40},{16,240},{24,56},{32,0},{40,72},{48,16},{56,88},{64... | collective-permute-start | bytes 589832 | tf_op jit(solution)/shard_map/ppermute | solution.py:439
  117.3 1.5 %collective-permute-start.38 = (bf16[96,1024]{1,0:T(8,128)(2,1)S(1)}, bf16[96,1024]{1,0:T(8,128)(2,1)S(1)}, u32[]{:S(2)}, u32[]{:S(2)}) collective-permute-start(bf16[96,1024]{1,0:T(8,128)(2,1)S(1)} %fusion.10), channel_id=1, source_target_pairs={{0,8},{8,0},{16,24},{24,16},{32,40},{40,32},{48,56},{56,48},{64,72... | collective-permute-start | bytes 589832 | tf_op jit(solution)/shard_map/ppermute | solution.py:435

commit v5 on v4

--- a/solution.py
+++ b/solution.py
@@ -548,7 +548,6 @@
         waited = rings[0].hop(i, [waited])
         if i == 1:
             sums[3] = over_tensor(after(sent[1], waited), 3)
-            sums[2] = over_tensor(after(sent[2], waited), 2)
         if i == 3:
             parts = [sums[1], sums[3], sums[2]]
             in_hbm = lambda a: pltpu.with_memory_space_constraint(a, pltpu.HBM)
@@ -556,8 +555,10 @@
                 in_hbm(own_part), in_hbm(route_part), [in_hbm(a) for a in parts]
             )
         for ring in rings[1:]:
-            needed = ([sums[1]], [sums[3], sums[2]], [message] if i == 3 else [])[i - 1]
+            needed = ([sums[1]], [sums[3]], [message] if i == 3 else [])[i - 1]
             waited = ring.hop(i, [waited, *needed])
+        if i == 1:
+            sums[2] = over_tensor(after(sent[2], waited), 2)
     whole_rows = jnp.concatenate([ring.finish() for ring in rings], axis=2)
     kept = lax.dynamic_index_in_dim(whole_rows, core, 0, keepdims=False)
     swapped = over_dp(lax.dynamic_index_in_dim(whole_rows, 1 - core, 0, keepdims=False), 1)

time: 122 us -> 118 us (0.967); the launches traced: 120 us -> 118 us
  local copies, waits for them, and re-layouts: 2.69 us -> 0.79 us
    ppermute x14, waiting for transfers between devices: 9.64 us -> 14.8 us  [over_tensor(): return lax.ppermute(x, 'tensor', [(i, i ^ k) for i in range(n_tensor)])]
    ppermute x14, waiting for transfers between devices: 9.92 us -> 5.75 us  [along_z(): return lax.ppermute(x, 'dp', pairs)]
    unnamed x18 -> x14, local copies, waits for them, and re-layouts: 2.59 us -> 0.7 us
  transfers between devices with their start and end apart: 39 -> 39, of which waited for: 12 -> 12; matrix products, arithmetic and copies ran while one was open for 7% -> 7% of each run, Pallas kernels for 15% -> 16%
where the time goes in v5:
time: 118 us
  starting transfers between devices  57.5 us (49%)
  Pallas kernels  25 us (21%)
  waiting for transfers between devices  23.4 us (20%)
  matrix products  5.92 us (5%)
  other arithmetic  4.44 us (4%)
    ppermute x14, starting transfers between devices, along_z(): return lax.ppermute(x, 'dp', pairs)  26 us
    ppermute x14, starting transfers between devices, over_tensor(): return lax.ppermute(x, 'tensor', [(i, i ^ k) for i in range(n_tensor)])  18.9 us
    ppermute x14, waiting for transfers between devices, over_tensor(): return lax.ppermute(x, 'tensor', [(i, i ^ k) for i in range(n_tensor)])  14.8 us
    ppermute x10, starting transfers between devices, over_dp(): return lax.ppermute(x, 'dp', [(i, i ^ k) for i in range(n_dp)])  10.5 us
    pallas_call x1, Pallas kernels, token_parts(): pl.pallas_call(back_kernel, grid_spec=pltpu.PrefetchScalarGridSpec(num_sc...  5.93 us
    ppermute x14, waiting for transfers between devices, along_z(): return lax.ppermute(x, 'dp', pairs)  5.75 us
    pallas_call x1, Pallas kernels, early(): pl.pallas_call(lambda *a: early_kernel(n, *a), grid_spec=pltpu.PrefetchSc...  5.45 us
    dot_general x8, matrix products, product(): return jnp.dot(a.reshape(n_z * half, CAP), b, preferred_element_type=F32)  4.64 us
  transfers between devices with their start and end apart: 39, of which 12 were waited for; matrix products, arithmetic and copies ran while one was open for 7% of the time, Pallas kernels for 16%

profile of v5, /device:TPU:2, one launch (start us, length us, event | category | flops | bytes accessed | tf_op | source)
XLA Modules:
  0.0 118.2 jit_solution(1633035757133340410)
XLA Ops:
  0.7 0.7 fusion.14
  1.7 1.9 %shard_map.93 = (bf16[256,384]{1,0:T(8,128)(2,1)S(1)}, bf16[192,256]{1,0:T(8,128)(2,1)S(1)}) custom-call(s32[4]{0:T(128)S(1)} %pad_add_fusion.info.a_0_, s32[1,512]{1,0:T(1,128)S(1)} %bitcast.70, bf16[512,384]{1,0:T(8,128)(2,1)} %tokens.1), custom_call_target="tpu_custom_call" | custom-call | flops 100663296 | bytes 786432 | tf_op jit(solution)/shard_map/pallas_call | solution.py:41
  3.6 1.7 %collective-permute-start = (bf16[256,384]{1,0:T(8,128)(2,1)S(1)}, bf16[256,384]{1,0:T(8,128)(2,1)S(1)}, u32[]{:S(2)}, u32[]{:S(2)}) collective-permute-start(bf16[256,384]{1,0:T(8,128)(2,1)S(1)} %get-tuple-element.79.a_1_), channel_id=1, source_target_pairs={{0,1},{1,0},{2,3},{3,2},{4,5},{5,4},{6,7},{7,6},{8,9},{9,8},{10,11... | collective-permute-start | bytes 589832 | tf_op jit(solution)/shard_map/ppermute | solution.py:432
  5.3 2.2 %collective-permute-start.1 = (bf16[256,384]{1,0:T(8,128)(2,1)S(1)}, bf16[256,384]{1,0:T(8,128)(2,1)S(1)}, u32[]{:S(2)}, u32[]{:S(2)}) collective-permute-start(bf16[256,384]{1,0:T(8,128)(2,1)S(1)} %get-tuple-element.79.a_1_), channel_id=1, source_target_pairs={{0,3},{1,2},{2,1},{3,0},{4,7},{5,6},{6,5},{7,4},{8,11},{9,10},{10,... | collective-permute-start | bytes 589832 | tf_op jit(solution)/shard_map/ppermute | solution.py:432
  8.0 2.2 %collective-permute-start.3 = (bf16[192,256]{1,0:T(8,128)(2,1)S(1)}, bf16[192,256]{1,0:T(8,128)(2,1)S(1)}, u32[]{:S(2)}, u32[]{:S(2)}) collective-permute-start(bf16[192,256]{1,0:T(8,128)(2,1)S(1)} %get-tuple-element.83), channel_id=1, source_target_pairs={{0,20},{1,21},{2,22},{3,23},{4,16},{5,17},{6,18},{7,19},{8,28},{9,... | collective-permute-start | bytes 294920 | tf_op jit(solution)/shard_map/ppermute | solution.py:444
  10.1 0.7 select_reduce_fusion.1
  10.9 1.7 %shard_map.94 = (bf16[256,1024]{1,0:T(8,128)(2,1)S(1)}, f32[256,1]{1,0:T(8,128)S(1)}) custom-call(s32[1,512]{1,0:T(1,128)S(1)} %bitcast.71, f32[1,512]{1,0:T(1,128)S(1)} %bitcast.72, bf16[512,1024]{1,0:T(8,128)(2,1)} %cot.1), custom_call_target="tpu_custom_call" | custom-call | flops 268435456 | bytes 2097152 | tf_op jit(solution)/shard_map/pallas_call | solution.py:71
  13.5 1.9 %collective-permute-start.4 = (bf16[256,384]{1,0:T(8,128)(2,1)S(1)}, bf16[256,384]{1,0:T(8,128)(2,1)S(1)}, u32[]{:S(2)}, u32[]{:S(2)}) collective-permute-start(bf16[256,384]{1,0:T(8,128)(2,1)S(1)} %collective-permute-done.a_3_), channel_id=1, source_target_pairs={{0,4},{1,5},{2,6},{3,7},{4,0},{5,1},{6,2},{7,3},{8,12},{9,13},{10,... | collective-permute-start | bytes 589832 | tf_op jit(solution)/shard_map/ppermute | solution.py:432
  15.5 1.2 %collective-permute-start.6 = (bf16[256,384]{1,0:T(8,128)(2,1)S(1)}, bf16[256,384]{1,0:T(8,128)(2,1)S(1)}, u32[]{:S(2)}, u32[]{:S(2)}) collective-permute-start(bf16[256,384]{1,0:T(8,128)(2,1)S(1)} %get-tuple-element.79.a_1_), channel_id=1, source_target_pairs={{0,2},{1,3},{2,0},{3,1},{4,6},{5,7},{6,4},{7,5},{8,10},{9,11},{10,... | collective-permute-start | bytes 589832 | tf_op jit(solution)/shard_map/ppermute | solution.py:432
  16.8 2.3 %collective-permute-start.7 = (bf16[256,384]{1,0:T(8,128)(2,1)S(1)}, bf16[256,384]{1,0:T(8,128)(2,1)S(1)}, u32[]{:S(2)}, u32[]{:S(2)}) collective-permute-start(bf16[256,384]{1,0:T(8,128)(2,1)S(1)} %collective-permute-done.2.a_2_), channel_id=1, source_target_pairs={{0,2},{1,3},{2,0},{3,1},{4,6},{5,7},{6,4},{7,5},{8,10},{9,11},{10,... | collective-permute-start | bytes 589832 | tf_op jit(solution)/shard_map/ppermute | solution.py:432
  19.1 2.8 %collective-permute-start.8 = (bf16[192,256]{1,0:T(8,128)(2,1)S(1)}, bf16[192,256]{1,0:T(8,128)(2,1)S(1)}, u32[]{:S(2)}, u32[]{:S(2)}) collective-permute-start(bf16[192,256]{1,0:T(8,128)(2,1)S(1)} %get-tuple-element.83), channel_id=1, source_target_pairs={{0,16},{8,24},{16,0},{24,8},{32,48},{40,56},{48,32},{56,40},{64,80... | collective-permute-start | bytes 294920 | tf_op jit(solution)/shard_map/ppermute | solution.py:435
  21.9 5.5 %shard_map.95 = (f32[256,1024]{1,0:T(8,128)S(1)}, f32[256,1024]{1,0:T(8,128)S(1)}, bf16[4,192,256]{2,1,0:T(8,128)(2,1)S(1)}, bf16[3072,1024]{1,0:T(8,128)(2,1)S(1)}, bf16[3072,1024]{1,0:T(8,128)(2,1)S(1)}) custom-call(s32[9]{0:T(128)S(1)} %stack.62.a_0_, bf16[256,384]{1,0:T(8,128)(2,1)S(1)} %get-tuple-element.79.a_1_, ...), custom_call_target="tpu_custom_call" | custom-call | flops 1610612736 | bytes 12582912 | tf_op jit(solution)/shard_map/pallas_call | solution.py:135
  27.4 4.0 %shard_map.96 = (bf16[256,512]{1,0:T(8,128)(2,1)S(1)}, bf16[256,512]{1,0:T(8,128)(2,1)S(1)}, bf16[256,512]{1,0:T(8,128)(2,1)S(1)}, bf16[256,512]{1,0:T(8,128)(2,...) custom-call(s32[4]{0:T(128)S(1)} %pad_add_fusion.info.a_0_, ...), custom_call_target="tpu_custom_call" | custom-call | flops 1610612736 | bytes 4194304 | tf_op jit(solution)/shard_map/pallas_call | solution.py:222
  32.0 0.7 collective-permute-start.15
  32.7 2.5 %collective-permute-start.14 = (bf16[256,512]{1,0:T(8,128)(2,1)S(1)}, bf16[256,512]{1,0:T(8,128)(2,1)S(1)}, u32[]{:S(2)}, u32[]{:S(2)}) collective-permute-start(bf16[256,512]{1,0:T(8,128)(2,1)S(1)} %get-tuple-element.99.refs_0_), channel_id=1, source_target_pairs={{0,16},{8,24},{16,0},{24,8},{32,48},{40,56},{48,32},{56,40},{64,80... | collective-permute-start | bytes 786440 | tf_op jit(solution)/shard_map/ppermute | solution.py:435
  35.8 0.8 collective-permute-start.10
  36.6 1.8 %collective-permute-start.11 = (bf16[2,192,256]{2,1,0:T(8,128)(2,1)S(1)}, bf16[2,192,256]{2,1,0:T(8,128)(2,1)S(1)}, u32[]{:S(2)}, u32[]{:S(2)}) collective-permute-start(bf16[2,192,256]{2,1,0:T(8,128)(2,1)S(1)} %pad_maximum_fusion.refs_5_.a_1_), channel_id=1, source_target_pairs={{0,2},{1,3},{2,0},{3,1},{4,6},{5,7},{6,4},{7,5},{8,10},{9,11},{10,... | collective-permute-start | bytes 589832 | tf_op jit(solution)/shard_map/ppermute | solution.py:432
  38.4 2.2 %collective-permute-start.12 = (bf16[2,192,256]{2,1,0:T(8,128)(2,1)S(1)}, bf16[2,192,256]{2,1,0:T(8,128)(2,1)S(1)}, u32[]{:S(2)}, u32[]{:S(2)}) collective-permute-start(bf16[2,192,256]{2,1,0:T(8,128)(2,1)S(1)} %pad_maximum_fusion.refs_5_.a_1_), channel_id=1, source_target_pairs={{0,3},{1,2},{2,1},{3,0},{4,7},{5,6},{6,5},{7,4},{8,11},{9,10},{10,... | collective-permute-start | bytes 589832 | tf_op jit(solution)/shard_map/ppermute | solution.py:432
  41.2 5.9 %shard_map.97 = (f32[2,384,256]{2,1,0:T(8,128)S(1)}, bf16[2,400,256]{2,1,0:T(8,128)(2,1)S(1)}, bf16[2,400,256]{2,1,0:T(8,128)(2,1)S(1)}, bf16[2,400,256]{2,1,0:T(8,128)(2,1)S(1)}) custom-call(s32[4]{0:T(128)S(1)} %pad_add_fusion.info.a_0_, bf16[256,512]{1,0:T(8,128)(2,1)S(1)} %get-tuple-element.99.refs_0_, bf16[256,512]{1,0:T(8,128)(2,1)S(1)} %get-tuple-element.126.refs_1_, ...), custom_call_target="tpu_custom_call" | custom-call | flops 3221225472 | bytes 12582912 | tf_op jit(solution)/shard_map/pallas_call | solution.py:296
  47.7 2.6 %collective-permute-done.12.a_4_ = bf16[2,192,256]{2,1,0:T(8,128)(2,1)S(1)} collective-permute-done((bf16[2,192,256]{2,1,0:T(8,128)(2,1)S(1)}, bf16[2,192,256]{2,1,0:T(8,128)(2,1)S(1)}, u32[]{:S(2)}, u32[]{:S(2)}) %collective-permute-start.12) | collective-permute-done | bytes 196640 | tf_op jit(solution)/shard_map/ppermute | solution.py:432
  51.0 1.4 %collective-permute-start.22 = (bf16[256,512]{1,0:T(8,128)(2,1)S(1)}, bf16[256,512]{1,0:T(8,128)(2,1)S(1)}, u32[]{:S(2)}, u32[]{:S(2)}) collective-permute-start(bf16[256,512]{1,0:T(8,128)(2,1)S(1)} %get-tuple-element.127.refs_3_), channel_id=1, source_target_pairs={{0,24},{8,16},{16,8},{24,0},{32,56},{40,48},{48,40},{56,32},{64,88... | collective-permute-start | bytes 786440 | tf_op jit(solution)/shard_map/ppermute | solution.py:435
  52.5 2.3 %collective-permute-start.21 = (bf16[256,512]{1,0:T(8,128)(2,1)S(1)}, bf16[256,512]{1,0:T(8,128)(2,1)S(1)}, u32[]{:S(2)}, u32[]{:S(2)}) collective-permute-start(bf16[256,512]{1,0:T(8,128)(2,1)S(1)} %get-tuple-element.126.refs_1_), channel_id=1, source_target_pairs={{0,16},{8,24},{16,0},{24,8},{32,48},{40,56},{48,32},{56,40},{64,80... | collective-permute-start | bytes 786440 | tf_op jit(solution)/shard_map/ppermute | solution.py:435
  56.7 2.0 %collective-permute-start.18 = (bf16[192,512]{1,0:T(8,128)(2,1)S(1)}, bf16[192,512]{1,0:T(8,128)(2,1)S(1)}, u32[]{:S(2)}, u32[]{:S(2)}) collective-permute-start(bf16[192,512]{1,0:T(8,128)(2,1)S(1)} %get-tuple-element.123._.a_2_), channel_id=1, source_target_pairs={{0,32},{8,232},{16,48},{24,248},{32,64},{40,8},{48,80},{56,24},{64... | collective-permute-start | bytes 589832 | tf_op jit(solution)/shard_map/ppermute | solution.py:439
  58.8 4.0 %collective-permute-start.19 = (bf16[192,512]{1,0:T(8,128)(2,1)S(1)}, bf16[192,512]{1,0:T(8,128)(2,1)S(1)}, u32[]{:S(2)}, u32[]{:S(2)}) collective-permute-start(bf16[192,512]{1,0:T(8,128)(2,1)S(1)} %get-tuple-element.125), channel_id=1, source_target_pairs={{0,224},{8,40},{16,240},{24,56},{32,0},{40,72},{48,16},{56,88},{64... | collective-permute-start | bytes 589832 | tf_op jit(solution)/shard_map/ppermute | solution.py:439
  64.0 2.8 %collective-permute-done.21 = bf16[256,512]{1,0:T(8,128)(2,1)S(1)} collective-permute-done((bf16[256,512]{1,0:T(8,128)(2,1)S(1)}, bf16[256,512]{1,0:T(8,128)(2,1)S(1)}, u32[]{:S(2)}, u32[]{:S(2)}) %collective-permute-start.21) | collective-permute-done | bytes 262176 | tf_op jit(solution)/shard_map/ppermute | solution.py:435
  67.5 2.0 %collective-permute-start.24 = (bf16[192,512]{1,0:T(8,128)(2,1)S(1)}, bf16[192,512]{1,0:T(8,128)(2,1)S(1)}, u32[]{:S(2)}, u32[]{:S(2)}) collective-permute-start(bf16[192,512]{1,0:T(8,128)(2,1)S(1)} %get-tuple-element.128.a_4_), channel_id=1, source_target_pairs={{0,32},{8,232},{16,48},{24,248},{32,64},{40,8},{48,80},{56,24},{64... | collective-permute-start | bytes 589832 | tf_op jit(solution)/shard_map/ppermute | solution.py:439
  69.5 4.0 %collective-permute-start.25 = (bf16[192,512]{1,0:T(8,128)(2,1)S(1)}, bf16[192,512]{1,0:T(8,128)(2,1)S(1)}, u32[]{:S(2)}, u32[]{:S(2)}) collective-permute-start(bf16[192,512]{1,0:T(8,128)(2,1)S(1)} %get-tuple-element.131), channel_id=1, source_target_pairs={{0,224},{8,40},{16,240},{24,56},{32,0},{40,72},{48,16},{56,88},{64... | collective-permute-start | bytes 589832 | tf_op jit(solution)/shard_map/ppermute | solution.py:439
  73.6 2.3 %collective-permute-start.23 = (bf16[2,400,256]{2,1,0:T(8,128)(2,1)S(1)}, bf16[2,400,256]{2,1,0:T(8,128)(2,1)S(1)}, u32[]{:S(2)}, u32[]{:S(2)}) collective-permute-start(bf16[2,400,256]{2,1,0:T(8,128)(2,1)S(1)} %shard_map.104), channel_id=1, source_target_pairs={{0,3},{1,2},{2,1},{3,0},{4,7},{5,6},{6,5},{7,4},{8,11},{9,10},{10,... | collective-permute-start | bytes 1228808 | tf_op jit(solution)/shard_map/ppermute | solution.py:432
  75.9 1.6 %collective-permute-done.24.a_2_ = bf16[192,512]{1,0:T(8,128)(2,1)S(1)} collective-permute-done((bf16[192,512]{1,0:T(8,128)(2,1)S(1)}, bf16[192,512]{1,0:T(8,128)(2,1)S(1)}, u32[]{:S(2)}, u32[]{:S(2)}) %collective-permute-start.24) | collective-permute-done | bytes 196640 | tf_op jit(solution)/shard_map/ppermute | solution.py:439
  77.5 3.0 %collective-permute-start.29 = (bf16[192,512]{1,0:T(8,128)(2,1)S(1)}, bf16[192,512]{1,0:T(8,128)(2,1)S(1)}, u32[]{:S(2)}, u32[]{:S(2)}) collective-permute-start(bf16[192,512]{1,0:T(8,128)(2,1)S(1)} %get-tuple-element.135), channel_id=1, source_target_pairs={{0,224},{8,40},{16,240},{24,56},{32,0},{40,72},{48,16},{56,88},{64... | collective-permute-start | bytes 589832 | tf_op jit(solution)/shard_map/ppermute | solution.py:439
  81.3 0.8 shard_map.106
  82.5 1.8 %collective-permute-done.28.a_2_ = bf16[192,512]{1,0:T(8,128)(2,1)S(1)} collective-permute-done((bf16[192,512]{1,0:T(8,128)(2,1)S(1)}, bf16[192,512]{1,0:T(8,128)(2,1)S(1)}, u32[]{:S(2)}, u32[]{:S(2)}) %collective-permute-start.28) | collective-permute-done | bytes 196640 | tf_op jit(solution)/shard_map/ppermute | solution.py:439
  84.3 1.5 %collective-permute-start.32 = (bf16[192,512]{1,0:T(8,128)(2,1)S(1)}, bf16[192,512]{1,0:T(8,128)(2,1)S(1)}, u32[]{:S(2)}, u32[]{:S(2)}) collective-permute-start(bf16[192,512]{1,0:T(8,128)(2,1)S(1)} %get-tuple-element.137), channel_id=1, source_target_pairs={{0,224},{8,40},{16,240},{24,56},{32,0},{40,72},{48,16},{56,88},{64... | collective-permute-start | bytes 589832 | tf_op jit(solution)/shard_map/ppermute | solution.py:439
  85.8 0.7 shard_map.108
  87.1 7.2 %collective-permute-done.23.third.a_5_ = bf16[2,400,256]{2,1,0:T(8,128)(2,1)S(1)} collective-permute-done((bf16[2,400,256]{2,1,0:T(8,128)(2,1)S(1)}, bf16[2,400,256]{2,1,0:T(8,128)(2,1)S(1)}, u32[]{:S(2)}, u32[]{:S(2)}) %collective-permute-start.23) | collective-permute-done | bytes 409632 | tf_op jit(solution)/shard_map/ppermute | solution.py:432
  94.3 0.8 shard_map.109
  95.1 2.9 %collective-permute-start.36 = (bf16[192,512]{1,0:T(8,128)(2,1)}, bf16[192,512]{1,0:T(8,128)(2,1)}, u32[]{:S(2)}, u32[]{:S(2)}) collective-permute-start(bf16[192,512]{1,0:T(8,128)(2,1)} %get-tuple-element.140), channel_id=1, source_target_pairs={{0,224},{8,40},{16,240},{24,56},{32,0},{40,72},{48,16},{56,88},{64... | collective-permute-start | bytes 589832 | tf_op jit(solution)/shard_map/ppermute | solution.py:439
  98.1 2.1 %collective-permute-start.33 = (bf16[192,512]{1,0:T(8,128)(2,1)S(1)}, bf16[192,512]{1,0:T(8,128)(2,1)}, u32[]{:S(2)}, u32[]{:S(2)}) collective-permute-start(bf16[192,512]{1,0:T(8,128)(2,1)S(1)} %shard_map.110.a_2_), channel_id=1, source_target_pairs={{0,32},{8,232},{16,48},{24,248},{32,64},{40,8},{48,80},{56,24},{64... | collective-permute-start | bytes 589832 | tf_op jit(solution)/shard_map/ppermute | solution.py:439
  100.3 1.8 %shard_map.107 = (f32[384,256]{1,0:T(8,128)S(1)}, f32[1,256]{1,0:T(1,128)S(1)}, bf16[400,256]{1,0:T(8,128)(2,1)S(1)}) custom-call(f32[2,384,256]{2,1,0:T(8,128)} %copy-done.3, f32[1,256]{1,0:T(1,128)} %copy-done.6, bf16[2,400,256]{2,1,0:T(8,128)(2,1)} %copy-done.1, bf16[2,400,256]{2,1,0:T(8,128)(2,1)} %copy-done.2, ...), custom_call_target="tpu_custom_call" | custom-call | flops 786432 | bytes 2949120 | tf_op jit(solution)/shard_map/pallas_call | solution.py:347
  102.0 1.6 %collective-permute-done.36.a_1_ = bf16[192,512]{1,0:T(8,128)(2,1)} collective-permute-done((bf16[192,512]{1,0:T(8,128)(2,1)}, bf16[192,512]{1,0:T(8,128)(2,1)}, u32[]{:S(2)}, u32[]{:S(2)}) %collective-permute-start.36) | collective-permute-done | bytes 196640 | tf_op jit(solution)/shard_map/ppermute | solution.py:439
  103.7 1.0 shard_map.111
  104.7 3.8 %collective-permute-start.37 = (bf16[192,512]{1,0:T(8,128)(2,1)S(1)}, bf16[192,512]{1,0:T(8,128)(2,1)S(1)}, u32[]{:S(2)}, u32[]{:S(2)}) collective-permute-start(bf16[192,512]{1,0:T(8,128)(2,1)S(1)} %shard_map.111), channel_id=1, source_target_pairs={{0,224},{8,40},{16,240},{24,56},{32,0},{40,72},{48,16},{56,88},{64... | collective-permute-start | bytes 589832 | tf_op jit(solution)/shard_map/ppermute | solution.py:439
  108.5 1.2 %fusion.6 = bf16[192,512]{1,0:T(8,128)(2,1)S(1)} fusion(f32[1536,512]{1,0:T(8,128)} %copy-done, bf16[192,512]{1,0:T(8,128)(2,1)} %collective-permute-done.34, bf16[192,512]{1,0:T(8,128)(2,1)} %collective-permute-done.33), kind=kLoop, calls=%fused_computation.20 | loop fusion | flops 491520 | bytes 983040 | tf_op jit(solution)/shard_map/convert_element_type | solution.py:537
  109.7 1.3 %collective-permute-start.27 = (bf16[400,256]{1,0:T(8,128)(2,1)S(1)}, bf16[400,256]{1,0:T(8,128)(2,1)S(1)}, u32[]{:S(2)}, u32[]{:S(2)}) collective-permute-start(bf16[400,256]{1,0:T(8,128)(2,1)S(1)} %get-tuple-element.134.a_3_), channel_id=1, source_target_pairs={{0,4},{1,5},{2,6},{3,7},{4,0},{5,1},{6,2},{7,3},{8,12},{9,13},{10,... | collective-permute-start | bytes 614408 | tf_op jit(solution)/shard_map/ppermute | solution.py:432
  111.8 3.7 %collective-permute-done.27 = bf16[400,256]{1,0:T(8,128)(2,1)S(1)} collective-permute-done((bf16[400,256]{1,0:T(8,128)(2,1)S(1)}, bf16[400,256]{1,0:T(8,128)(2,1)S(1)}, u32[]{:S(2)}, u32[]{:S(2)}) %collective-permute-start.27) | collective-permute-done | bytes 204832 | tf_op jit(solution)/shard_map/ppermute | solution.py:432
  115.6 0.7 select_reduce_fusion
  116.3 1.1 convolution_convert_fusion
  117.4 0.8 broadcast_select_fusion
  (88 shorter events, 11.8 us)
Async XLA Ops:
  1.6 25.8 %copy-start.4 = (s32[512]{0:T(512)}, s32[512]{0:T(512)S(1)}, u32[]{:S(2)}) copy-start(s32[512]{0:T(512)S(1)} %convert_select_fusion) | copy-start | bytes 6148
  3.6 9.1 %collective-permute-start = (bf16[256,384]{1,0:T(8,128)(2,1)S(1)}, bf16[256,384]{1,0:T(8,128)(2,1)S(1)}, u32[]{:S(2)}, u32[]{:S(2)}) collective-permute-start(bf16[256,384]{1,0:T(8,128)(2,1)S(1)} %get-tuple-element.79.a_1_), channel_id=1, source_target_pairs={{0,1},{1,0},{2,3},{3,2},{4,5},{5,4},{6,7},{7,6},{8,9},{9,8},{10,11... | collective-permute-start | bytes 589832 | tf_op jit(solution)/shard_map/ppermute | solution.py:432
  5.3 7.6 %collective-permute-start.1 = (bf16[256,384]{1,0:T(8,128)(2,1)S(1)}, bf16[256,384]{1,0:T(8,128)(2,1)S(1)}, u32[]{:S(2)}, u32[]{:S(2)}) collective-permute-start(bf16[256,384]{1,0:T(8,128)(2,1)S(1)} %get-tuple-element.79.a_1_), channel_id=1, source_target_pairs={{0,3},{1,2},{2,1},{3,0},{4,7},{5,6},{6,5},{7,4},{8,11},{9,10},{10,... | collective-permute-start | bytes 589832 | tf_op jit(solution)/shard_map/ppermute | solution.py:432
  7.4 6.1 %collective-permute-start.2 = (bf16[256,384]{1,0:T(8,128)(2,1)S(1)}, bf16[256,384]{1,0:T(8,128)(2,1)S(1)}, u32[]{:S(2)}, u32[]{:S(2)}) collective-permute-start(bf16[256,384]{1,0:T(8,128)(2,1)S(1)} %get-tuple-element.79.a_1_), channel_id=1, source_target_pairs={{0,4},{1,5},{2,6},{3,7},{4,0},{5,1},{6,2},{7,3},{8,12},{9,13},{10,... | collective-permute-start | bytes 589832 | tf_op jit(solution)/shard_map/ppermute | solution.py:432
  8.0 4.7 %collective-permute-start.3 = (bf16[192,256]{1,0:T(8,128)(2,1)S(1)}, bf16[192,256]{1,0:T(8,128)(2,1)S(1)}, u32[]{:S(2)}, u32[]{:S(2)}) collective-permute-start(bf16[192,256]{1,0:T(8,128)(2,1)S(1)} %get-tuple-element.83), channel_id=1, source_target_pairs={{0,20},{1,21},{2,22},{3,23},{4,16},{5,17},{6,18},{7,19},{8,28},{9,... | collective-permute-start | bytes 294920 | tf_op jit(solution)/shard_map/ppermute | solution.py:444
  13.5 13.9 %collective-permute-start.4 = (bf16[256,384]{1,0:T(8,128)(2,1)S(1)}, bf16[256,384]{1,0:T(8,128)(2,1)S(1)}, u32[]{:S(2)}, u32[]{:S(2)}) collective-permute-start(bf16[256,384]{1,0:T(8,128)(2,1)S(1)} %collective-permute-done.a_3_), channel_id=1, source_target_pairs={{0,4},{1,5},{2,6},{3,7},{4,0},{5,1},{6,2},{7,3},{8,12},{9,13},{10,... | collective-permute-start | bytes 589832 | tf_op jit(solution)/shard_map/ppermute | solution.py:432
  15.4 12.0 %collective-permute-start.5 = (bf16[256,384]{1,0:T(8,128)(2,1)S(1)}, bf16[256,384]{1,0:T(8,128)(2,1)S(1)}, u32[]{:S(2)}, u32[]{:S(2)}) collective-permute-start(bf16[256,384]{1,0:T(8,128)(2,1)S(1)} %collective-permute-done.1.a_4_), channel_id=1, source_target_pairs={{0,4},{1,5},{2,6},{3,7},{4,0},{5,1},{6,2},{7,3},{8,12},{9,13},{10,... | collective-permute-start | bytes 589832 | tf_op jit(solution)/shard_map/ppermute | solution.py:432
  15.5 11.9 %collective-permute-start.6 = (bf16[256,384]{1,0:T(8,128)(2,1)S(1)}, bf16[256,384]{1,0:T(8,128)(2,1)S(1)}, u32[]{:S(2)}, u32[]{:S(2)}) collective-permute-start(bf16[256,384]{1,0:T(8,128)(2,1)S(1)} %get-tuple-element.79.a_1_), channel_id=1, source_target_pairs={{0,2},{1,3},{2,0},{3,1},{4,6},{5,7},{6,4},{7,5},{8,10},{9,11},{10,... | collective-permute-start | bytes 589832 | tf_op jit(solution)/shard_map/ppermute | solution.py:432
  16.8 10.6 %collective-permute-start.7 = (bf16[256,384]{1,0:T(8,128)(2,1)S(1)}, bf16[256,384]{1,0:T(8,128)(2,1)S(1)}, u32[]{:S(2)}, u32[]{:S(2)}) collective-permute-start(bf16[256,384]{1,0:T(8,128)(2,1)S(1)} %collective-permute-done.2.a_2_), channel_id=1, source_target_pairs={{0,2},{1,3},{2,0},{3,1},{4,6},{5,7},{6,4},{7,5},{8,10},{9,11},{10,... | collective-permute-start | bytes 589832 | tf_op jit(solution)/shard_map/ppermute | solution.py:432
  19.1 8.3 %collective-permute-start.8 = (bf16[192,256]{1,0:T(8,128)(2,1)S(1)}, bf16[192,256]{1,0:T(8,128)(2,1)S(1)}, u32[]{:S(2)}, u32[]{:S(2)}) collective-permute-start(bf16[192,256]{1,0:T(8,128)(2,1)S(1)} %get-tuple-element.83), channel_id=1, source_target_pairs={{0,16},{8,24},{16,0},{24,8},{32,48},{40,56},{48,32},{56,40},{64,80... | collective-permute-start | bytes 294920 | tf_op jit(solution)/shard_map/ppermute | solution.py:435
  31.4 9.8 %copy-start.6 = (f32[1,256]{1,0:T(1,128)}, f32[1,256]{1,0:T(1,128)S(1)}, u32[]{:S(2)}) copy-start(f32[1,256]{1,0:T(1,128)S(1)} %get-tuple-element.103.refs_4_.route) | copy-start | bytes 3076
  31.4 4.4 %collective-permute-start.9 = (bf16[8,192,256]{2,1,0:T(8,128)(2,1)S(1)}, bf16[8,192,256]{2,1,0:T(8,128)(2,1)S(1)}, u32[]{:S(2)}, u32[]{:S(2)}) collective-permute-start(bf16[8,192,256]{2,1,0:T(8,128)(2,1)S(1)} %get-tuple-element.97), channel_id=1, source_target_pairs={{0,8},{8,0},{16,24},{24,16},{32,40},{40,32},{48,56},{56,48},{64,72... | collective-permute-start | bytes 2359304 | tf_op jit(solution)/shard_map/ppermute | solution.py:435
  31.5 6.9 %collective-permute-start.13 = (bf16[256,512]{1,0:T(8,128)(2,1)S(1)}, bf16[256,512]{1,0:T(8,128)(2,1)S(1)}, u32[]{:S(2)}, u32[]{:S(2)}) collective-permute-start(bf16[256,512]{1,0:T(8,128)(2,1)S(1)} %get-tuple-element.101.refs_2_), channel_id=1, source_target_pairs={{0,8},{8,0},{16,24},{24,16},{32,40},{40,32},{48,56},{56,48},{64,72... | collective-permute-start | bytes 786440 | tf_op jit(solution)/shard_map/ppermute | solution.py:435
  32.0 19.0 %collective-permute-start.15 = (bf16[256,512]{1,0:T(8,128)(2,1)S(1)}, bf16[256,512]{1,0:T(8,128)(2,1)S(1)}, u32[]{:S(2)}, u32[]{:S(2)}) collective-permute-start(bf16[256,512]{1,0:T(8,128)(2,1)S(1)} %get-tuple-element.101.refs_2_), channel_id=1, source_target_pairs={{0,24},{8,16},{16,8},{24,0},{32,56},{40,48},{48,40},{56,32},{64,88... | collective-permute-start | bytes 786440 | tf_op jit(solution)/shard_map/ppermute | solution.py:435
  32.7 18.3 %collective-permute-start.14 = (bf16[256,512]{1,0:T(8,128)(2,1)S(1)}, bf16[256,512]{1,0:T(8,128)(2,1)S(1)}, u32[]{:S(2)}, u32[]{:S(2)}) collective-permute-start(bf16[256,512]{1,0:T(8,128)(2,1)S(1)} %get-tuple-element.99.refs_0_), channel_id=1, source_target_pairs={{0,16},{8,24},{16,0},{24,8},{32,48},{40,56},{48,32},{56,40},{64,80... | collective-permute-start | bytes 786440 | tf_op jit(solution)/shard_map/ppermute | solution.py:435
  35.8 11.3 %collective-permute-start.10 = (bf16[2,192,256]{2,1,0:T(8,128)(2,1)S(1)}, bf16[2,192,256]{2,1,0:T(8,128)(2,1)S(1)}, u32[]{:S(2)}, u32[]{:S(2)}) collective-permute-start(bf16[2,192,256]{2,1,0:T(8,128)(2,1)S(1)} %pad_maximum_fusion.refs_5_.a_1_), channel_id=1, source_target_pairs={{0,1},{1,0},{2,3},{3,2},{4,5},{5,4},{6,7},{7,6},{8,9},{9,8},{10,11... | collective-permute-start | bytes 589832 | tf_op jit(solution)/shard_map/ppermute | solution.py:432
  36.6 11.1 %collective-permute-start.11 = (bf16[2,192,256]{2,1,0:T(8,128)(2,1)S(1)}, bf16[2,192,256]{2,1,0:T(8,128)(2,1)S(1)}, u32[]{:S(2)}, u32[]{:S(2)}) collective-permute-start(bf16[2,192,256]{2,1,0:T(8,128)(2,1)S(1)} %pad_maximum_fusion.refs_5_.a_1_), channel_id=1, source_target_pairs={{0,2},{1,3},{2,0},{3,1},{4,6},{5,7},{6,4},{7,5},{8,10},{9,11},{10,... | collective-permute-start | bytes 589832 | tf_op jit(solution)/shard_map/ppermute | solution.py:432
  38.4 11.8 %collective-permute-start.12 = (bf16[2,192,256]{2,1,0:T(8,128)(2,1)S(1)}, bf16[2,192,256]{2,1,0:T(8,128)(2,1)S(1)}, u32[]{:S(2)}, u32[]{:S(2)}) collective-permute-start(bf16[2,192,256]{2,1,0:T(8,128)(2,1)S(1)} %pad_maximum_fusion.refs_5_.a_1_), channel_id=1, source_target_pairs={{0,3},{1,2},{2,1},{3,0},{4,7},{5,6},{6,5},{7,4},{8,11},{9,10},{10,... | collective-permute-start | bytes 589832 | tf_op jit(solution)/shard_map/ppermute | solution.py:432
  47.1 8.8 %copy-start.3 = (f32[2,384,256]{2,1,0:T(8,128)}, f32[2,384,256]{2,1,0:T(8,128)S(1)}, u32[]{:S(2)}) copy-start(f32[2,384,256]{2,1,0:T(8,128)S(1)} %get-tuple-element.110.own) | copy-start | bytes 2359300
  50.9 5.0 %collective-permute-start.16 = (bf16[8,192,256]{2,1,0:T(8,128)(2,1)S(1)}, bf16[8,192,256]{2,1,0:T(8,128)(2,1)S(1)}, u32[]{:S(2)}, u32[]{:S(2)}) collective-permute-start(bf16[8,192,256]{2,1,0:T(8,128)(2,1)S(1)} %get-tuple-element.121), channel_id=1, source_target_pairs={{0,8},{8,0},{16,24},{24,16},{32,40},{40,32},{48,56},{56,48},{64,72... | collective-permute-start | bytes 2359304 | tf_op jit(solution)/shard_map/ppermute | solution.py:435
  51.0 12.4 %collective-permute-start.22 = (bf16[256,512]{1,0:T(8,128)(2,1)S(1)}, bf16[256,512]{1,0:T(8,128)(2,1)S(1)}, u32[]{:S(2)}, u32[]{:S(2)}) collective-permute-start(bf16[256,512]{1,0:T(8,128)(2,1)S(1)} %get-tuple-element.127.refs_3_), channel_id=1, source_target_pairs={{0,24},{8,16},{16,8},{24,0},{32,56},{40,48},{48,40},{56,32},{64,88... | collective-permute-start | bytes 786440 | tf_op jit(solution)/shard_map/ppermute | solution.py:435
  52.4 2.9 %collective-permute-start.20 = (bf16[256,512]{1,0:T(8,128)(2,1)S(1)}, bf16[256,512]{1,0:T(8,128)(2,1)S(1)}, u32[]{:S(2)}, u32[]{:S(2)}) collective-permute-start(bf16[256,512]{1,0:T(8,128)(2,1)S(1)} %get-tuple-element.127.refs_3_), channel_id=1, source_target_pairs={{0,8},{8,0},{16,24},{24,16},{32,40},{40,32},{48,56},{56,48},{64,72... | collective-permute-start | bytes 786440 | tf_op jit(solution)/shard_map/ppermute | solution.py:435
  52.5 14.3 %collective-permute-start.21 = (bf16[256,512]{1,0:T(8,128)(2,1)S(1)}, bf16[256,512]{1,0:T(8,128)(2,1)S(1)}, u32[]{:S(2)}, u32[]{:S(2)}) collective-permute-start(bf16[256,512]{1,0:T(8,128)(2,1)S(1)} %get-tuple-element.126.refs_1_), channel_id=1, source_target_pairs={{0,16},{8,24},{16,0},{24,8},{32,48},{40,56},{48,32},{56,40},{64,80... | collective-permute-start | bytes 786440 | tf_op jit(solution)/shard_map/ppermute | solution.py:435
  56.6 41.5 %copy-start = (f32[1536,512]{1,0:T(8,128)}, f32[1536,512]{1,0:T(8,128)S(1)}, u32[]{:S(2)}) copy-start(f32[1536,512]{1,0:T(8,128)S(1)} %add_add_fusion) | copy-start | bytes 9437188
  56.7 16.8 %collective-permute-start.18 = (bf16[192,512]{1,0:T(8,128)(2,1)S(1)}, bf16[192,512]{1,0:T(8,128)(2,1)S(1)}, u32[]{:S(2)}, u32[]{:S(2)}) collective-permute-start(bf16[192,512]{1,0:T(8,128)(2,1)S(1)} %get-tuple-element.123._.a_2_), channel_id=1, source_target_pairs={{0,32},{8,232},{16,48},{24,248},{32,64},{40,8},{48,80},{56,24},{64... | collective-permute-start | bytes 589832 | tf_op jit(solution)/shard_map/ppermute | solution.py:439
  58.7 21.8 %collective-permute-start.17 = (bf16[2,400,256]{2,1,0:T(8,128)(2,1)S(1)}, bf16[2,400,256]{2,1,0:T(8,128)(2,1)S(1)}, u32[]{:S(2)}, u32[]{:S(2)}) collective-permute-start(bf16[2,400,256]{2,1,0:T(8,128)(2,1)S(1)} %shard_map.100), channel_id=1, source_target_pairs={{0,1},{1,0},{2,3},{3,2},{4,5},{5,4},{6,7},{7,6},{8,9},{9,8},{10,11... | collective-permute-start | bytes 1228808 | tf_op jit(solution)/shard_map/ppermute | solution.py:432
  58.8 14.6 %collective-permute-start.19 = (bf16[192,512]{1,0:T(8,128)(2,1)S(1)}, bf16[192,512]{1,0:T(8,128)(2,1)S(1)}, u32[]{:S(2)}, u32[]{:S(2)}) collective-permute-start(bf16[192,512]{1,0:T(8,128)(2,1)S(1)} %get-tuple-element.125), channel_id=1, source_target_pairs={{0,224},{8,40},{16,240},{24,56},{32,0},{40,72},{48,16},{56,88},{64... | collective-permute-start | bytes 589832 | tf_op jit(solution)/shard_map/ppermute | solution.py:439
  67.5 10.1 %collective-permute-start.24 = (bf16[192,512]{1,0:T(8,128)(2,1)S(1)}, bf16[192,512]{1,0:T(8,128)(2,1)S(1)}, u32[]{:S(2)}, u32[]{:S(2)}) collective-permute-start(bf16[192,512]{1,0:T(8,128)(2,1)S(1)} %get-tuple-element.128.a_4_), channel_id=1, source_target_pairs={{0,32},{8,232},{16,48},{24,248},{32,64},{40,8},{48,80},{56,24},{64... | collective-permute-start | bytes 589832 | tf_op jit(solution)/shard_map/ppermute | solution.py:439
  69.5 11.1 %collective-permute-start.25 = (bf16[192,512]{1,0:T(8,128)(2,1)S(1)}, bf16[192,512]{1,0:T(8,128)(2,1)S(1)}, u32[]{:S(2)}, u32[]{:S(2)}) collective-permute-start(bf16[192,512]{1,0:T(8,128)(2,1)S(1)} %get-tuple-element.131), channel_id=1, source_target_pairs={{0,224},{8,40},{16,240},{24,56},{32,0},{40,72},{48,16},{56,88},{64... | collective-permute-start | bytes 589832 | tf_op jit(solution)/shard_map/ppermute | solution.py:439
  73.6 20.7 %collective-permute-start.23 = (bf16[2,400,256]{2,1,0:T(8,128)(2,1)S(1)}, bf16[2,400,256]{2,1,0:T(8,128)(2,1)S(1)}, u32[]{:S(2)}, u32[]{:S(2)}) collective-permute-start(bf16[2,400,256]{2,1,0:T(8,128)(2,1)S(1)} %shard_map.104), channel_id=1, source_target_pairs={{0,3},{1,2},{2,1},{3,0},{4,7},{5,6},{6,5},{7,4},{8,11},{9,10},{10,... | collective-permute-start | bytes 1228808 | tf_op jit(solution)/shard_map/ppermute | solution.py:432
  75.9 8.4 %collective-permute-start.28 = (bf16[192,512]{1,0:T(8,128)(2,1)S(1)}, bf16[192,512]{1,0:T(8,128)(2,1)S(1)}, u32[]{:S(2)}, u32[]{:S(2)}) collective-permute-start(bf16[192,512]{1,0:T(8,128)(2,1)S(1)} %get-tuple-element.129._.a_4_), channel_id=1, source_target_pairs={{0,32},{8,232},{16,48},{24,248},{32,64},{40,8},{48,80},{56,24},{64... | collective-permute-start | bytes 589832 | tf_op jit(solution)/shard_map/ppermute | solution.py:439
  77.5 8.3 %collective-permute-start.29 = (bf16[192,512]{1,0:T(8,128)(2,1)S(1)}, bf16[192,512]{1,0:T(8,128)(2,1)S(1)}, u32[]{:S(2)}, u32[]{:S(2)}) collective-permute-start(bf16[192,512]{1,0:T(8,128)(2,1)S(1)} %get-tuple-element.135), channel_id=1, source_target_pairs={{0,224},{8,40},{16,240},{24,56},{32,0},{40,72},{48,16},{56,88},{64... | collective-permute-start | bytes 589832 | tf_op jit(solution)/shard_map/ppermute | solution.py:439
  80.5 0.8 copy-start.1
  82.1 18.2 %collective-permute-start.26 = (bf16[2,400,256]{2,1,0:T(8,128)(2,1)}, bf16[2,400,256]{2,1,0:T(8,128)(2,1)}, u32[]{:S(2)}, u32[]{:S(2)}) collective-permute-start(bf16[2,400,256]{2,1,0:T(8,128)(2,1)} %shard_map.106), channel_id=1, source_target_pairs={{0,2},{1,3},{2,0},{3,1},{4,6},{5,7},{6,4},{7,5},{8,10},{9,11},{10,... | collective-permute-start | bytes 1228808 | tf_op jit(solution)/shard_map/ppermute | solution.py:432
  82.5 11.7 %collective-permute-start.31 = (bf16[192,512]{1,0:T(8,128)(2,1)S(1)}, bf16[192,512]{1,0:T(8,128)(2,1)S(1)}, u32[]{:S(2)}, u32[]{:S(2)}) collective-permute-start(bf16[192,512]{1,0:T(8,128)(2,1)S(1)} %get-tuple-element.132._.a_4_), channel_id=1, source_target_pairs={{0,32},{8,232},{16,48},{24,248},{32,64},{40,8},{48,80},{56,24},{64... | collective-permute-start | bytes 589832 | tf_op jit(solution)/shard_map/ppermute | solution.py:439
  84.3 10.0 %collective-permute-start.32 = (bf16[192,512]{1,0:T(8,128)(2,1)S(1)}, bf16[192,512]{1,0:T(8,128)(2,1)S(1)}, u32[]{:S(2)}, u32[]{:S(2)}) collective-permute-start(bf16[192,512]{1,0:T(8,128)(2,1)S(1)} %get-tuple-element.137), channel_id=1, source_target_pairs={{0,224},{8,40},{16,240},{24,56},{32,0},{40,72},{48,16},{56,88},{64... | collective-permute-start | bytes 589832 | tf_op jit(solution)/shard_map/ppermute | solution.py:439
  86.5 11.5 %collective-permute-start.30 = (bf16[192,512]{1,0:T(8,128)(2,1)S(1)}, bf16[192,512]{1,0:T(8,128)(2,1)S(1)}, u32[]{:S(2)}, u32[]{:S(2)}) collective-permute-start(bf16[192,512]{1,0:T(8,128)(2,1)S(1)} %get-tuple-element.136.a_4_), channel_id=1, source_target_pairs={{0,32},{8,232},{16,48},{24,248},{32,64},{40,8},{48,80},{56,24},{64... | collective-permute-start | bytes 589832 | tf_op jit(solution)/shard_map/ppermute | solution.py:439
  94.3 0.8 copy-start.2
  95.1 8.6 %collective-permute-start.36 = (bf16[192,512]{1,0:T(8,128)(2,1)}, bf16[192,512]{1,0:T(8,128)(2,1)}, u32[]{:S(2)}, u32[]{:S(2)}) collective-permute-start(bf16[192,512]{1,0:T(8,128)(2,1)} %get-tuple-element.140), channel_id=1, source_target_pairs={{0,224},{8,40},{16,240},{24,56},{32,0},{40,72},{48,16},{56,88},{64... | collective-permute-start | bytes 589832 | tf_op jit(solution)/shard_map/ppermute | solution.py:439
  98.0 10.4 %collective-permute-start.34 = (bf16[192,512]{1,0:T(8,128)(2,1)}, bf16[192,512]{1,0:T(8,128)(2,1)}, u32[]{:S(2)}, u32[]{:S(2)}) collective-permute-start(bf16[192,512]{1,0:T(8,128)(2,1)} %get-tuple-element.139), channel_id=1, source_target_pairs={{0,224},{8,40},{16,240},{24,56},{32,0},{40,72},{48,16},{56,88},{64... | collective-permute-start | bytes 589832 | tf_op jit(solution)/shard_map/ppermute | solution.py:439
  98.1 10.3 %collective-permute-start.33 = (bf16[192,512]{1,0:T(8,128)(2,1)S(1)}, bf16[192,512]{1,0:T(8,128)(2,1)}, u32[]{:S(2)}, u32[]{:S(2)}) collective-permute-start(bf16[192,512]{1,0:T(8,128)(2,1)S(1)} %shard_map.110.a_2_), channel_id=1, source_target_pairs={{0,32},{8,232},{16,48},{24,248},{32,64},{40,8},{48,80},{56,24},{64... | collective-permute-start | bytes 589832 | tf_op jit(solution)/shard_map/ppermute | solution.py:439
  100.2 10.8 %collective-permute-start.35 = (bf16[192,512]{1,0:T(8,128)(2,1)S(1)}, bf16[192,512]{1,0:T(8,128)(2,1)S(1)}, u32[]{:S(2)}, u32[]{:S(2)}) collective-permute-start(bf16[192,512]{1,0:T(8,128)(2,1)S(1)} %get-tuple-element.138.a_2_), channel_id=1, source_target_pairs={{0,32},{8,232},{16,48},{24,248},{32,64},{40,8},{48,80},{56,24},{64... | collective-permute-start | bytes 589832 | tf_op jit(solution)/shard_map/ppermute | solution.py:439
  103.7 11.9 %copy-start.5 = (s32[512]{0:T(512)S(1)}, s32[512]{0:T(512)}, u32[]{:S(2)}) copy-start(s32[512]{0:T(512)} %copy-done.4) | copy-start | bytes 6148
  104.7 7.0 %collective-permute-start.37 = (bf16[192,512]{1,0:T(8,128)(2,1)S(1)}, bf16[192,512]{1,0:T(8,128)(2,1)S(1)}, u32[]{:S(2)}, u32[]{:S(2)}) collective-permute-start(bf16[192,512]{1,0:T(8,128)(2,1)S(1)} %shard_map.111), channel_id=1, source_target_pairs={{0,224},{8,40},{16,240},{24,56},{32,0},{40,72},{48,16},{56,88},{64... | collective-permute-start | bytes 589832 | tf_op jit(solution)/shard_map/ppermute | solution.py:439
  109.7 5.8 %collective-permute-start.27 = (bf16[400,256]{1,0:T(8,128)(2,1)S(1)}, bf16[400,256]{1,0:T(8,128)(2,1)S(1)}, u32[]{:S(2)}, u32[]{:S(2)}) collective-permute-start(bf16[400,256]{1,0:T(8,128)(2,1)S(1)} %get-tuple-element.134.a_3_), channel_id=1, source_target_pairs={{0,4},{1,5},{2,6},{3,7},{4,0},{5,1},{6,2},{7,3},{8,12},{9,13},{10,... | collective-permute-start | bytes 614408 | tf_op jit(solution)/shard_map/ppermute | solution.py:432
  111.7 5.6 %collective-permute-start.38 = (bf16[96,1024]{1,0:T(8,128)(2,1)S(1)}, bf16[96,1024]{1,0:T(8,128)(2,1)S(1)}, u32[]{:S(2)}, u32[]{:S(2)}) collective-permute-start(bf16[96,1024]{1,0:T(8,128)(2,1)S(1)} %fusion.10), channel_id=1, source_target_pairs={{0,8},{8,0},{16,24},{24,16},{32,40},{40,32},{48,56},{56,48},{64,72... | collective-permute-start | bytes 589832 | tf_op jit(solution)/shard_map/ppermute | solution.py:435
